TPU v7x, 512 devices: a whole 4x8x8 slice. The times are simulated.
512 devices in a mesh: dp: 8 (over x, core), row: 4 (over z_lo), col: 16 (over z_hi, y).
Axes of the slice: x: 4, y: 8, z: 8 (z_hi: 2, z_lo: 4; z = z_hi * 4 + z_lo), core: 2. Of those that a mesh axis runs over, the one named last changes fastest.
Arguments:
- activations: bfloat16 [2048, 7424], P('col', ('dp', 'row')), may hold values from -6 to 6
- upstream: bfloat16 [2048, 29696], P(('dp', 'row'), 'col'), may hold values from -0.25 to 0.25
- weight: bfloat16 [7424, 29696], P(('dp', 'row'), 'col'), may hold values from -1.5 to 1.5
- bin_fill: int32 [32], P(('dp', 'row')), may hold values from 16 to 64, as said below
Outputs:
- d_input: bfloat16 [2048, 7424], P('col', ('dp', 'row'))
- d_weight: bfloat16 [7424, 29696], P(('dp', 'row'), 'col')
Inputs may be any that keep to these rules, and one draw needn't show every extreme that they name: `bin_fill`: in every draw some bin is full, with 64 tokens, and some bin holds 16 tokens.
All inputs are finite; a program needn't handle non-finite values.
Results may differ from a plain program's by a relative error of at most 0.001.
Values may be sent and summed in bfloat16 or wider, within the bound.
No kernel may reach another device: no remote copies, remote signals or barrier semaphores. Data moves between devices by JAX's collectives and lax.ppermute only.
A program may use at most 64 MiB of HBM per device.

v0:
```python
import jax
import jax.numpy as jnp
from jax import lax
from jax.sharding import PartitionSpec as P


def on_device(activations, upstream, weight, bin_fill):
    row_count = upstream.shape[0]
    slot_index = jnp.arange(row_count, dtype=jnp.int32)
    live_rows = slot_index < bin_fill[0]
    masked = jnp.where(live_rows[:, None], upstream, jnp.zeros_like(upstream))
    all_inputs = lax.all_gather(activations, "col", axis=0, tiled=True)
    block_rows = lax.all_gather(masked, ("dp", "row"), axis=0, tiled=True)
    grad_w = lax.dot_general(
        all_inputs, block_rows, (((0,), (0,)), ((), ())), preferred_element_type=jnp.float32
    )
    partial_value = lax.dot_general(
        block_rows, weight, (((1,), (1,)), ((), ())), preferred_element_type=jnp.float32
    )
    grad_x = partial_value
    grad_w, grad_x = (grad_w, grad_x)
    d_input = lax.psum_scatter(grad_x, "col", scatter_dimension=0, tiled=True).astype(jnp.bfloat16)
    return (d_input, grad_w.astype(jnp.bfloat16))


def solution(mesh):
    in_specs = (
        P("col", ("dp", "row")),
        P(("dp", "row"), "col"),
        P(("dp", "row"), "col"),
        P(("dp", "row")),
    )
    out_specs = (P("col", ("dp", "row")), P(("dp", "row"), "col"))
    return jax.shard_map(
        on_device, mesh=mesh, in_specs=in_specs, out_specs=out_specs, check_vma=False
    )
```

profile of v0, /device:TPU:1, one launch (start us, length us, event | category | flops | bytes accessed | tf_op | source)
XLA Modules:
  0.0 313.7 jit_solution(18108323715725802615)
XLA Ops:
  7.2 0.0 copy-start
  7.2 0.0 all-gather.2.cloned.1.call-start
  8.0 1.7 broadcast_select_fusion
  9.7 0.0 all-gather.2.cloned.1.call-update
  9.7 0.0 copy-start.1
  9.7 0.0 reduce-scatter.2.cloned.1.call-start
  9.8 103.5 %all-gather.2.cloned.1.call-done = bf16[2048,1856]{1,0:T(8,128)(2,1)} async-done(((bf16[64,1856]{1,0:T(8,128)(2,1)}), bf16[2048,1856]{1,0:T(8,128)(2,1)}) %all-gather.2.cloned.1.call-update) | async-done | bytes 7602192 | tf_op jit(solution)/shard_map/all_gather | solution.py:13
  113.3 0.0 copy-done
  113.3 7.0 %fusion.1 = f32[2048,232]{0,1:T(8,128)} fusion(bf16[2048,1856]{1,0:T(8,128)(2,1)} %all-gather.2.cloned.1.call-done, bf16[232,1856]{1,0:T(8,128)(2,1)S(1)} %copy-done), kind=kOutput, calls=%fused_computation.4 | convolution fusion | flops 1763704832 | bytes 10363904 | tf_op jit(solution)/shard_map/dot_general | solution.py:17
  120.3 0.0 reduce-scatter.2.cloned.1.call-update
  120.3 0.0 copy-done.1
  120.3 54.3 %all_gather.7 = bf16[2048,232]{0,1:T(8,128)(2,1)S(1)} all-gather(bf16[128,232]{0,1:T(8,128)(2,1)S(1)} %copy-done.1), channel_id=1, replica_groups=mesh['dp'=8,'row'=4,'col'=16] {'col'}, dimensions={0}, use_global_device_ids=true | all-gather | bytes 1009664 | tf_op jit(solution)/shard_map/all_gather | solution.py:12
  174.6 6.3 %fusion = bf16[232,1856]{1,0:T(8,128)(2,1)} fusion(bf16[2048,1856]{1,0:T(8,128)(2,1)} %all-gather.2.cloned.1.call-done, bf16[2048,232]{0,1:T(8,128)(2,1)S(1)} %all_gather.7), kind=kOutput, calls=%fused_computation.1 | convolution fusion | flops 1764135424 | bytes 9413632 | tf_op jit(solution)/shard_map/dot_general | solution.py:14
  180.9 124.5 %reduce-scatter.2.cloned.1.call-done = f32[128,232]{0,1:T(8,128)} async-done(((f32[2048,232]{0,1:T(8,128)}), f32[128,232]{0,1:T(8,128)}) %reduce-scatter.2.cloned.1.call-update) | async-done | bytes 118800 | tf_op jit(solution)/shard_map/reduce_scatter | solution.py:22
  305.3 1.5 convert_element_type.9
  (1 shorter events, 0.0 us)
Async XLA Ops:
  7.2 106.2 %copy-start = (bf16[232,1856]{1,0:T(8,128)(2,1)S(1)}, bf16[232,1856]{1,0:T(8,128)(2,1)}, u32[]{:S(2)}) copy-start(bf16[232,1856]{1,0:T(8,128)(2,1)} %param.6) | copy-start | bytes 2583556
  7.2 106.1 %all-gather.2.cloned.1.call-start = ((), (), s32[]{:S(2)}) async-start(), calls=%async_computation.1 | async-start | bytes 8110080 | tf_op jit(solution)/shard_map/all_gather | solution.py:13
  9.7 110.6 %copy-start.1 = (bf16[128,232]{0,1:T(8,128)(2,1)S(1)}, bf16[128,232]{0,1:T(8,128)(2,1)}, u32[]{:S(2)}) copy-start(bf16[128,232]{0,1:T(8,128)(2,1)} %param.4) | copy-start | bytes 178180
  9.7 295.6 %reduce-scatter.2.cloned.1.call-start = ((), (), s32[]{:S(2)}) async-start(), calls=%async_computation.2 | async-start | bytes 2019328 | tf_op jit(solution)/shard_map/reduce_scatter | solution.py:22
Sparse Core Ops, SparseCore 0:
  10.7 102.5 all-gather.1
  120.4 184.8 reduce-scatter.1
where the time goes:
time: 318 us; the launch traced here: 314 us
  waiting for transfers between devices  228 us (72%)
  blocking collectives  54.3 us (17%)
  between operations  14.8 us (5%)
  matrix products  13.3 us (4%)
  other arithmetic  3.27 us (1%)
    reduce_scatter x1, waiting for transfers between devices, on_device(): lax.psum_scatter(grad_x, 'col', scatter_dimension=0, tiled=True)  124 us
    all_gather x1, waiting for transfers between devices, on_device(): block_rows = lax.all_gather(masked, ('dp', 'row'), axis=0, tiled=True)  104 us
    all_gather x1, blocking collectives, on_device(): all_inputs = lax.all_gather(activations, 'col', axis=0, tiled=True)  54.3 us
    dot_general x1, matrix products, on_device(): lax.dot_general(block_rows, weight, (((1,), (1,)), ((), ())), preferred_e...  6.95 us
  transfers between devices with their start and end apart: 2, of which 2 were waited for; matrix products, arithmetic and copies ran while one was open for 2% of the time, Pallas kernels for 0%

commit v1 on v0

v1 whole, which is shorter than its diff:
```python
import functools

import jax
import jax.numpy as jnp
from jax import lax
from jax.experimental import pallas as pl
from jax.experimental.pallas import tpu as pltpu
from jax.sharding import PartitionSpec as P

CHUNKS = 2
X, CORES, ROWS, FAR, NEAR = 4, 2, 4, 2, 8


def over_x(shift):
    return [(x * CORES + k, (x + shift) % X * CORES + k) for x in range(X) for k in range(CORES)]


def over_core():
    return [(i, i ^ 1) for i in range(X * CORES)]


def over_row(flip):
    return [(i, i ^ flip) for i in range(ROWS)]


def over_near(shift):
    return [(f * NEAR + y, f * NEAR + (y + shift) % NEAR) for f in range(FAR) for y in range(NEAR)]


def over_far():
    return [(i, (i + NEAR) % (FAR * NEAR)) for i in range(FAR * NEAR)]


def partial_kernel(live, places, *refs):
    (where_ref, pieces, weight_ref, tokens, sums, sems) = (
        refs[0], refs[1:1 + len(places)], refs[1 + len(places)], refs[2 + len(places)], refs[3 + len(places):-1], refs[-1])
    copies = []
    n = 0
    for piece, blocks in zip(pieces, places):
        for place in range(blocks):
            copies.append(pltpu.make_async_copy(
                piece.at[pl.ds(place * live, live)],
                tokens.at[pl.ds(pl.multiple_of(where_ref[n] * live, live), live)],
                sems.at[n]))
            n += 1
    for copy in copies:
        copy.start()
    for copy in copies:
        copy.wait()
    width = sums[0].shape[1]
    group = max(256 // width, 1)
    for first in range(0, NEAR, group):
        result = lax.dot_general(
            weight_ref[...], tokens[first * width:(first + group) * width],
            (((1,), (1,)), ((), ())), preferred_element_type=jnp.float32)
        for j in range(group):
            sums[first + j][...] = result[:, j * width:(j + 1) * width]


def partials(pieces, places, where, weight, live):
    features, hidden = weight.shape
    width = 4 * live
    rows = NEAR * width
    out_shape = [jax.ShapeDtypeStruct((rows, hidden), jnp.bfloat16)]
    out_shape += [jax.ShapeDtypeStruct((features, width), jnp.float32)] * NEAR
    vmem = pl.BlockSpec(memory_space=pltpu.VMEM)
    return pl.pallas_call(
        functools.partial(partial_kernel, live, places),
        out_shape=out_shape,
        in_specs=[pl.BlockSpec(memory_space=pltpu.SMEM)] + [pl.BlockSpec(memory_space=pl.ANY)] * len(pieces) + [vmem],
        out_specs=[vmem] * (1 + NEAR),
        scratch_shapes=[pltpu.SemaphoreType.DMA((sum(places),))],
        compiler_params=pltpu.CompilerParams(vmem_limit_bytes=40 << 20),
        cost_estimate=pl.CostEstimate(
            flops=2 * rows * hidden * features, bytes_accessed=4 * rows * hidden, transcendentals=0),
    )(where, *pieces, weight)


def weight_grad_kernel(chunks, *refs):
    inputs, tokens, out, held = refs[:NEAR], refs[NEAR:NEAR + chunks], refs[-2], refs[-1]
    features, width = out.shape[0], inputs[0].shape[1]
    for k in range(chunks):
        for y in range(NEAR):
            first = (k * NEAR + y) * width
            held[:, first:first + width] = inputs[y][k * features:(k + 1) * features, :]
    step = 128
    hidden = out.shape[1]
    rows = NEAR * width
    for first in range(0, hidden, 256):
        last = min(first + 256, hidden)
        total = None
        for k in range(chunks):
            part = lax.dot_general(
                held[:, k * rows:(k + 1) * rows], tokens[k][:, first:last],
                (((1,), (0,)), ((), ())), preferred_element_type=jnp.float32)
            total = part if total is None else total + part
        out[:, first:last] = total.astype(out.dtype)


def weight_grad(inputs, tokens):
    chunks = len(tokens)
    features = inputs[0].shape[0] // chunks
    rows, hidden = tokens[0].shape
    vmem = pl.BlockSpec(memory_space=pltpu.VMEM)
    return pl.pallas_call(
        functools.partial(weight_grad_kernel, chunks),
        out_shape=jax.ShapeDtypeStruct((features, hidden), jnp.bfloat16),
        in_specs=[vmem] * (NEAR + chunks),
        out_specs=vmem,
        scratch_shapes=[pltpu.VMEM((features, chunks * rows), jnp.bfloat16)],
        compiler_params=pltpu.CompilerParams(vmem_limit_bytes=40 << 20),
        cost_estimate=pl.CostEstimate(
            flops=2 * chunks * rows * hidden * features, bytes_accessed=2 * chunks * rows * hidden, transcendentals=0),
    )(*inputs, *tokens)


def on_device(activations, upstream, weight, bin_fill):
    bin_len, hidden = upstream.shape
    features = activations.shape[1]
    live = bin_len // CHUNKS
    dp, row, col = lax.axis_index("dp"), lax.axis_index("row"), lax.axis_index("col")
    x, core = dp // CORES, dp % CORES
    far, near = col // NEAR, col % NEAR

    slot_index = jnp.arange(bin_len, dtype=jnp.int32)
    masked = jnp.where((slot_index < bin_fill[0])[:, None], upstream, jnp.zeros_like(upstream))

    mine = activations.T.reshape(features, 2, CHUNKS, live)
    mine = mine.transpose(2, 0, 1, 3).reshape(CHUNKS * features, 2 * live)
    other = lax.ppermute(mine, "col", over_far())
    mine = jnp.where(far == 0, jnp.concatenate([mine, other], 1), jnp.concatenate([other, mine], 1))
    inputs = [None] * NEAR
    inputs[0] = mine
    up = down = mine
    for step in range(1, NEAR // 2 + 1):
        up = lax.ppermute(up, "col", over_near(1))
        inputs[-step % NEAR] = up
        if step < NEAR // 2:
            down = lax.ppermute(down, "col", over_near(-1))
            inputs[step] = down

    def place(x_of, core_of, flip):
        row_of = row ^ flip
        near_of = (x_of % 2 * 2 + core_of) * 2 + row_of // 2
        return ((near_of - near) % NEAR * 2 + x_of // 2) * 2 + row_of % 2

    tokens, sums = [], []
    for k in range(CHUNKS):
        block = masked[k * live:(k + 1) * live]
        four = jnp.concatenate([block] + [lax.ppermute(block, "row", over_row(flip)) for flip in (1, 2, 3)], 0)
        left = lax.ppermute(four, "dp", over_x(1))
        right = lax.ppermute(four, "dp", over_x(-1))
        across = [lax.ppermute(left[:2 * live], "dp", over_x(1)), lax.ppermute(right[2 * live:], "dp", over_x(-1))]
        own = [four, left, right] + across
        pieces = own + [lax.ppermute(piece, "dp", over_core()) for piece in own]
        places, where = [], []
        for core_of in (core, 1 - core):
            for x_of, flips in ((x, (0, 1, 2, 3)), ((x + 3) % X, (0, 1, 2, 3)), ((x + 1) % X, (0, 1, 2, 3)), ((x + 2) % X, (0, 1)), ((x + 2) % X, (2, 3))):
                places.append(len(flips))
                where += [place(x_of, core_of, flip) for flip in flips]
        held, *parts = partials(pieces, places, jnp.stack(where).astype(jnp.int32), weight, live)
        tokens.append(held)
        up, down = parts[4], parts[5]
        for step in range(1, 5):
            up = lax.ppermute(up, "col", over_near(1)) + parts[4 - step]
            if step < 4:
                down = lax.ppermute(down, "col", over_near(-1))
                if step < 3:
                    down = down + parts[5 + step]
        sums.append(up + down)

    half = 2 * live
    keep = jnp.concatenate([jnp.where(far == 0, s[:, :half], s[:, half:]) for s in sums], 1)
    send = jnp.concatenate([jnp.where(far == 0, s[:, half:], s[:, :half]) for s in sums], 1)
    total = keep + lax.ppermute(send, "col", over_far())
    d_input = total.reshape(features, CHUNKS, 2, live).transpose(0, 2, 1, 3).reshape(features, 2 * bin_len)
    d_input = d_input.T.astype(jnp.bfloat16)
    return d_input, weight_grad(inputs, tokens)


def solution(mesh):
    in_specs = (
        P("col", ("dp", "row")),
        P(("dp", "row"), "col"),
        P(("dp", "row"), "col"),
        P(("dp", "row")),
    )
    out_specs = (P("col", ("dp", "row")), P(("dp", "row"), "col"))
    return jax.shard_map(
        on_device, mesh=mesh, in_specs=in_specs, out_specs=out_specs, check_vma=False
    )
```

time: 318 us -> 204 us (0.64)
  the two profiles are of different devices: /device:TPU:1 before, /device:TPU:64 now
where the time goes in v1:
time: 204 us; the launch traced here: 202 us
  starting transfers between devices  158 us (77%)
  Pallas kernels  16.4 us (8%)
  waiting for transfers between devices  16 us (8%)
  local copies, waits for them, and re-layouts  6.86 us (3%)
  between operations  3.52 us (2%)
    ppermute x9, starting transfers between devices, on_device(): down = lax.ppermute(down, 'col', over_near(-1))  43.5 us
    ppermute x6, starting transfers between devices, on_device(): lax.ppermute(block, 'row', over_row(flip))  23.2 us
    ppermute x10, starting transfers between devices, on_device(): pieces = own + [lax.ppermute(piece, 'dp', over_core()) for piece in own]  21.1 us
    ppermute x8, starting transfers between devices, on_device(): up = lax.ppermute(up, 'col', over_near(1)) + parts[4 - step]  18.5 us
    pallas_call x2, Pallas kernels, partials(): pl.pallas_call(functools.partial(partial_kernel, live, places), out_shape...  13.2 us
    ppermute x2, starting transfers between devices, on_device(): lax.ppermute(right[2 * live:], 'dp', over_x(-1))  10.3 us
    ppermute x2, starting transfers between devices, on_device(): right = lax.ppermute(four, 'dp', over_x(-1))  10.3 us
    ppermute x4, starting transfers between devices, on_device(): up = lax.ppermute(up, 'col', over_near(1))  9.26 us
  transfers between devices with their start and end apart: 47, of which 5 were waited for; matrix products, arithmetic and copies ran while one was open for 2% of the time, Pallas kernels for 8%

profile of v1, /device:TPU:64, one launch (start us, length us, event | category | flops | bytes accessed | tf_op | source)
XLA Modules:
  0.0 202.3 jit_solution(14647053270480581921)
XLA Ops:
  2.5 4.3 %collective-permute-start.21 = (bf16[32,1856]{1,0:T(8,128)(2,1)S(1)}, bf16[32,1856]{1,0:T(8,128)(2,1)S(1)}, u32[]{:S(2)}, u32[]{:S(2)}) collective-permute-start(bf16[32,1856]{1,0:T(8,128)(2,1)S(1)} %get-tuple-element.41), channel_id=1, source_target_pairs={{0,48},{16,32},{32,16},{48,0},{1,49},{17,33},{33,17},{49,1},{2,50}... | collective-permute-start | bytes 356360 | tf_op jit(solution)/shard_map/ppermute | solution.py:150
  6.7 6.9 %collective-permute-start.20 = (bf16[32,1856]{1,0:T(8,128)(2,1)S(1)}, bf16[32,1856]{1,0:T(8,128)(2,1)S(1)}, u32[]{:S(2)}, u32[]{:S(2)}) collective-permute-start(bf16[32,1856]{1,0:T(8,128)(2,1)S(1)} %get-tuple-element.41), channel_id=1, source_target_pairs={{0,32},{16,48},{32,0},{48,16},{1,33},{17,49},{33,1},{49,17},{2,34}... | collective-permute-start | bytes 356360 | tf_op jit(solution)/shard_map/ppermute | solution.py:150
  15.6 2.5 %collective-permute-start.2 = (bf16[32,1856]{1,0:T(8,128)(2,1)S(1)}, bf16[32,1856]{1,0:T(8,128)(2,1)S(1)}, u32[]{:S(2)}, u32[]{:S(2)}) collective-permute-start(bf16[32,1856]{1,0:T(8,128)(2,1)S(1)} %get-tuple-element.40), channel_id=1, source_target_pairs={{0,48},{16,32},{32,16},{48,0},{1,49},{17,33},{33,17},{49,1},{2,50}... | collective-permute-start | bytes 356360 | tf_op jit(solution)/shard_map/ppermute | solution.py:150
  18.1 5.7 %collective-permute-start.1 = (bf16[32,1856]{1,0:T(8,128)(2,1)S(1)}, bf16[32,1856]{1,0:T(8,128)(2,1)S(1)}, u32[]{:S(2)}, u32[]{:S(2)}) collective-permute-start(bf16[32,1856]{1,0:T(8,128)(2,1)S(1)} %get-tuple-element.40), channel_id=1, source_target_pairs={{0,32},{16,48},{32,0},{48,16},{1,33},{17,49},{33,1},{49,17},{2,34}... | collective-permute-start | bytes 356360 | tf_op jit(solution)/shard_map/ppermute | solution.py:150
  27.7 5.1 %collective-permute-start.23 = (bf16[128,1856]{1,0:T(8,128)(2,1)S(1)}, bf16[128,1856]{1,0:T(8,128)(2,1)}, u32[]{:S(2)}, u32[]{:S(2)}) collective-permute-start(bf16[128,1856]{1,0:T(8,128)(2,1)S(1)} %pad_maximum_fusion.1.refs_1_), channel_id=1, source_target_pairs={{0,384},{64,448},{128,0},{192,64},{256,128},{320,192},{384,256},{4... | collective-permute-start | bytes 1425416 | tf_op jit(solution)/shard_map/ppermute | solution.py:152
  36.8 5.1 %collective-permute-start.4 = (bf16[128,1856]{1,0:T(8,128)(2,1)S(1)}, bf16[128,1856]{1,0:T(8,128)(2,1)S(1)}, u32[]{:S(2)}, u32[]{:S(2)}) collective-permute-start(bf16[128,1856]{1,0:T(8,128)(2,1)S(1)} %pad_maximum_fusion.refs_1_), channel_id=1, source_target_pairs={{0,384},{64,448},{128,0},{192,64},{256,128},{320,192},{384,256},{4... | collective-permute-start | bytes 1425416 | tf_op jit(solution)/shard_map/ppermute | solution.py:152
  43.2 6.5 %collective-permute-start.39 = (bf16[464,64]{1,0:T(8,128)(2,1)S(1)}, bf16[464,64]{1,0:T(8,128)(2,1)S(1)}, u32[]{:S(2)}, u32[]{:S(2)}) collective-permute-start(bf16[464,64]{1,0:T(8,128)(2,1)S(1)} %copy.13), channel_id=1, source_target_pairs={{0,8},{1,9},{2,10},{3,11},{4,12},{5,13},{6,14},{7,15},{8,0},{9,1},... | collective-permute-start | bytes 178184 | tf_op jit(solution)/shard_map/ppermute | solution.py:130
  49.7 7.1 %collective-permute-done.39 = bf16[464,64]{1,0:T(8,128)(2,1)S(1)} collective-permute-done((bf16[464,64]{1,0:T(8,128)(2,1)S(1)}, bf16[464,64]{1,0:T(8,128)(2,1)S(1)}, u32[]{:S(2)}, u32[]{:S(2)}) %collective-permute-start.39) | collective-permute-done | bytes 59424 | tf_op jit(solution)/shard_map/ppermute | solution.py:130
  60.7 2.4 %collective-permute-start.28 = (bf16[128,1856]{1,0:T(8,128)(2,1)}, bf16[128,1856]{1,0:T(8,128)(2,1)S(1)}, u32[]{:S(2)}, u32[]{:S(2)}) collective-permute-start(bf16[128,1856]{1,0:T(8,128)(2,1)} %collective-permute-done.23.refs_3_), channel_id=1, source_target_pairs={{0,64},{64,0},{128,192},{192,128},{256,320},{320,256},{384,448},{4... | collective-permute-start | bytes 1425416 | tf_op jit(solution)/shard_map/ppermute | solution.py:155
  64.1 5.1 %collective-permute-start.25 = (bf16[64,1856]{1,0:T(8,128)(2,1)S(1)}, bf16[64,1856]{1,0:T(8,128)(2,1)}, u32[]{:S(2)}, u32[]{:S(2)}) collective-permute-start(bf16[64,1856]{1,0:T(8,128)(2,1)S(1)} %slice.51), channel_id=1, source_target_pairs={{0,384},{64,448},{128,0},{192,64},{256,128},{320,192},{384,256},{4... | collective-permute-start | bytes 712712 | tf_op jit(solution)/shard_map/ppermute | solution.py:153
  71.2 5.1 %collective-permute-start.6 = (bf16[64,1856]{1,0:T(8,128)(2,1)S(1)}, bf16[64,1856]{1,0:T(8,128)(2,1)S(1)}, u32[]{:S(2)}, u32[]{:S(2)}) collective-permute-start(bf16[64,1856]{1,0:T(8,128)(2,1)S(1)} %slice.46), channel_id=1, source_target_pairs={{0,384},{64,448},{128,0},{192,64},{256,128},{320,192},{384,256},{4... | collective-permute-start | bytes 712712 | tf_op jit(solution)/shard_map/ppermute | solution.py:153
  81.9 2.4 %collective-permute-start.9 = (bf16[128,1856]{1,0:T(8,128)(2,1)S(1)}, bf16[128,1856]{1,0:T(8,128)(2,1)}, u32[]{:S(2)}, u32[]{:S(2)}) collective-permute-start(bf16[128,1856]{1,0:T(8,128)(2,1)S(1)} %collective-permute-done.4.refs_3_), channel_id=1, source_target_pairs={{0,64},{64,0},{128,192},{192,128},{256,320},{320,256},{384,448},{4... | collective-permute-start | bytes 1425416 | tf_op jit(solution)/shard_map/ppermute | solution.py:155
  87.8 2.4 %collective-permute-start.30 = (bf16[64,1856]{1,0:T(8,128)(2,1)}, bf16[64,1856]{1,0:T(8,128)(2,1)}, u32[]{:S(2)}, u32[]{:S(2)}) collective-permute-start(bf16[64,1856]{1,0:T(8,128)(2,1)} %collective-permute-done.25.refs_5_), channel_id=1, source_target_pairs={{0,64},{64,0},{128,192},{192,128},{256,320},{320,256},{384,448},{4... | collective-permute-start | bytes 712712 | tf_op jit(solution)/shard_map/ppermute | solution.py:155
  93.2 2.4 %collective-permute-start.11 = (bf16[64,1856]{1,0:T(8,128)(2,1)}, bf16[64,1856]{1,0:T(8,128)(2,1)}, u32[]{:S(2)}, u32[]{:S(2)}) collective-permute-start(bf16[64,1856]{1,0:T(8,128)(2,1)} %copy-done.7), channel_id=1, source_target_pairs={{0,64},{64,0},{128,192},{192,128},{256,320},{320,256},{384,448},{4... | collective-permute-start | bytes 712712 | tf_op jit(solution)/shard_map/ppermute | solution.py:155
  97.9 6.3 %shard_map.60 = (bf16[1024,1856]{1,0:T(8,128)(2,1)S(1)}, f32[232,128]{1,0:T(8,128)S(1)}, f32[232,128]{1,0:T(8,128)S(1)}, f32[232,128]{1,0:T(8,128)S(1)}, f32[232...) custom-call(s32[32]{0:T(128)S(1)} %stack.164.refs_0_, ...), custom_call_target="tpu_custom_call" | custom-call | flops 881852416 | bytes 7602176 | tf_op jit(solution)/shard_map/pallas_call | solution.py:67
  104.3 2.4 %collective-permute-start.31 = (f32[232,128]{1,0:T(8,128)S(1)}, f32[232,128]{1,0:T(8,128)S(1)}, u32[]{:S(2)}, u32[]{:S(2)}) collective-permute-start(f32[232,128]{1,0:T(8,128)S(1)} %get-tuple-element.28), channel_id=1, source_target_pairs={{0,1},{1,2},{2,3},{3,4},{4,5},{5,6},{6,7},{7,0},{8,9},{9,10},{10,1... | collective-permute-start | bytes 356360 | tf_op jit(solution)/shard_map/ppermute | solution.py:165
  106.9 3.5 %collective-permute-start.43 = (bf16[464,128]{1,0:T(8,128)(2,1)S(1)}, bf16[464,128]{1,0:T(8,128)(2,1)S(1)}, u32[]{:S(2)}, u32[]{:S(2)}) collective-permute-start(bf16[464,128]{1,0:T(8,128)(2,1)S(1)} %maximum_select_fusion.refs_0_), channel_id=1, source_target_pairs={{0,1},{1,2},{2,3},{3,4},{4,5},{5,6},{6,7},{7,0},{8,9},{9,10},{10,1... | collective-permute-start | bytes 356360 | tf_op jit(solution)/shard_map/ppermute | solution.py:136
  110.4 6.8 %shard_map.59 = (bf16[1024,1856]{1,0:T(8,128)(2,1)S(1)}, f32[232,128]{1,0:T(8,128)S(1)}, f32[232,128]{1,0:T(8,128)S(1)}, f32[232,128]{1,0:T(8,128)S(1)}, f32[232...) custom-call(s32[32]{0:T(128)S(1)} %stack.164.refs_0_, ...), custom_call_target="tpu_custom_call" | custom-call | flops 881852416 | bytes 7602176 | tf_op jit(solution)/shard_map/pallas_call | solution.py:67
  117.3 3.5 %collective-permute-start.12 = (f32[232,128]{1,0:T(8,128)S(1)}, f32[232,128]{1,0:T(8,128)S(1)}, u32[]{:S(2)}, u32[]{:S(2)}) collective-permute-start(f32[232,128]{1,0:T(8,128)S(1)} %get-tuple-element.20), channel_id=1, source_target_pairs={{0,1},{1,2},{2,3},{3,4},{4,5},{5,6},{6,7},{7,0},{8,9},{9,10},{10,1... | collective-permute-start | bytes 356360 | tf_op jit(solution)/shard_map/ppermute | solution.py:165
  120.7 3.6 %collective-permute-start.35 = (f32[232,128]{1,0:T(8,128)S(1)}, f32[232,128]{1,0:T(8,128)S(1)}, u32[]{:S(2)}, u32[]{:S(2)}) collective-permute-start(f32[232,128]{1,0:T(8,128)S(1)} %get-tuple-element.33), channel_id=1, source_target_pairs={{0,7},{1,0},{2,1},{3,2},{4,3},{5,4},{6,5},{7,6},{8,15},{9,8},{10,9... | collective-permute-start | bytes 356360 | tf_op jit(solution)/shard_map/ppermute | solution.py:167
  124.4 3.0 %collective-permute-start.32 = (f32[232,128]{1,0:T(8,128)S(1)}, f32[232,128]{1,0:T(8,128)S(1)}, u32[]{:S(2)}, u32[]{:S(2)}) collective-permute-start(f32[232,128]{1,0:T(8,128)S(1)} %add.1001), channel_id=1, source_target_pairs={{0,1},{1,2},{2,3},{3,4},{4,5},{5,6},{6,7},{7,0},{8,9},{9,10},{10,1... | collective-permute-start | bytes 356360 | tf_op jit(solution)/shard_map/ppermute | solution.py:165
  127.4 4.0 %collective-permute-start.40 = (bf16[464,128]{1,0:T(8,128)(2,1)S(1)}, bf16[464,128]{1,0:T(8,128)(2,1)S(1)}, u32[]{:S(2)}, u32[]{:S(2)}) collective-permute-start(bf16[464,128]{1,0:T(8,128)(2,1)S(1)} %maximum_select_fusion.refs_0_), channel_id=1, source_target_pairs={{0,7},{1,0},{2,1},{3,2},{4,3},{5,4},{6,5},{7,6},{8,15},{9,8},{10,9... | collective-permute-start | bytes 356360 | tf_op jit(solution)/shard_map/ppermute | solution.py:139
  133.4 5.1 %collective-permute-start.16 = (f32[232,128]{1,0:T(8,128)S(1)}, f32[232,128]{1,0:T(8,128)S(1)}, u32[]{:S(2)}, u32[]{:S(2)}) collective-permute-start(f32[232,128]{1,0:T(8,128)S(1)} %get-tuple-element.25), channel_id=1, source_target_pairs={{0,7},{1,0},{2,1},{3,2},{4,3},{5,4},{6,5},{7,6},{8,15},{9,8},{10,9... | collective-permute-start | bytes 356360 | tf_op jit(solution)/shard_map/ppermute | solution.py:167
  140.5 5.1 %collective-permute-start.36 = (f32[232,128]{1,0:T(8,128)S(1)}, f32[232,128]{1,0:T(8,128)S(1)}, u32[]{:S(2)}, u32[]{:S(2)}) collective-permute-start(f32[232,128]{1,0:T(8,128)S(1)} %add.1005), channel_id=1, source_target_pairs={{0,7},{1,0},{2,1},{3,2},{4,3},{5,4},{6,5},{7,6},{8,15},{9,8},{10,9... | collective-permute-start | bytes 356360 | tf_op jit(solution)/shard_map/ppermute | solution.py:167
  147.6 5.1 %collective-permute-start.41 = (bf16[464,128]{1,0:T(8,128)(2,1)S(1)}, bf16[464,128]{1,0:T(8,128)(2,1)S(1)}, u32[]{:S(2)}, u32[]{:S(2)}) collective-permute-start(bf16[464,128]{1,0:T(8,128)(2,1)S(1)} %collective-permute-done.40.refs_1_), channel_id=1, source_target_pairs={{0,7},{1,0},{2,1},{3,2},{4,3},{5,4},{6,5},{7,6},{8,15},{9,8},{10,9... | collective-permute-start | bytes 356360 | tf_op jit(solution)/shard_map/ppermute | solution.py:139
  154.7 5.1 %collective-permute-start.17 = (f32[232,128]{1,0:T(8,128)S(1)}, f32[232,128]{1,0:T(8,128)S(1)}, u32[]{:S(2)}, u32[]{:S(2)}) collective-permute-start(f32[232,128]{1,0:T(8,128)S(1)} %add.998), channel_id=1, source_target_pairs={{0,7},{1,0},{2,1},{3,2},{4,3},{5,4},{6,5},{7,6},{8,15},{9,8},{10,9... | collective-permute-start | bytes 356360 | tf_op jit(solution)/shard_map/ppermute | solution.py:167
  161.9 5.1 %collective-permute-start.37 = (f32[232,128]{1,0:T(8,128)S(1)}, f32[232,128]{1,0:T(8,128)S(1)}, u32[]{:S(2)}, u32[]{:S(2)}) collective-permute-start(f32[232,128]{1,0:T(8,128)S(1)} %add.1006), channel_id=1, source_target_pairs={{0,7},{1,0},{2,1},{3,2},{4,3},{5,4},{6,5},{7,6},{8,15},{9,8},{10,9... | collective-permute-start | bytes 356360 | tf_op jit(solution)/shard_map/ppermute | solution.py:167
  169.0 5.1 %collective-permute-start.42 = (bf16[464,128]{1,0:T(8,128)(2,1)S(1)}, bf16[464,128]{1,0:T(8,128)(2,1)S(1)}, u32[]{:S(2)}, u32[]{:S(2)}) collective-permute-start(bf16[464,128]{1,0:T(8,128)(2,1)S(1)} %collective-permute-done.41.refs_2_), channel_id=1, source_target_pairs={{0,7},{1,0},{2,1},{3,2},{4,3},{5,4},{6,5},{7,6},{8,15},{9,8},{10,9... | collective-permute-start | bytes 356360 | tf_op jit(solution)/shard_map/ppermute | solution.py:139
  176.1 5.1 %collective-permute-start.18 = (f32[232,128]{1,0:T(8,128)S(1)}, f32[232,128]{1,0:T(8,128)S(1)}, u32[]{:S(2)}, u32[]{:S(2)}) collective-permute-start(f32[232,128]{1,0:T(8,128)S(1)} %add.999), channel_id=1, source_target_pairs={{0,7},{1,0},{2,1},{3,2},{4,3},{5,4},{6,5},{7,6},{8,15},{9,8},{10,9... | collective-permute-start | bytes 356360 | tf_op jit(solution)/shard_map/ppermute | solution.py:167
  183.6 5.6 %collective-permute-done.15 = f32[232,128]{1,0:T(8,128)S(1)} collective-permute-done((f32[232,128]{1,0:T(8,128)S(1)}, f32[232,128]{1,0:T(8,128)S(1)}, u32[]{:S(2)}, u32[]{:S(2)}) %collective-permute-start.15) | collective-permute-done | bytes 118816 | tf_op jit(solution)/shard_map/ppermute | solution.py:165
  189.5 7.4 %collective-permute-start.38 = (f32[232,128]{1,0:T(8,128)S(1)}, f32[232,128]{1,0:T(8,128)S(1)}, u32[]{:S(2)}, u32[]{:S(2)}) collective-permute-start(f32[232,128]{1,0:T(8,128)S(1)} %pad_maximum_fusion.2), channel_id=1, source_target_pairs={{0,8},{1,9},{2,10},{3,11},{4,12},{5,13},{6,14},{7,15},{8,0},{9,1},... | collective-permute-start | bytes 356360 | tf_op jit(solution)/shard_map/ppermute | solution.py:175
  196.9 3.2 %shard_map.61 = bf16[232,1856]{1,0:T(8,128)(2,1)} custom-call(bf16[464,128]{1,0:T(8,128)(2,1)S(1)} %maximum_select_fusion.refs_0_, bf16[464,128]{1,0:T(8,128)(2,1)S(1)} %collective-permute-done.40.refs_1_, bf16[464,128]{1,0:T(8,128)(2,1)S(1)} %collective-permute-done.41.refs_2_, bf16[464,128]{1,0:T(8,128)(2,1)S(1)} %collective-permute-done.42.refs_3_, ...), custom_call_target="tpu_custom_call" | custom-call | flops 1763704832 | bytes 7602176 | tf_op jit(solution)/shard_map/pallas_call | solution.py:105
  (121 shorter events, 50.5 us)
Async XLA Ops:
  2.5 21.4 %collective-permute-start.21 = (bf16[32,1856]{1,0:T(8,128)(2,1)S(1)}, bf16[32,1856]{1,0:T(8,128)(2,1)S(1)}, u32[]{:S(2)}, u32[]{:S(2)}) collective-permute-start(bf16[32,1856]{1,0:T(8,128)(2,1)S(1)} %get-tuple-element.41), channel_id=1, source_target_pairs={{0,48},{16,32},{32,16},{48,0},{1,49},{17,33},{33,17},{49,1},{2,50}... | collective-permute-start | bytes 356360 | tf_op jit(solution)/shard_map/ppermute | solution.py:150
  6.7 19.0 %collective-permute-start.20 = (bf16[32,1856]{1,0:T(8,128)(2,1)S(1)}, bf16[32,1856]{1,0:T(8,128)(2,1)S(1)}, u32[]{:S(2)}, u32[]{:S(2)}) collective-permute-start(bf16[32,1856]{1,0:T(8,128)(2,1)S(1)} %get-tuple-element.41), channel_id=1, source_target_pairs={{0,32},{16,48},{32,0},{48,16},{1,33},{17,49},{33,1},{49,17},{2,34}... | collective-permute-start | bytes 356360 | tf_op jit(solution)/shard_map/ppermute | solution.py:150
  15.6 17.3 %collective-permute-start.2 = (bf16[32,1856]{1,0:T(8,128)(2,1)S(1)}, bf16[32,1856]{1,0:T(8,128)(2,1)S(1)}, u32[]{:S(2)}, u32[]{:S(2)}) collective-permute-start(bf16[32,1856]{1,0:T(8,128)(2,1)S(1)} %get-tuple-element.40), channel_id=1, source_target_pairs={{0,48},{16,32},{32,16},{48,0},{1,49},{17,33},{33,17},{49,1},{2,50}... | collective-permute-start | bytes 356360 | tf_op jit(solution)/shard_map/ppermute | solution.py:150
  18.1 16.7 %collective-permute-start.1 = (bf16[32,1856]{1,0:T(8,128)(2,1)S(1)}, bf16[32,1856]{1,0:T(8,128)(2,1)S(1)}, u32[]{:S(2)}, u32[]{:S(2)}) collective-permute-start(bf16[32,1856]{1,0:T(8,128)(2,1)S(1)} %get-tuple-element.40), channel_id=1, source_target_pairs={{0,32},{16,48},{32,0},{48,16},{1,33},{17,49},{33,1},{49,17},{2,34}... | collective-permute-start | bytes 356360 | tf_op jit(solution)/shard_map/ppermute | solution.py:150
  25.8 17.4 %collective-permute-start.22 = (bf16[128,1856]{1,0:T(8,128)(2,1)S(1)}, bf16[128,1856]{1,0:T(8,128)(2,1)S(1)}, u32[]{:S(2)}, u32[]{:S(2)}) collective-permute-start(bf16[128,1856]{1,0:T(8,128)(2,1)S(1)} %pad_maximum_fusion.1.refs_1_), channel_id=1, source_target_pairs={{0,128},{64,192},{128,256},{192,320},{256,384},{320,448},{384,0},{... | collective-permute-start | bytes 1425416 | tf_op jit(solution)/shard_map/ppermute | solution.py:151
  27.7 31.0 %collective-permute-start.23 = (bf16[128,1856]{1,0:T(8,128)(2,1)S(1)}, bf16[128,1856]{1,0:T(8,128)(2,1)}, u32[]{:S(2)}, u32[]{:S(2)}) collective-permute-start(bf16[128,1856]{1,0:T(8,128)(2,1)S(1)} %pad_maximum_fusion.1.refs_1_), channel_id=1, source_target_pairs={{0,384},{64,448},{128,0},{192,64},{256,128},{320,192},{384,256},{4... | collective-permute-start | bytes 1425416 | tf_op jit(solution)/shard_map/ppermute | solution.py:152
  32.9 27.8 %collective-permute-start.26 = (bf16[128,1856]{1,0:T(8,128)(2,1)S(1)}, bf16[128,1856]{1,0:T(8,128)(2,1)}, u32[]{:S(2)}, u32[]{:S(2)}) collective-permute-start(bf16[128,1856]{1,0:T(8,128)(2,1)S(1)} %pad_maximum_fusion.1.refs_1_), channel_id=1, source_target_pairs={{0,64},{64,0},{128,192},{192,128},{256,320},{320,256},{384,448},{4... | collective-permute-start | bytes 1425416 | tf_op jit(solution)/shard_map/ppermute | solution.py:155
  34.9 29.2 %collective-permute-start.3 = (bf16[128,1856]{1,0:T(8,128)(2,1)S(1)}, bf16[128,1856]{1,0:T(8,128)(2,1)S(1)}, u32[]{:S(2)}, u32[]{:S(2)}) collective-permute-start(bf16[128,1856]{1,0:T(8,128)(2,1)S(1)} %pad_maximum_fusion.refs_1_), channel_id=1, source_target_pairs={{0,128},{64,192},{128,256},{192,320},{256,384},{320,448},{384,0},{... | collective-permute-start | bytes 1425416 | tf_op jit(solution)/shard_map/ppermute | solution.py:151
  36.8 32.4 %collective-permute-start.4 = (bf16[128,1856]{1,0:T(8,128)(2,1)S(1)}, bf16[128,1856]{1,0:T(8,128)(2,1)S(1)}, u32[]{:S(2)}, u32[]{:S(2)}) collective-permute-start(bf16[128,1856]{1,0:T(8,128)(2,1)S(1)} %pad_maximum_fusion.refs_1_), channel_id=1, source_target_pairs={{0,384},{64,448},{128,0},{192,64},{256,128},{320,192},{384,256},{4... | collective-permute-start | bytes 1425416 | tf_op jit(solution)/shard_map/ppermute | solution.py:152
  58.8 25.6 %collective-permute-start.27 = (bf16[128,1856]{1,0:T(8,128)(2,1)S(1)}, bf16[128,1856]{1,0:T(8,128)(2,1)S(1)}, u32[]{:S(2)}, u32[]{:S(2)}) collective-permute-start(bf16[128,1856]{1,0:T(8,128)(2,1)S(1)} %collective-permute-done.22.refs_2_), channel_id=1, source_target_pairs={{0,64},{64,0},{128,192},{192,128},{256,320},{320,256},{384,448},{4... | collective-permute-start | bytes 1425416 | tf_op jit(solution)/shard_map/ppermute | solution.py:155
  60.7 26.3 %collective-permute-start.28 = (bf16[128,1856]{1,0:T(8,128)(2,1)}, bf16[128,1856]{1,0:T(8,128)(2,1)S(1)}, u32[]{:S(2)}, u32[]{:S(2)}) collective-permute-start(bf16[128,1856]{1,0:T(8,128)(2,1)} %collective-permute-done.23.refs_3_), channel_id=1, source_target_pairs={{0,64},{64,0},{128,192},{192,128},{256,320},{320,256},{384,448},{4... | collective-permute-start | bytes 1425416 | tf_op jit(solution)/shard_map/ppermute | solution.py:155
  76.4 27.9 %collective-permute-start.7 = (bf16[128,1856]{1,0:T(8,128)(2,1)S(1)}, bf16[128,1856]{1,0:T(8,128)(2,1)}, u32[]{:S(2)}, u32[]{:S(2)}) collective-permute-start(bf16[128,1856]{1,0:T(8,128)(2,1)S(1)} %pad_maximum_fusion.refs_1_), channel_id=1, source_target_pairs={{0,64},{64,0},{128,192},{192,128},{256,320},{320,256},{384,448},{4... | collective-permute-start | bytes 1425416 | tf_op jit(solution)/shard_map/ppermute | solution.py:155
  80.0 26.9 %collective-permute-start.8 = (bf16[128,1856]{1,0:T(8,128)(2,1)S(1)}, bf16[128,1856]{1,0:T(8,128)(2,1)}, u32[]{:S(2)}, u32[]{:S(2)}) collective-permute-start(bf16[128,1856]{1,0:T(8,128)(2,1)S(1)} %collective-permute-done.3.refs_2_), channel_id=1, source_target_pairs={{0,64},{64,0},{128,192},{192,128},{256,320},{320,256},{384,448},{4... | collective-permute-start | bytes 1425416 | tf_op jit(solution)/shard_map/ppermute | solution.py:155
  81.9 28.5 %collective-permute-start.9 = (bf16[128,1856]{1,0:T(8,128)(2,1)S(1)}, bf16[128,1856]{1,0:T(8,128)(2,1)}, u32[]{:S(2)}, u32[]{:S(2)}) collective-permute-start(bf16[128,1856]{1,0:T(8,128)(2,1)S(1)} %collective-permute-done.4.refs_3_), channel_id=1, source_target_pairs={{0,64},{64,0},{128,192},{192,128},{256,320},{320,256},{384,448},{4... | collective-permute-start | bytes 1425416 | tf_op jit(solution)/shard_map/ppermute | solution.py:155
  91.3 19.1 %collective-permute-start.10 = (bf16[64,1856]{1,0:T(8,128)(2,1)}, bf16[64,1856]{1,0:T(8,128)(2,1)}, u32[]{:S(2)}, u32[]{:S(2)}) collective-permute-start(bf16[64,1856]{1,0:T(8,128)(2,1)} %copy-done.5), channel_id=1, source_target_pairs={{0,64},{64,0},{128,192},{192,128},{256,320},{320,256},{384,448},{4... | collective-permute-start | bytes 712712 | tf_op jit(solution)/shard_map/ppermute | solution.py:155
  93.2 17.2 %collective-permute-start.11 = (bf16[64,1856]{1,0:T(8,128)(2,1)}, bf16[64,1856]{1,0:T(8,128)(2,1)}, u32[]{:S(2)}, u32[]{:S(2)}) collective-permute-start(bf16[64,1856]{1,0:T(8,128)(2,1)} %copy-done.7), channel_id=1, source_target_pairs={{0,64},{64,0},{128,192},{192,128},{256,320},{320,256},{384,448},{4... | collective-permute-start | bytes 712712 | tf_op jit(solution)/shard_map/ppermute | solution.py:155
  104.3 20.0 %collective-permute-start.31 = (f32[232,128]{1,0:T(8,128)S(1)}, f32[232,128]{1,0:T(8,128)S(1)}, u32[]{:S(2)}, u32[]{:S(2)}) collective-permute-start(f32[232,128]{1,0:T(8,128)S(1)} %get-tuple-element.28), channel_id=1, source_target_pairs={{0,1},{1,2},{2,3},{3,4},{4,5},{5,6},{6,7},{7,0},{8,9},{9,10},{10,1... | collective-permute-start | bytes 356360 | tf_op jit(solution)/shard_map/ppermute | solution.py:165
  106.9 24.6 %collective-permute-start.43 = (bf16[464,128]{1,0:T(8,128)(2,1)S(1)}, bf16[464,128]{1,0:T(8,128)(2,1)S(1)}, u32[]{:S(2)}, u32[]{:S(2)}) collective-permute-start(bf16[464,128]{1,0:T(8,128)(2,1)S(1)} %maximum_select_fusion.refs_0_), channel_id=1, source_target_pairs={{0,1},{1,2},{2,3},{3,4},{4,5},{5,6},{6,7},{7,0},{8,9},{9,10},{10,1... | collective-permute-start | bytes 356360 | tf_op jit(solution)/shard_map/ppermute | solution.py:136
  120.7 17.8 %collective-permute-start.35 = (f32[232,128]{1,0:T(8,128)S(1)}, f32[232,128]{1,0:T(8,128)S(1)}, u32[]{:S(2)}, u32[]{:S(2)}) collective-permute-start(f32[232,128]{1,0:T(8,128)S(1)} %get-tuple-element.33), channel_id=1, source_target_pairs={{0,7},{1,0},{2,1},{3,2},{4,3},{5,4},{6,5},{7,6},{8,15},{9,8},{10,9... | collective-permute-start | bytes 356360 | tf_op jit(solution)/shard_map/ppermute | solution.py:167
  127.4 18.3 %collective-permute-start.40 = (bf16[464,128]{1,0:T(8,128)(2,1)S(1)}, bf16[464,128]{1,0:T(8,128)(2,1)S(1)}, u32[]{:S(2)}, u32[]{:S(2)}) collective-permute-start(bf16[464,128]{1,0:T(8,128)(2,1)S(1)} %maximum_select_fusion.refs_0_), channel_id=1, source_target_pairs={{0,7},{1,0},{2,1},{3,2},{4,3},{5,4},{6,5},{7,6},{8,15},{9,8},{10,9... | collective-permute-start | bytes 356360 | tf_op jit(solution)/shard_map/ppermute | solution.py:139
  131.4 16.2 %collective-permute-start.44 = (bf16[464,128]{1,0:T(8,128)(2,1)S(1)}, bf16[464,128]{1,0:T(8,128)(2,1)S(1)}, u32[]{:S(2)}, u32[]{:S(2)}) collective-permute-start(bf16[464,128]{1,0:T(8,128)(2,1)S(1)} %collective-permute-done.43.refs_7_), channel_id=1, source_target_pairs={{0,1},{1,2},{2,3},{3,4},{4,5},{5,6},{6,7},{7,0},{8,9},{9,10},{10,1... | collective-permute-start | bytes 356360 | tf_op jit(solution)/shard_map/ppermute | solution.py:136
  133.4 19.4 %collective-permute-start.16 = (f32[232,128]{1,0:T(8,128)S(1)}, f32[232,128]{1,0:T(8,128)S(1)}, u32[]{:S(2)}, u32[]{:S(2)}) collective-permute-start(f32[232,128]{1,0:T(8,128)S(1)} %get-tuple-element.25), channel_id=1, source_target_pairs={{0,7},{1,0},{2,1},{3,2},{4,3},{5,4},{6,5},{7,6},{8,15},{9,8},{10,9... | collective-permute-start | bytes 356360 | tf_op jit(solution)/shard_map/ppermute | solution.py:167
  138.6 16.2 %collective-permute-start.13 = (f32[232,128]{1,0:T(8,128)S(1)}, f32[232,128]{1,0:T(8,128)S(1)}, u32[]{:S(2)}, u32[]{:S(2)}) collective-permute-start(f32[232,128]{1,0:T(8,128)S(1)} %add.994), channel_id=1, source_target_pairs={{0,1},{1,2},{2,3},{3,4},{4,5},{5,6},{6,7},{7,0},{8,9},{9,10},{10,1... | collective-permute-start | bytes 356360 | tf_op jit(solution)/shard_map/ppermute | solution.py:165
  140.5 19.4 %collective-permute-start.36 = (f32[232,128]{1,0:T(8,128)S(1)}, f32[232,128]{1,0:T(8,128)S(1)}, u32[]{:S(2)}, u32[]{:S(2)}) collective-permute-start(f32[232,128]{1,0:T(8,128)S(1)} %add.1005), channel_id=1, source_target_pairs={{0,7},{1,0},{2,1},{3,2},{4,3},{5,4},{6,5},{7,6},{8,15},{9,8},{10,9... | collective-permute-start | bytes 356360 | tf_op jit(solution)/shard_map/ppermute | solution.py:167
  145.7 16.2 %collective-permute-start.33 = (f32[232,128]{1,0:T(8,128)S(1)}, f32[232,128]{1,0:T(8,128)S(1)}, u32[]{:S(2)}, u32[]{:S(2)}) collective-permute-start(f32[232,128]{1,0:T(8,128)S(1)} %add.1002), channel_id=1, source_target_pairs={{0,1},{1,2},{2,3},{3,4},{4,5},{5,6},{6,7},{7,0},{8,9},{9,10},{10,1... | collective-permute-start | bytes 356360 | tf_op jit(solution)/shard_map/ppermute | solution.py:165
  147.6 19.4 %collective-permute-start.41 = (bf16[464,128]{1,0:T(8,128)(2,1)S(1)}, bf16[464,128]{1,0:T(8,128)(2,1)S(1)}, u32[]{:S(2)}, u32[]{:S(2)}) collective-permute-start(bf16[464,128]{1,0:T(8,128)(2,1)S(1)} %collective-permute-done.40.refs_1_), channel_id=1, source_target_pairs={{0,7},{1,0},{2,1},{3,2},{4,3},{5,4},{6,5},{7,6},{8,15},{9,8},{10,9... | collective-permute-start | bytes 356360 | tf_op jit(solution)/shard_map/ppermute | solution.py:139
  152.8 16.2 %collective-permute-start.45 = (bf16[464,128]{1,0:T(8,128)(2,1)S(1)}, bf16[464,128]{1,0:T(8,128)(2,1)S(1)}, u32[]{:S(2)}, u32[]{:S(2)}) collective-permute-start(bf16[464,128]{1,0:T(8,128)(2,1)S(1)} %collective-permute-done.44.refs_6_), channel_id=1, source_target_pairs={{0,1},{1,2},{2,3},{3,4},{4,5},{5,6},{6,7},{7,0},{8,9},{9,10},{10,1... | collective-permute-start | bytes 356360 | tf_op jit(solution)/shard_map/ppermute | solution.py:136
  154.7 19.4 %collective-permute-start.17 = (f32[232,128]{1,0:T(8,128)S(1)}, f32[232,128]{1,0:T(8,128)S(1)}, u32[]{:S(2)}, u32[]{:S(2)}) collective-permute-start(f32[232,128]{1,0:T(8,128)S(1)} %add.998), channel_id=1, source_target_pairs={{0,7},{1,0},{2,1},{3,2},{4,3},{5,4},{6,5},{7,6},{8,15},{9,8},{10,9... | collective-permute-start | bytes 356360 | tf_op jit(solution)/shard_map/ppermute | solution.py:167
  159.9 16.2 %collective-permute-start.14 = (f32[232,128]{1,0:T(8,128)S(1)}, f32[232,128]{1,0:T(8,128)S(1)}, u32[]{:S(2)}, u32[]{:S(2)}) collective-permute-start(f32[232,128]{1,0:T(8,128)S(1)} %add.995), channel_id=1, source_target_pairs={{0,1},{1,2},{2,3},{3,4},{4,5},{5,6},{6,7},{7,0},{8,9},{9,10},{10,1... | collective-permute-start | bytes 356360 | tf_op jit(solution)/shard_map/ppermute | solution.py:165
  161.9 19.4 %collective-permute-start.37 = (f32[232,128]{1,0:T(8,128)S(1)}, f32[232,128]{1,0:T(8,128)S(1)}, u32[]{:S(2)}, u32[]{:S(2)}) collective-permute-start(f32[232,128]{1,0:T(8,128)S(1)} %add.1006), channel_id=1, source_target_pairs={{0,7},{1,0},{2,1},{3,2},{4,3},{5,4},{6,5},{7,6},{8,15},{9,8},{10,9... | collective-permute-start | bytes 356360 | tf_op jit(solution)/shard_map/ppermute | solution.py:167
  169.0 27.9 %collective-permute-start.42 = (bf16[464,128]{1,0:T(8,128)(2,1)S(1)}, bf16[464,128]{1,0:T(8,128)(2,1)S(1)}, u32[]{:S(2)}, u32[]{:S(2)}) collective-permute-start(bf16[464,128]{1,0:T(8,128)(2,1)S(1)} %collective-permute-done.41.refs_2_), channel_id=1, source_target_pairs={{0,7},{1,0},{2,1},{3,2},{4,3},{5,4},{6,5},{7,6},{8,15},{9,8},{10,9... | collective-permute-start | bytes 356360 | tf_op jit(solution)/shard_map/ppermute | solution.py:139
  174.1 22.7 %collective-permute-start.46 = (bf16[464,128]{1,0:T(8,128)(2,1)S(1)}, bf16[464,128]{1,0:T(8,128)(2,1)S(1)}, u32[]{:S(2)}, u32[]{:S(2)}) collective-permute-start(bf16[464,128]{1,0:T(8,128)(2,1)S(1)} %collective-permute-done.45.refs_5_), channel_id=1, source_target_pairs={{0,1},{1,2},{2,3},{3,4},{4,5},{5,6},{6,7},{7,0},{8,9},{9,10},{10,1... | collective-permute-start | bytes 356360 | tf_op jit(solution)/shard_map/ppermute | solution.py:136
  (26 other events, 322.0 us)

commit v2 on v0

v2 whole, which is shorter than its diff:
```python
import functools

import jax
import jax.numpy as jnp
from jax import lax
from jax.experimental import pallas as pl
from jax.experimental.pallas import tpu as pltpu
from jax.sharding import Mesh
from jax.sharding import PartitionSpec as P

CHUNKS = 2
X, CORES, ROWS, FAR, NEAR = 4, 2, 4, 2, 8
BLOCKS = 4
VMEM = pl.BlockSpec(memory_space=pltpu.VMEM)


def flips(size, flip):
    return [(i, i ^ flip) for i in range(size)]


def partial_kernel(live, packed, where_ref, *refs):
    pieces, (weight_ref, tokens, sums, sems) = refs[:-4], refs[-4:]
    copies = []
    for i, piece in enumerate(pieces):
        for j in range(BLOCKS):
            n = i * BLOCKS + j
            copies.append(pltpu.make_async_copy(
                piece.at[pl.ds(j * live, live)],
                tokens.at[pl.ds(pl.multiple_of(where_ref[n] * live, live), live)],
                sems.at[n]))
    for copy in copies:
        copy.start()
    for copy in copies:
        copy.wait()
    features = weight_ref.shape[0]
    lanes = 128
    left = lax.broadcasted_iota(jnp.int32, (packed, lanes), 1) < lanes // 2
    for first in range(0, NEAR, 2):
        result = lax.dot_general(
            weight_ref[...], tokens[first * lanes:(first + 2) * lanes],
            (((1,), (1,)), ((), ())), preferred_element_type=jnp.float32)
        for j in range(2):
            here = result[:, j * lanes:(j + 1) * lanes]
            turned = pltpu.roll(here, lanes // 2, 1)
            sums[first + j] = jnp.where(left, here[:packed], turned[features - packed:])
            sums[NEAR + first + j] = jnp.where(left, turned[:packed], here[features - packed:])


def partials(pieces, where, weight, live, packed):
    features, hidden = weight.shape
    rows = BLOCKS * len(pieces) * live
    return pl.pallas_call(
        functools.partial(partial_kernel, live, packed),
        out_shape=[
            jax.ShapeDtypeStruct((rows, hidden), jnp.bfloat16),
            jax.ShapeDtypeStruct((FAR * NEAR, packed, 128), jnp.float32),
        ],
        in_specs=[pl.BlockSpec(memory_space=pltpu.SMEM)] + [pl.BlockSpec(memory_space=pl.ANY)] * len(pieces) + [VMEM],
        out_specs=[VMEM] * 2,
        scratch_shapes=[pltpu.SemaphoreType.DMA((BLOCKS * len(pieces),))],
        compiler_params=pltpu.CompilerParams(vmem_limit_bytes=40 << 20),
        cost_estimate=pl.CostEstimate(
            flops=2 * rows * hidden * features, bytes_accessed=4 * rows * hidden, transcendentals=0),
    )(where, *pieces, weight)


def weight_grad_kernel(inputs, *refs):
    tokens, (out, held) = refs[:-2], refs[-2:]
    features, hidden = out.shape
    width = inputs.shape[2]
    rows = NEAR * width
    for k in range(len(tokens)):
        for y in range(NEAR):
            first = k * rows + y * width
            held[:, first:first + width] = inputs[y, k * features:(k + 1) * features, :]
    for first in range(0, hidden, 256):
        last = min(first + 256, hidden)
        total = None
        for k in range(len(tokens)):
            part = lax.dot_general(
                held[:, k * rows:(k + 1) * rows], tokens[k][:, first:last],
                (((1,), (0,)), ((), ())), preferred_element_type=jnp.float32)
            total = part if total is None else total + part
        out[:, first:last] = total.astype(out.dtype)


def weight_grad(inputs, tokens):
    chunks = len(tokens)
    features = inputs.shape[1] // chunks
    rows, hidden = tokens[0].shape
    return pl.pallas_call(
        weight_grad_kernel,
        out_shape=jax.ShapeDtypeStruct((features, hidden), jnp.bfloat16),
        in_specs=[VMEM] * (1 + chunks),
        out_specs=VMEM,
        scratch_shapes=[pltpu.VMEM((features, chunks * rows), jnp.bfloat16)],
        compiler_params=pltpu.CompilerParams(vmem_limit_bytes=40 << 20),
        cost_estimate=pl.CostEstimate(
            flops=2 * chunks * rows * hidden * features, bytes_accessed=2 * chunks * rows * hidden, transcendentals=0),
    )(inputs, *tokens)


def add_kernel(first_ref, second_ref, out):
    features, lanes = out.shape
    parts = []
    for ref in (first_ref, second_ref):
        total = ref[0]
        for i in range(1, FAR * NEAR):
            total = total + ref[i]
        packed = total.shape[0]
        turned = pltpu.roll(total, lanes // 2, 1)
        parts.append(jnp.concatenate([total[:features - packed], turned], 0))
    first, second = parts
    lane = lax.broadcasted_iota(jnp.int32, (features, lanes), 1)
    quarter = lanes // 4
    result = jnp.where(
        lane < quarter, first,
        jnp.where(lane < 2 * quarter, pltpu.roll(second, quarter, 1),
                  jnp.where(lane < 3 * quarter, pltpu.roll(first, quarter, 1), pltpu.roll(second, 2 * quarter, 1))))
    out[...] = result.astype(out.dtype)


def add_up(received, features):
    return pl.pallas_call(
        add_kernel,
        out_shape=jax.ShapeDtypeStruct((features, 128), jnp.bfloat16),
        in_specs=[VMEM] * 2,
        out_specs=VMEM,
        compiler_params=pltpu.CompilerParams(vmem_limit_bytes=40 << 20),
    )(*received)


def on_device(activations, upstream, weight, bin_fill):
    bin_len, hidden = upstream.shape
    features = activations.shape[1]
    live = bin_len // CHUNKS
    packed = (features // 2 + 7) // 8 * 8
    x, core, row, far = (lax.axis_index(name) for name in ("x", "core", "row", "far"))

    slot_index = jnp.arange(bin_len, dtype=jnp.int32)
    masked = jnp.where((slot_index < bin_fill[0])[:, None], upstream, jnp.zeros_like(upstream))

    mine = activations.T.reshape(features, 2, CHUNKS, live)
    mine = mine.transpose(2, 0, 1, 3).reshape(CHUNKS * features, 2 * live)
    other = lax.ppermute(mine, "far", flips(FAR, 1))
    mine = jnp.where(far == 0, jnp.concatenate([mine, other], 1), jnp.concatenate([other, mine], 1))
    inputs = lax.all_to_all(jnp.broadcast_to(mine, (NEAR,) + mine.shape), "near", 0, 0)

    def place(x_of, core_of, row_of):
        near_of = (x_of % 2 * 2 + core_of) * 2 + row_of // 2
        return (near_of * 2 + x_of // 2) * 2 + row_of % 2

    tokens, received = [], []
    for k in range(CHUNKS):
        block = masked[k * live:(k + 1) * live]
        line = lax.all_to_all(jnp.broadcast_to(block, (ROWS,) + block.shape), "row", 0, 0)
        low, high = (line[:2].reshape(2 * live, hidden), line[2:].reshape(2 * live, hidden))
        low = jnp.concatenate([low, lax.ppermute(low, "x", flips(X, 1))], 0)
        high = jnp.concatenate([high, lax.ppermute(high, "x", flips(X, 3))], 0)
        own = [low, high, lax.ppermute(low, "x", flips(X, 3)), lax.ppermute(high, "x", flips(X, 1))]
        pieces = own + [lax.ppermute(piece, "core", flips(CORES, 1)) for piece in own]
        where = []
        for core_of in (core, 1 - core):
            for x_pair, rows in (((x, x ^ 1), (0, 1)), ((x, x ^ 3), (2, 3)), ((x ^ 3, x ^ 2), (0, 1)), ((x ^ 1, x ^ 2), (2, 3))):
                where += [place(x_of, core_of, row_of) for x_of in x_pair for row_of in rows]
        held, sums = partials(pieces, jnp.stack(where).astype(jnp.int32), weight, live, packed)
        tokens.append(held)
        received.append(lax.all_to_all(sums, ("far", "near"), 0, 0))
    d_weight = weight_grad(inputs, tokens)
    return add_up(received, features).T, d_weight


def solution(mesh):
    fine = Mesh(mesh.devices.reshape(X, CORES, ROWS, FAR, NEAR), ("x", "core", "row", "far", "near"))
    tall, wide = ("x", "core", "row"), ("far", "near")
    return jax.shard_map(
        on_device, mesh=fine,
        in_specs=(P(wide, tall), P(tall, wide), P(tall, wide), P(tall)),
        out_specs=(P(wide, tall), P(tall, wide)), check_vma=False,
    )
```

time: 318 us -> 190 us (0.60)
  waiting for transfers between devices: 228 us -> 33.8 us
  starting transfers between devices: 0.08 us -> 96.8 us
  blocking collectives: 54.3 us -> 20.6 us
  Pallas kernels: 0 us -> 18.6 us
  local copies, waits for them, and re-layouts: 0.02 us -> 14.3 us
  matrix products: 13.3 us -> 0 us
  between operations: 14.8 us -> 1.84 us
    reduce_scatter x1 -> x0, waiting for transfers between devices: 124 us -> none  [on_device(): lax.psum_scatter(grad_x, 'col', scatter_dimension=0, tiled=True)]
    all_gather x1 -> x0, waiting for transfers between devices: 104 us -> none  [on_device(): block_rows = lax.all_gather(masked, ('dp', 'row'), axis=0, tiled=True)]
    ppermute x0 -> x17, starting transfers between devices: none -> 63.4 us  [the longest x8 31.3 us: on_device(): lax.ppermute(piece, 'core', flips(CORES, 1))]
    all_gather x1 -> x0, blocking collectives: 54.3 us -> none  [on_device(): all_inputs = lax.all_gather(activations, 'col', axis=0, tiled=True)]
    all_to_all x0 -> x4, starting transfers between devices: none -> 33.4 us  [the longest x2 22.9 us: on_device(): received.append(lax.all_to_all(sums, ('far', 'near'), 0, 0))]
    all_to_all x0 -> x4, waiting for transfers between devices: none -> 20.6 us  [the longest x2 20.6 us: on_device(): received.append(lax.all_to_all(sums, ('far', 'near'), 0, 0))]
    all_to_all x0 -> x1, blocking collectives: none -> 20.6 us  [on_device(): lax.all_to_all(jnp.broadcast_to(block, (ROWS,) + block.shape), 'row', 0, 0)]
    pallas_call x0 -> x4, Pallas kernels: none -> 18.6 us  [the longest x2 14.6 us: partials(): pl.pallas_call(functools.partial(partial_kernel, live, packed), out_shape...]
  transfers between devices with their start and end apart: 2 -> 21, of which waited for: 2 -> 8; matrix products, arithmetic and copies ran while one was open for 2% -> 2% of each run, Pallas kernels for 0% -> 9%
where the time goes in v2:
time: 190 us; the launch traced here: 188 us
  starting transfers between devices  96.8 us (51%)
  waiting for transfers between devices  33.8 us (18%)
  blocking collectives  20.6 us (11%)
  Pallas kernels  18.6 us (10%)
  local copies, waits for them, and re-layouts  14.3 us (8%)
  other arithmetic  2.17 us (1%)
    ppermute x8, starting transfers between devices, on_device(): lax.ppermute(piece, 'core', flips(CORES, 1))  31.3 us
    all_to_all x2, starting transfers between devices, on_device(): received.append(lax.all_to_all(sums, ('far', 'near'), 0, 0))  22.9 us
    all_to_all x1, blocking collectives, on_device(): lax.all_to_all(jnp.broadcast_to(block, (ROWS,) + block.shape), 'row', 0, 0)  20.6 us
    all_to_all x2, waiting for transfers between devices, on_device(): received.append(lax.all_to_all(sums, ('far', 'near'), 0, 0))  20.6 us
    pallas_call x2, Pallas kernels, partials(): pl.pallas_call(functools.partial(partial_kernel, live, packed), out_shape...  14.6 us
    unnamed x19, local copies, waits for them, and re-layouts  10.1 us
    ppermute x2, starting transfers between devices, on_device(): high = jnp.concatenate([high, lax.ppermute(high, 'x', flips(X, 3))], 0)  9.44 us
    ppermute x1, starting transfers between devices, on_device(): other = lax.ppermute(mine, 'far', flips(FAR, 1))  7.91 us
  transfers between devices with their start and end apart: 21, of which 8 were waited for; matrix products, arithmetic and copies ran while one was open for 2% of the time, Pallas kernels for 9%

profile of v2, /device:TPU:1, one launch (start us, length us, event | category | flops | bytes accessed | tf_op | source)
XLA Modules:
  0.0 188.2 jit_solution(7053741721594099761)
XLA Ops:
  2.4 20.6 %all_to_all.25 = bf16[4,32,1856]{2,1,0:T(8,128)(2,1)S(1)} all-to-all(bf16[4,32,1856]{2,1,0:T(8,128)(2,1)S(1)} %broadcast_in_dim.24), channel_id=1, replica_groups=mesh['x'=4,'core'=2,'row'=4,'far'=2,'near'=8] {'row'}, dimensions={0} | all-to-all | bytes 950272 | tf_op jit(solution)/shard_map/all_to_all | solution.py:156
  23.9 3.6 %all-to-all-start = ((bf16[4,32,1856]{2,1,0:T(8,128)(2,1)}), bf16[4,32,1856]{2,1,0:T(8,128)(2,1)S(1)}, u32[]{:S(2)}, u32[]{:S(2)}) async-start(bf16[4,32,1856]{2,1,0:T(8,128)(2,1)} %broadcast_in_dim.23), calls=%async_computation | async-start | bytes 983040 | tf_op jit(solution)/shard_map/all_to_all | solution.py:156
  27.8 7.9 %collective-permute-start.16 = (bf16[464,64]{0,1:T(8,128)(2,1)S(1)}, bf16[464,64]{0,1:T(8,128)(2,1)S(1)}, u32[]{:S(2)}, u32[]{:S(2)}) collective-permute-start(bf16[464,64]{0,1:T(8,128)(2,1)S(1)} %reshape.31), channel_id=1, source_target_pairs={{0,8},{8,0},{1,9},{9,1},{2,10},{10,2},{3,11},{11,3},{4,12},{12,4},... | collective-permute-start | bytes 178184 | tf_op jit(solution)/shard_map/ppermute | solution.py:145
  36.4 3.1 %collective-permute-start.8 = (bf16[64,1856]{1,0:T(8,128)(2,1)S(1)}, bf16[64,1856]{1,0:T(8,128)(2,1)S(1)}, u32[]{:S(2)}, u32[]{:S(2)}) collective-permute-start(bf16[64,1856]{1,0:T(8,128)(2,1)S(1)} %bitcast.46), channel_id=1, source_target_pairs={{0,128},{128,0},{256,384},{384,256},{1,129},{129,1},{257,385},{385... | collective-permute-start | bytes 712712 | tf_op jit(solution)/shard_map/ppermute | solution.py:158
  39.6 2.4 %collective-permute-done.16 = bf16[464,64]{0,1:T(8,128)(2,1)S(1)} collective-permute-done((bf16[464,64]{0,1:T(8,128)(2,1)S(1)}, bf16[464,64]{0,1:T(8,128)(2,1)S(1)}, u32[]{:S(2)}, u32[]{:S(2)}) %collective-permute-start.16) | collective-permute-done | bytes 59424 | tf_op jit(solution)/shard_map/ppermute | solution.py:145
  43.3 6.8 %all-to-all-start.4 = ((bf16[8,464,128]{2,1,0:T(8,128)(2,1)}), bf16[8,464,128]{2,1,0:T(8,128)(2,1)S(1)}, u32[]{:S(2)}, u32[]{:S(2)}) async-start(bf16[8,464,128]{2,1,0:T(8,128)(2,1)} %broadcast_in_dim.25), calls=%async_computation.4 | async-start | bytes 1900544 | tf_op jit(solution)/shard_map/all_to_all | solution.py:147
  50.1 4.4 %collective-permute-start.9 = (bf16[64,1856]{1,0:T(8,128)(2,1)}, bf16[64,1856]{1,0:T(8,128)(2,1)S(1)}, u32[]{:S(2)}, u32[]{:S(2)}) collective-permute-start(bf16[64,1856]{1,0:T(8,128)(2,1)} %bitcast.36), channel_id=1, source_target_pairs={{0,384},{128,256},{256,128},{384,0},{1,385},{129,257},{257,129},{3... | collective-permute-start | bytes 712712 | tf_op jit(solution)/shard_map/ppermute | solution.py:159
  54.5 2.1 %collective-permute-start.10 = (bf16[128,1856]{1,0:T(8,128)(2,1)S(1)}, bf16[128,1856]{1,0:T(8,128)(2,1)S(1)}, u32[]{:S(2)}, u32[]{:S(2)}) collective-permute-start(bf16[128,1856]{1,0:T(8,128)(2,1)S(1)} %pad_maximum_fusion.2.refs_0_), channel_id=1, source_target_pairs={{0,384},{128,256},{256,128},{384,0},{1,385},{129,257},{257,129},{3... | collective-permute-start | bytes 1425416 | tf_op jit(solution)/shard_map/ppermute | solution.py:160
  59.4 2.2 %collective-permute-start.11 = (bf16[128,1856]{1,0:T(8,128)(2,1)S(1)}, bf16[128,1856]{1,0:T(8,128)(2,1)}, u32[]{:S(2)}, u32[]{:S(2)}) collective-permute-start(bf16[128,1856]{1,0:T(8,128)(2,1)S(1)} %pad_maximum_fusion.3.refs_1_), channel_id=1, source_target_pairs={{0,128},{128,0},{256,384},{384,256},{1,129},{129,1},{257,385},{385... | collective-permute-start | bytes 1425416 | tf_op jit(solution)/shard_map/ppermute | solution.py:160
  61.6 9.3 %collective-permute-start.12 = (bf16[128,1856]{1,0:T(8,128)(2,1)S(1)}, bf16[128,1856]{1,0:T(8,128)(2,1)}, u32[]{:S(2)}, u32[]{:S(2)}) collective-permute-start(bf16[128,1856]{1,0:T(8,128)(2,1)S(1)} %pad_maximum_fusion.2.refs_0_), channel_id=1, source_target_pairs={{0,64},{64,0},{1,65},{65,1},{2,66},{66,2},{3,67},{67,3},{4,68},{68... | collective-permute-start | bytes 1425416 | tf_op jit(solution)/shard_map/ppermute | solution.py:161
  71.0 1.9 %collective-permute-start.13 = (bf16[128,1856]{1,0:T(8,128)(2,1)S(1)}, bf16[128,1856]{1,0:T(8,128)(2,1)}, u32[]{:S(2)}, u32[]{:S(2)}) collective-permute-start(bf16[128,1856]{1,0:T(8,128)(2,1)S(1)} %pad_maximum_fusion.3.refs_1_), channel_id=1, source_target_pairs={{0,64},{64,0},{1,65},{65,1},{2,66},{66,2},{3,67},{67,3},{4,68},{68... | collective-permute-start | bytes 1425416 | tf_op jit(solution)/shard_map/ppermute | solution.py:161
  72.9 2.7 %collective-permute-start.14 = (bf16[128,1856]{1,0:T(8,128)(2,1)S(1)}, bf16[128,1856]{1,0:T(8,128)(2,1)}, u32[]{:S(2)}, u32[]{:S(2)}) collective-permute-start(bf16[128,1856]{1,0:T(8,128)(2,1)S(1)} %collective-permute-done.10.refs_2_), channel_id=1, source_target_pairs={{0,64},{64,0},{1,65},{65,1},{2,66},{66,2},{3,67},{67,3},{4,68},{68... | collective-permute-start | bytes 1425416 | tf_op jit(solution)/shard_map/ppermute | solution.py:161
  75.7 3.7 %collective-permute-start.15 = (bf16[128,1856]{1,0:T(8,128)(2,1)}, bf16[128,1856]{1,0:T(8,128)(2,1)}, u32[]{:S(2)}, u32[]{:S(2)}) collective-permute-start(bf16[128,1856]{1,0:T(8,128)(2,1)} %collective-permute-done.11.refs_3_), channel_id=1, source_target_pairs={{0,64},{64,0},{1,65},{65,1},{2,66},{66,2},{3,67},{67,3},{4,68},{68... | collective-permute-start | bytes 1425416 | tf_op jit(solution)/shard_map/ppermute | solution.py:161
  81.2 6.2 %shard_map.60 = (bf16[1024,1856]{1,0:T(8,128)(2,1)S(1)}, f32[16,120,128]{2,1,0:T(8,128)S(1)}) custom-call(s32[32]{0:T(128)S(1)} %stack.164.where_ref, bf16[128,1856]{1,0:T(8,128)(2,1)S(1)} %pad_maximum_fusion.2.refs_0_, bf16[128,1856]{1,0:T(8,128)(2,1)S(1)} %pad_maximum_fusion.3.refs_1_, bf16[128,1856]{1,0:T(8,128)(2,1)S(1)} %collective-permute-done.10.refs_2_, ...), custom_call_target="tpu_custom_call" | custom-call | flops 881852416 | bytes 7602176 | tf_op jit(solution)/shard_map/pallas_call | solution.py:52
  87.5 1.9 copy-done
  90.3 11.8 %all-to-all-start.3 = ((f32[16,120,128]{2,1,0:T(8,128)}), f32[16,120,128]{2,1,0:T(8,128)S(1)}, u32[]{:S(2)}, u32[]{:S(2)}) async-start(f32[16,120,128]{2,1,0:T(8,128)} %copy-done.5), calls=%async_computation.3 | async-start | bytes 1966080 | tf_op jit(solution)/shard_map/all_to_all | solution.py:168
  103.2 5.1 %collective-permute-start.1 = (bf16[64,1856]{1,0:T(8,128)(2,1)S(1)}, bf16[64,1856]{1,0:T(8,128)(2,1)S(1)}, u32[]{:S(2)}, u32[]{:S(2)}) collective-permute-start(bf16[64,1856]{1,0:T(8,128)(2,1)S(1)} %bitcast.50), channel_id=1, source_target_pairs={{0,384},{128,256},{256,128},{384,0},{1,385},{129,257},{257,129},{3... | collective-permute-start | bytes 712712 | tf_op jit(solution)/shard_map/ppermute | solution.py:159
  108.3 1.9 %collective-permute-start = (bf16[64,1856]{1,0:T(8,128)(2,1)S(1)}, bf16[64,1856]{1,0:T(8,128)(2,1)S(1)}, u32[]{:S(2)}, u32[]{:S(2)}) collective-permute-start(bf16[64,1856]{1,0:T(8,128)(2,1)S(1)} %bitcast.48), channel_id=1, source_target_pairs={{0,128},{128,0},{256,384},{384,256},{1,129},{129,1},{257,385},{385... | collective-permute-start | bytes 712712 | tf_op jit(solution)/shard_map/ppermute | solution.py:158
  110.2 3.8 %collective-permute-done.1 = bf16[64,1856]{1,0:T(8,128)(2,1)S(1)} collective-permute-done((bf16[64,1856]{1,0:T(8,128)(2,1)S(1)}, bf16[64,1856]{1,0:T(8,128)(2,1)S(1)}, u32[]{:S(2)}, u32[]{:S(2)}) %collective-permute-start.1) | collective-permute-done | bytes 237600 | tf_op jit(solution)/shard_map/ppermute | solution.py:159
  114.0 1.9 %collective-permute-start.3 = (bf16[128,1856]{1,0:T(8,128)(2,1)S(1)}, bf16[128,1856]{1,0:T(8,128)(2,1)S(1)}, u32[]{:S(2)}, u32[]{:S(2)}) collective-permute-start(bf16[128,1856]{1,0:T(8,128)(2,1)S(1)} %pad_maximum_fusion.1.refs_1_), channel_id=1, source_target_pairs={{0,128},{128,0},{256,384},{384,256},{1,129},{129,1},{257,385},{385... | collective-permute-start | bytes 1425416 | tf_op jit(solution)/shard_map/ppermute | solution.py:160
  116.7 3.5 %collective-permute-start.2 = (bf16[128,1856]{1,0:T(8,128)(2,1)S(1)}, bf16[128,1856]{1,0:T(8,128)(2,1)S(1)}, u32[]{:S(2)}, u32[]{:S(2)}) collective-permute-start(bf16[128,1856]{1,0:T(8,128)(2,1)S(1)} %pad_maximum_fusion.refs_0_), channel_id=1, source_target_pairs={{0,384},{128,256},{256,128},{384,0},{1,385},{129,257},{257,129},{3... | collective-permute-start | bytes 1425416 | tf_op jit(solution)/shard_map/ppermute | solution.py:160
  120.2 3.7 %collective-permute-start.5 = (bf16[128,1856]{1,0:T(8,128)(2,1)S(1)}, bf16[128,1856]{1,0:T(8,128)(2,1)S(1)}, u32[]{:S(2)}, u32[]{:S(2)}) collective-permute-start(bf16[128,1856]{1,0:T(8,128)(2,1)S(1)} %pad_maximum_fusion.1.refs_1_), channel_id=1, source_target_pairs={{0,64},{64,0},{1,65},{65,1},{2,66},{66,2},{3,67},{67,3},{4,68},{68... | collective-permute-start | bytes 1425416 | tf_op jit(solution)/shard_map/ppermute | solution.py:161
  124.0 1.9 %collective-permute-start.4 = (bf16[128,1856]{1,0:T(8,128)(2,1)S(1)}, bf16[128,1856]{1,0:T(8,128)(2,1)S(1)}, u32[]{:S(2)}, u32[]{:S(2)}) collective-permute-start(bf16[128,1856]{1,0:T(8,128)(2,1)S(1)} %pad_maximum_fusion.refs_0_), channel_id=1, source_target_pairs={{0,64},{64,0},{1,65},{65,1},{2,66},{66,2},{3,67},{67,3},{4,68},{68... | collective-permute-start | bytes 1425416 | tf_op jit(solution)/shard_map/ppermute | solution.py:161
  127.4 4.0 %collective-permute-start.7 = (bf16[128,1856]{1,0:T(8,128)(2,1)S(1)}, bf16[128,1856]{1,0:T(8,128)(2,1)S(1)}, u32[]{:S(2)}, u32[]{:S(2)}) collective-permute-start(bf16[128,1856]{1,0:T(8,128)(2,1)S(1)} %collective-permute-done.3.refs_3_), channel_id=1, source_target_pairs={{0,64},{64,0},{1,65},{65,1},{2,66},{66,2},{3,67},{67,3},{4,68},{68... | collective-permute-start | bytes 1425416 | tf_op jit(solution)/shard_map/ppermute | solution.py:161
  131.4 3.9 %collective-permute-start.6 = (bf16[128,1856]{1,0:T(8,128)(2,1)S(1)}, bf16[128,1856]{1,0:T(8,128)(2,1)S(1)}, u32[]{:S(2)}, u32[]{:S(2)}) collective-permute-start(bf16[128,1856]{1,0:T(8,128)(2,1)S(1)} %collective-permute-done.2.refs_2_), channel_id=1, source_target_pairs={{0,64},{64,0},{1,65},{65,1},{2,66},{66,2},{3,67},{67,3},{4,68},{68... | collective-permute-start | bytes 1425416 | tf_op jit(solution)/shard_map/ppermute | solution.py:161
  136.8 8.4 %shard_map.59 = (bf16[1024,1856]{1,0:T(8,128)(2,1)S(1)}, f32[16,120,128]{2,1,0:T(8,128)S(1)}) custom-call(s32[32]{0:T(128)S(1)} %stack.164.where_ref, bf16[128,1856]{1,0:T(8,128)(2,1)S(1)} %pad_maximum_fusion.refs_0_, bf16[128,1856]{1,0:T(8,128)(2,1)S(1)} %pad_maximum_fusion.1.refs_1_, bf16[128,1856]{1,0:T(8,128)(2,1)S(1)} %collective-permute-done.2.refs_2_, ...), custom_call_target="tpu_custom_call" | custom-call | flops 881852416 | bytes 7602176 | tf_op jit(solution)/shard_map/pallas_call | solution.py:52
  145.2 1.9 %copy-done.2 = bf16[1024,1856]{1,0:T(8,128)(2,1)} copy-done((bf16[1024,1856]{1,0:T(8,128)(2,1)}, bf16[1024,1856]{1,0:T(8,128)(2,1)S(1)}, u32[]{:S(2)}) %copy-start.2) | copy-done | bytes 3801112
  148.2 11.2 %all-to-all-start.1 = ((f32[16,120,128]{2,1,0:T(8,128)}), f32[16,120,128]{2,1,0:T(8,128)S(1)}, u32[]{:S(2)}, u32[]{:S(2)}) async-start(f32[16,120,128]{2,1,0:T(8,128)} %copy-done.6), calls=%async_computation.1 | async-start | bytes 1966080 | tf_op jit(solution)/shard_map/all_to_all | solution.py:168
  159.3 2.1 %copy-done.1 = bf16[1024,1856]{1,0:T(8,128)(2,1)S(1)} copy-done((bf16[1024,1856]{1,0:T(8,128)(2,1)S(1)}, bf16[1024,1856]{1,0:T(8,128)(2,1)}, u32[]{:S(2)}) %copy-start.1) | copy-done | bytes 3801112
  161.5 2.1 %copy-done.3 = bf16[1024,1856]{1,0:T(8,128)(2,1)S(1)} copy-done((bf16[1024,1856]{1,0:T(8,128)(2,1)S(1)}, bf16[1024,1856]{1,0:T(8,128)(2,1)}, u32[]{:S(2)}) %copy-start.3) | copy-done | bytes 3801112
  163.6 3.1 %shard_map.62 = bf16[232,1856]{1,0:T(8,128)(2,1)} custom-call(bf16[8,464,128]{2,1,0:T(8,128)(2,1)S(1)} %all-to-all-done.4.inputs, bf16[1024,1856]{1,0:T(8,128)(2,1)S(1)} %copy-done.3, bf16[1024,1856]{1,0:T(8,128)(2,1)S(1)} %copy-done.1), custom_call_target="tpu_custom_call" | custom-call | flops 1763704832 | bytes 7602176 | tf_op jit(solution)/shard_map/pallas_call | solution.py:91
  166.7 20.6 %all-to-all-done.1.first_ref = f32[16,120,128]{2,1,0:T(8,128)S(1)} async-done(((f32[16,120,128]{2,1,0:T(8,128)}), f32[16,120,128]{2,1,0:T(8,128)S(1)}, u32[]{:S(2)}, u32[]{:S(2)}) %all-to-all-start.1) | async-done | bytes 983072 | tf_op jit(solution)/shard_map/all_to_all | solution.py:168
  (51 shorter events, 16.4 us)
Async XLA Ops:
  0.6 26.9 %copy-start.8 = (bf16[128,232]{0,1:T(8,128)(2,1)S(1)}, bf16[128,232]{0,1:T(8,128)(2,1)}, u32[]{:S(2)}) copy-start(bf16[128,232]{0,1:T(8,128)(2,1)} %param.4) | copy-start | bytes 178180
  23.9 57.4 %copy-start.4 = (bf16[232,1856]{1,0:T(8,128)(2,1)S(1)}, bf16[232,1856]{1,0:T(8,128)(2,1)}, u32[]{:S(2)}) copy-start(bf16[232,1856]{1,0:T(8,128)(2,1)} %refs_8_.3) | copy-start | bytes 2583556
  23.9 18.3 %all-to-all-start = ((bf16[4,32,1856]{2,1,0:T(8,128)(2,1)}), bf16[4,32,1856]{2,1,0:T(8,128)(2,1)S(1)}, u32[]{:S(2)}, u32[]{:S(2)}) async-start(bf16[4,32,1856]{2,1,0:T(8,128)(2,1)} %broadcast_in_dim.23), calls=%async_computation | async-start | bytes 983040 | tf_op jit(solution)/shard_map/all_to_all | solution.py:156
  27.8 14.2 %collective-permute-start.16 = (bf16[464,64]{0,1:T(8,128)(2,1)S(1)}, bf16[464,64]{0,1:T(8,128)(2,1)S(1)}, u32[]{:S(2)}, u32[]{:S(2)}) collective-permute-start(bf16[464,64]{0,1:T(8,128)(2,1)S(1)} %reshape.31), channel_id=1, source_target_pairs={{0,8},{8,0},{1,9},{9,1},{2,10},{10,2},{3,11},{11,3},{4,12},{12,4},... | collective-permute-start | bytes 178184 | tf_op jit(solution)/shard_map/ppermute | solution.py:145
  36.4 18.0 %collective-permute-start.8 = (bf16[64,1856]{1,0:T(8,128)(2,1)S(1)}, bf16[64,1856]{1,0:T(8,128)(2,1)S(1)}, u32[]{:S(2)}, u32[]{:S(2)}) collective-permute-start(bf16[64,1856]{1,0:T(8,128)(2,1)S(1)} %bitcast.46), channel_id=1, source_target_pairs={{0,128},{128,0},{256,384},{384,256},{1,129},{129,1},{257,385},{385... | collective-permute-start | bytes 712712 | tf_op jit(solution)/shard_map/ppermute | solution.py:158
  42.2 12.3 %copy-start.7 = (bf16[4,32,1856]{2,1,0:T(8,128)(2,1)}, bf16[4,32,1856]{2,1,0:T(8,128)(2,1)S(1)}, u32[]{:S(2)}) copy-start(bf16[4,32,1856]{2,1,0:T(8,128)(2,1)S(1)} %all-to-all-done) | copy-start | bytes 1425412
  43.3 47.0 %all-to-all-start.4 = ((bf16[8,464,128]{2,1,0:T(8,128)(2,1)}), bf16[8,464,128]{2,1,0:T(8,128)(2,1)S(1)}, u32[]{:S(2)}, u32[]{:S(2)}) async-start(bf16[8,464,128]{2,1,0:T(8,128)(2,1)} %broadcast_in_dim.25), calls=%async_computation.4 | async-start | bytes 1900544 | tf_op jit(solution)/shard_map/all_to_all | solution.py:147
  50.1 8.3 %collective-permute-start.9 = (bf16[64,1856]{1,0:T(8,128)(2,1)}, bf16[64,1856]{1,0:T(8,128)(2,1)S(1)}, u32[]{:S(2)}, u32[]{:S(2)}) collective-permute-start(bf16[64,1856]{1,0:T(8,128)(2,1)} %bitcast.36), channel_id=1, source_target_pairs={{0,384},{128,256},{256,128},{384,0},{1,385},{129,257},{257,129},{3... | collective-permute-start | bytes 712712 | tf_op jit(solution)/shard_map/ppermute | solution.py:159
  54.5 18.4 %collective-permute-start.10 = (bf16[128,1856]{1,0:T(8,128)(2,1)S(1)}, bf16[128,1856]{1,0:T(8,128)(2,1)S(1)}, u32[]{:S(2)}, u32[]{:S(2)}) collective-permute-start(bf16[128,1856]{1,0:T(8,128)(2,1)S(1)} %pad_maximum_fusion.2.refs_0_), channel_id=1, source_target_pairs={{0,384},{128,256},{256,128},{384,0},{1,385},{129,257},{257,129},{3... | collective-permute-start | bytes 1425416 | tf_op jit(solution)/shard_map/ppermute | solution.py:160
  59.4 16.2 %collective-permute-start.11 = (bf16[128,1856]{1,0:T(8,128)(2,1)S(1)}, bf16[128,1856]{1,0:T(8,128)(2,1)}, u32[]{:S(2)}, u32[]{:S(2)}) collective-permute-start(bf16[128,1856]{1,0:T(8,128)(2,1)S(1)} %pad_maximum_fusion.3.refs_1_), channel_id=1, source_target_pairs={{0,128},{128,0},{256,384},{384,256},{1,129},{129,1},{257,385},{385... | collective-permute-start | bytes 1425416 | tf_op jit(solution)/shard_map/ppermute | solution.py:160
  61.6 18.0 %collective-permute-start.12 = (bf16[128,1856]{1,0:T(8,128)(2,1)S(1)}, bf16[128,1856]{1,0:T(8,128)(2,1)}, u32[]{:S(2)}, u32[]{:S(2)}) collective-permute-start(bf16[128,1856]{1,0:T(8,128)(2,1)S(1)} %pad_maximum_fusion.2.refs_0_), channel_id=1, source_target_pairs={{0,64},{64,0},{1,65},{65,1},{2,66},{66,2},{3,67},{67,3},{4,68},{68... | collective-permute-start | bytes 1425416 | tf_op jit(solution)/shard_map/ppermute | solution.py:161
  71.0 8.7 %collective-permute-start.13 = (bf16[128,1856]{1,0:T(8,128)(2,1)S(1)}, bf16[128,1856]{1,0:T(8,128)(2,1)}, u32[]{:S(2)}, u32[]{:S(2)}) collective-permute-start(bf16[128,1856]{1,0:T(8,128)(2,1)S(1)} %pad_maximum_fusion.3.refs_1_), channel_id=1, source_target_pairs={{0,64},{64,0},{1,65},{65,1},{2,66},{66,2},{3,67},{67,3},{4,68},{68... | collective-permute-start | bytes 1425416 | tf_op jit(solution)/shard_map/ppermute | solution.py:161
  72.9 6.8 %collective-permute-start.14 = (bf16[128,1856]{1,0:T(8,128)(2,1)S(1)}, bf16[128,1856]{1,0:T(8,128)(2,1)}, u32[]{:S(2)}, u32[]{:S(2)}) collective-permute-start(bf16[128,1856]{1,0:T(8,128)(2,1)S(1)} %collective-permute-done.10.refs_2_), channel_id=1, source_target_pairs={{0,64},{64,0},{1,65},{65,1},{2,66},{66,2},{3,67},{67,3},{4,68},{68... | collective-permute-start | bytes 1425416 | tf_op jit(solution)/shard_map/ppermute | solution.py:161
  75.7 5.6 %collective-permute-start.15 = (bf16[128,1856]{1,0:T(8,128)(2,1)}, bf16[128,1856]{1,0:T(8,128)(2,1)}, u32[]{:S(2)}, u32[]{:S(2)}) collective-permute-start(bf16[128,1856]{1,0:T(8,128)(2,1)} %collective-permute-done.11.refs_3_), channel_id=1, source_target_pairs={{0,64},{64,0},{1,65},{65,1},{2,66},{66,2},{3,67},{67,3},{4,68},{68... | collective-permute-start | bytes 1425416 | tf_op jit(solution)/shard_map/ppermute | solution.py:161
  87.5 1.9 copy-start
  89.3 1.0 copy-start.5
  90.3 57.9 %all-to-all-start.3 = ((f32[16,120,128]{2,1,0:T(8,128)}), f32[16,120,128]{2,1,0:T(8,128)S(1)}, u32[]{:S(2)}, u32[]{:S(2)}) async-start(f32[16,120,128]{2,1,0:T(8,128)} %copy-done.5), calls=%async_computation.3 | async-start | bytes 1966080 | tf_op jit(solution)/shard_map/all_to_all | solution.py:168
  103.2 10.8 %collective-permute-start.1 = (bf16[64,1856]{1,0:T(8,128)(2,1)S(1)}, bf16[64,1856]{1,0:T(8,128)(2,1)S(1)}, u32[]{:S(2)}, u32[]{:S(2)}) collective-permute-start(bf16[64,1856]{1,0:T(8,128)(2,1)S(1)} %bitcast.50), channel_id=1, source_target_pairs={{0,384},{128,256},{256,128},{384,0},{1,385},{129,257},{257,129},{3... | collective-permute-start | bytes 712712 | tf_op jit(solution)/shard_map/ppermute | solution.py:159
  108.3 8.4 %collective-permute-start = (bf16[64,1856]{1,0:T(8,128)(2,1)S(1)}, bf16[64,1856]{1,0:T(8,128)(2,1)S(1)}, u32[]{:S(2)}, u32[]{:S(2)}) collective-permute-start(bf16[64,1856]{1,0:T(8,128)(2,1)S(1)} %bitcast.48), channel_id=1, source_target_pairs={{0,128},{128,0},{256,384},{384,256},{1,129},{129,1},{257,385},{385... | collective-permute-start | bytes 712712 | tf_op jit(solution)/shard_map/ppermute | solution.py:158
  114.0 13.4 %collective-permute-start.3 = (bf16[128,1856]{1,0:T(8,128)(2,1)S(1)}, bf16[128,1856]{1,0:T(8,128)(2,1)S(1)}, u32[]{:S(2)}, u32[]{:S(2)}) collective-permute-start(bf16[128,1856]{1,0:T(8,128)(2,1)S(1)} %pad_maximum_fusion.1.refs_1_), channel_id=1, source_target_pairs={{0,128},{128,0},{256,384},{384,256},{1,129},{129,1},{257,385},{385... | collective-permute-start | bytes 1425416 | tf_op jit(solution)/shard_map/ppermute | solution.py:160
  116.7 14.7 %collective-permute-start.2 = (bf16[128,1856]{1,0:T(8,128)(2,1)S(1)}, bf16[128,1856]{1,0:T(8,128)(2,1)S(1)}, u32[]{:S(2)}, u32[]{:S(2)}) collective-permute-start(bf16[128,1856]{1,0:T(8,128)(2,1)S(1)} %pad_maximum_fusion.refs_0_), channel_id=1, source_target_pairs={{0,384},{128,256},{256,128},{384,0},{1,385},{129,257},{257,129},{3... | collective-permute-start | bytes 1425416 | tf_op jit(solution)/shard_map/ppermute | solution.py:160
  120.2 15.1 %collective-permute-start.5 = (bf16[128,1856]{1,0:T(8,128)(2,1)S(1)}, bf16[128,1856]{1,0:T(8,128)(2,1)S(1)}, u32[]{:S(2)}, u32[]{:S(2)}) collective-permute-start(bf16[128,1856]{1,0:T(8,128)(2,1)S(1)} %pad_maximum_fusion.1.refs_1_), channel_id=1, source_target_pairs={{0,64},{64,0},{1,65},{65,1},{2,66},{66,2},{3,67},{67,3},{4,68},{68... | collective-permute-start | bytes 1425416 | tf_op jit(solution)/shard_map/ppermute | solution.py:161
  124.0 11.4 %collective-permute-start.4 = (bf16[128,1856]{1,0:T(8,128)(2,1)S(1)}, bf16[128,1856]{1,0:T(8,128)(2,1)S(1)}, u32[]{:S(2)}, u32[]{:S(2)}) collective-permute-start(bf16[128,1856]{1,0:T(8,128)(2,1)S(1)} %pad_maximum_fusion.refs_0_), channel_id=1, source_target_pairs={{0,64},{64,0},{1,65},{65,1},{2,66},{66,2},{3,67},{67,3},{4,68},{68... | collective-permute-start | bytes 1425416 | tf_op jit(solution)/shard_map/ppermute | solution.py:161
  127.4 8.0 %collective-permute-start.7 = (bf16[128,1856]{1,0:T(8,128)(2,1)S(1)}, bf16[128,1856]{1,0:T(8,128)(2,1)S(1)}, u32[]{:S(2)}, u32[]{:S(2)}) collective-permute-start(bf16[128,1856]{1,0:T(8,128)(2,1)S(1)} %collective-permute-done.3.refs_3_), channel_id=1, source_target_pairs={{0,64},{64,0},{1,65},{65,1},{2,66},{66,2},{3,67},{67,3},{4,68},{68... | collective-permute-start | bytes 1425416 | tf_op jit(solution)/shard_map/ppermute | solution.py:161
  131.4 5.4 %collective-permute-start.6 = (bf16[128,1856]{1,0:T(8,128)(2,1)S(1)}, bf16[128,1856]{1,0:T(8,128)(2,1)S(1)}, u32[]{:S(2)}, u32[]{:S(2)}) collective-permute-start(bf16[128,1856]{1,0:T(8,128)(2,1)S(1)} %collective-permute-done.2.refs_2_), channel_id=1, source_target_pairs={{0,64},{64,0},{1,65},{65,1},{2,66},{66,2},{3,67},{67,3},{4,68},{68... | collective-permute-start | bytes 1425416 | tf_op jit(solution)/shard_map/ppermute | solution.py:161
  145.2 1.9 %copy-start.2 = (bf16[1024,1856]{1,0:T(8,128)(2,1)}, bf16[1024,1856]{1,0:T(8,128)(2,1)S(1)}, u32[]{:S(2)}) copy-start(bf16[1024,1856]{1,0:T(8,128)(2,1)S(1)} %get-tuple-element.8.refs_0_) | copy-start | bytes 11403268
  147.1 1.0 copy-start.6
  148.2 39.2 %all-to-all-start.1 = ((f32[16,120,128]{2,1,0:T(8,128)}), f32[16,120,128]{2,1,0:T(8,128)S(1)}, u32[]{:S(2)}, u32[]{:S(2)}) async-start(f32[16,120,128]{2,1,0:T(8,128)} %copy-done.6), calls=%async_computation.1 | async-start | bytes 1966080 | tf_op jit(solution)/shard_map/all_to_all | solution.py:168
  159.3 2.1 %copy-start.1 = (bf16[1024,1856]{1,0:T(8,128)(2,1)S(1)}, bf16[1024,1856]{1,0:T(8,128)(2,1)}, u32[]{:S(2)}) copy-start(bf16[1024,1856]{1,0:T(8,128)(2,1)} %copy-done) | copy-start | bytes 11403268
  161.5 2.1 %copy-start.3 = (bf16[1024,1856]{1,0:T(8,128)(2,1)S(1)}, bf16[1024,1856]{1,0:T(8,128)(2,1)}, u32[]{:S(2)}) copy-start(bf16[1024,1856]{1,0:T(8,128)(2,1)} %copy-done.2) | copy-start | bytes 11403268

commit v3 on v0

v3 whole, which is shorter than its diff:
```python
import functools

import jax
import jax.numpy as jnp
from jax import lax
from jax.experimental import pallas as pl
from jax.experimental.pallas import tpu as pltpu
from jax.sharding import Mesh
from jax.sharding import PartitionSpec as P

CHUNKS = 2
X, CORES, ROWS, FAR, NEAR = 4, 2, 4, 2, 8
BINS = X * CORES * ROWS
OWNERS = FAR * NEAR
VMEM = pl.BlockSpec(memory_space=pltpu.VMEM)
ANY = pl.BlockSpec(memory_space=pl.ANY)
TINY = 2.0 ** -100
SHIFT = 7.5
PARAMS = pltpu.CompilerParams(vmem_limit_bytes=60 << 20)
SMALL = pltpu.CompilerParams(vmem_limit_bytes=16 << 20)


def flips(size, flip):
    return [(i, i ^ flip) for i in range(size)]


def partial_kernel(live, chunk, counts, where_ref, *refs):
    pieces = refs[:len(counts)]
    own_ref, other_ref, tokens_out, sums_out, tokens, sums, in_sems, out_sems = refs[-8:]
    copies = []
    for piece, (first, blocks) in zip(pieces, counts):
        for j in range(blocks):
            n = len(copies)
            copies.append(pltpu.make_async_copy(
                piece.at[pl.ds(first + j * live, live)], tokens.at[where_ref[n]], in_sems.at[n]))
    for copy in copies:
        copy.start()
    for copy in copies:
        copy.wait()
    save = pltpu.make_async_copy(tokens, tokens_out, out_sems.at[0])
    save.start()
    features = own_ref.shape[0]
    rows, lanes = BINS * live, sums.shape[-1]
    lane = lax.broadcasted_iota(jnp.int32, (rows, lanes), 1)
    for i, ref in enumerate((own_ref, other_ref)):
        result = lax.dot_general(
            tokens[...].reshape(rows, ref.shape[1]), ref[...],
            (((1,), (1,)), ((), ())), preferred_element_type=jnp.float32)
        top = jnp.max(jnp.abs(result), axis=1, keepdims=True)
        power = jnp.ceil(jnp.log2(jnp.maximum(top, TINY)))
        raised = result * jnp.exp2(SHIFT - power)
        for _ in range(4):
            raised = raised * raised
        result = jnp.where(result < 0, -raised, raised)
        result = jnp.concatenate([result, jnp.zeros((rows, lanes - features), jnp.float32)], 1)
        coded = jnp.where(lane < features, result, power).astype(sums.dtype)
        sums[:, i] = coded.reshape(OWNERS, 2 * live, lanes)
    send = pltpu.make_async_copy(sums, sums_out.at[:, chunk], out_sems.at[1])
    send.start()
    save.wait()
    send.wait()


def partials(pieces, counts, where, own, other, live, chunk, after, earlier):
    features, hidden = own.shape
    rows = BINS * live
    lanes = features // 128 * 128 + 128
    coded = jax.ShapeDtypeStruct((OWNERS, CHUNKS, 2, 2 * live, lanes), jnp.bfloat16)
    tokens = jax.ShapeDtypeStruct((BINS, live, hidden), jnp.bfloat16)
    after = after + ([] if earlier is None else [earlier])
    return pl.pallas_call(
        functools.partial(partial_kernel, live, chunk, counts),
        out_shape=[tokens, coded],
        in_specs=[pl.BlockSpec(memory_space=pltpu.SMEM)] + [ANY] * (len(pieces) + len(after)) + [VMEM] * 2,
        out_specs=[ANY] * 2,
        input_output_aliases={} if earlier is None else {len(pieces) + len(after): 1},
        scratch_shapes=[
            pltpu.VMEM(tokens.shape, tokens.dtype),
            pltpu.VMEM((OWNERS, 2, 2 * live, lanes), coded.dtype),
            pltpu.SemaphoreType.DMA((BINS,)), pltpu.SemaphoreType.DMA((2,))],
        compiler_params=PARAMS,
        cost_estimate=pl.CostEstimate(
            flops=4 * rows * hidden * features, bytes_accessed=4 * rows * hidden, transcendentals=0),
    )(where, *pieces, *after, own, other)


def weight_grad_kernel(core_ref, inputs, more, *refs):
    parts, (out, held, tokens, sems) = refs[:-4], refs[-4:]
    core = core_ref[0]
    chunks = len(parts) // 2
    copies = []
    for n, part in enumerate(parts):
        half = core if n < chunks else 1 - core
        copies.append(pltpu.make_async_copy(part, tokens.at[:, half * chunks + n % chunks], sems.at[n]))
    for copy in copies:
        copy.start()
    features, hidden = out.shape
    width = inputs.shape[2]
    owner = core_ref[1]
    for i in range(OWNERS):
        flip = (i & 1) * NEAR + (i >> 1 & 1) * 4 + (i >> 2 & 1) * 2 + (i >> 3)
        first = pl.multiple_of((owner ^ flip) * width, width)
        held[:, pl.ds(first, width)] = inputs[i] if i < NEAR else more[i - NEAR]
    for copy in copies:
        copy.wait()
    for first in range(0, hidden, 256):
        last = min(first + 256, hidden)
        rows = tokens[:, :, :, first:last].reshape(held.shape[1], last - first)
        out[:, first:last] = lax.dot_general(
            held[...], rows, (((1,), (0,)), ((), ())), preferred_element_type=jnp.float32).astype(out.dtype)


def weight_grad(core, inputs, parts, live, features):
    hidden = parts[0].shape[2]
    width = inputs[0].shape[2]
    rows = BINS * live * len(parts)
    return pl.pallas_call(
        weight_grad_kernel,
        out_shape=jax.ShapeDtypeStruct((features, hidden), jnp.bfloat16),
        in_specs=[pl.BlockSpec(memory_space=pltpu.SMEM), VMEM, VMEM] + [ANY] * len(parts),
        out_specs=VMEM,
        scratch_shapes=[
            pltpu.VMEM((features, OWNERS * width), jnp.bfloat16),
            pltpu.VMEM((BINS, len(parts), live, hidden), jnp.bfloat16),
            pltpu.SemaphoreType.DMA((len(parts),))],
        compiler_params=PARAMS,
        cost_estimate=pl.CostEstimate(
            flops=2 * rows * hidden * features, bytes_accessed=2 * rows * hidden, transcendentals=0),
    )(core, *inputs, *parts)


def add_kernel(received, after, keep, send):
    del after
    features = keep.shape[1]
    live = received.shape[3] // 2
    for k in range(CHUNKS):
        for i, out in enumerate((keep, send)):
            total = None
            for n in range(OWNERS):
                coded = received[n, k, i].astype(jnp.float32)
                power = coded[:, features:features + 1] - SHIFT
                value = jnp.exp2(jnp.log2(jnp.abs(coded)) * 0.0625 + power)
                value = jnp.where(coded > 0, value, jnp.where(coded < 0, -value, 0.0))
                total = value if total is None else total + value
            for slot in range(2):
                first = (slot * CHUNKS + k) * live
                out[first:first + live] = total[slot * live:(slot + 1) * live, :features]


def add_up(received, features, after):
    rows = CHUNKS * received.shape[3]
    return pl.pallas_call(
        add_kernel,
        out_shape=[jax.ShapeDtypeStruct((rows, features), jnp.float32)] * 2,
        in_specs=[VMEM, ANY],
        out_specs=[VMEM] * 2,
        compiler_params=SMALL,
    )(received, after)


def merge_kernel(core_ref, mine, theirs, out, whole):
    half, features = mine.shape[0] // 2, mine.shape[1]
    for slot in range(2):
        for ref, part in ((mine, core_ref[0]), (theirs, 1 - core_ref[0])):
            first = pl.multiple_of((slot * 2 + part) * half, half)
            whole[pl.ds(first, half), :features] = ref[slot * half:(slot + 1) * half]
    out[...] = whole[...].T[:features].astype(out.dtype)


def merge(core, mine, theirs):
    rows, features = mine.shape
    return pl.pallas_call(
        merge_kernel,
        out_shape=jax.ShapeDtypeStruct((features, 2 * rows), jnp.bfloat16),
        in_specs=[pl.BlockSpec(memory_space=pltpu.SMEM), VMEM, VMEM],
        out_specs=VMEM,
        scratch_shapes=[pltpu.VMEM((2 * rows, (features + 127) // 128 * 128), jnp.float32)],
        compiler_params=SMALL,
    )(core, mine, theirs)


def on_device(activations, upstream, weight, bin_fill):
    bin_len, hidden = upstream.shape
    features = activations.shape[1]
    live = bin_len // (CORES * CHUNKS)
    x, core = lax.axis_index("x"), lax.axis_index("core")
    core_of = core.reshape(1).astype(jnp.int32)

    inputs = activations.T[None]
    inputs = jnp.concatenate([inputs, lax.ppermute(inputs, "far", flips(FAR, 1))], 0)
    other_weight = lax.ppermute(weight, "core", flips(CORES, 1))

    slot_index = jnp.arange(bin_len, dtype=jnp.int32)
    masked = jnp.where((slot_index < bin_fill[0])[:, None], upstream, jnp.zeros_like(upstream))
    both = lax.all_gather(masked, "core", axis=0)
    both, inputs = lax.optimization_barrier((both, inputs))
    both = lax.dynamic_slice_in_dim(both, core * CHUNKS * live, CHUNKS * live, 1)

    def over_x(array, flip):
        return lax.ppermute(array, "x", flips(X, flip))

    def over_row(block):
        block = block.reshape(-1, live, hidden)
        every = jnp.broadcast_to(block[None], (ROWS,) + block.shape)
        return lax.all_to_all(every, "row", 0, 0).reshape(-1, hidden)

    def run(chunk, pieces, after, earlier):
        counts, where = [], []
        for array, places in pieces:
            counts.append((0, len(places)))
            where += [(x_of * CORES + c) * ROWS + r for x_of, r, c in places]
        return partials(
            [array for array, _ in pieces], counts, jnp.stack(where).astype(jnp.int32),
            weight, other_weight, live, chunk, after, earlier)

    def wider(inputs, flip):
        return jnp.concatenate([inputs, lax.ppermute(inputs, "near", flips(NEAR, flip))], 0)

    x_1, x_2, x_3 = x ^ 1, x ^ 2, x ^ 3
    line = over_row(both[:, :live].reshape(CORES * live, hidden))
    first, second = both[0, live:], both[1, live:]
    first = jnp.concatenate([first, over_x(first, 1)], 0)
    second = jnp.concatenate([second, over_x(second, 3)], 0)
    first, second, inputs = lax.optimization_barrier((first, second, inputs))
    columns = jnp.concatenate([first, over_x(first, 3), second, over_x(second, 1)], 0)
    inputs = wider(inputs, 4)
    half = line.shape[0] // 2
    low, high = line[:half], line[half:]
    low = jnp.concatenate([low, over_x(low, 1)], 0)
    high = jnp.concatenate([high, over_x(high, 3)], 0)
    low, high, inputs = lax.optimization_barrier((low, high, inputs))
    row_first = low, over_x(low, 3), high, over_x(high, 1)
    inputs = wider(inputs, 2)
    plane = over_row(columns)
    inputs = [inputs, lax.ppermute(inputs, "near", flips(NEAR, 1))]

    held_0, coded = run(0, [
        (piece, [(x_of, r, c) for x_of in x_pair for r in rows for c in range(CORES)])
        for piece, x_pair, rows in zip(
            row_first, ((x, x_1), (x_3, x_2), (x, x_3), (x_1, x_2)), ((0, 1), (0, 1), (2, 3), (2, 3)))], [], None)
    order = [(x_of, 0) for x_of in (x, x_1, x_3, x_2)] + [(x_of, 1) for x_of in (x, x_3, x_1, x_2)]
    held_1, coded = run(1, [(plane, [(x_of, r, c) for r in range(ROWS) for x_of, c in order])], inputs[1:], coded)
    received = lax.all_to_all(coded, ("far", "near"), 0, 0)

    exchanged = [lax.ppermute(t, "core", flips(CORES, 1)) for t in (held_0, held_1)]
    place = lax.axis_index("far") * NEAR + lax.axis_index("near")
    d_weight = weight_grad(jnp.stack([core, place]).astype(jnp.int32), inputs, [held_0, held_1] + exchanged, live, features)

    keep, send = add_up(received, features, d_weight)
    d_input = merge(core_of, keep, lax.ppermute(send, "core", flips(CORES, 1)))
    return d_input.T, d_weight


def solution(mesh):
    fine = Mesh(mesh.devices.reshape(X, CORES, ROWS, FAR, NEAR), ("x", "core", "row", "far", "near"))
    tall, wide = ("x", "core", "row"), ("far", "near")
    return jax.shard_map(
        on_device, mesh=fine,
        in_specs=(P(wide, tall), P(tall, wide), P(tall, wide), P(tall)),
        out_specs=(P(wide, tall), P(tall, wide)), check_vma=False,
    )
```

time: 318 us -> 159 us (0.50)
  waiting for transfers between devices: 228 us -> 48.8 us
  starting transfers between devices: 0.08 us -> 71.6 us
  blocking collectives: 54.3 us -> 2.74 us
  Pallas kernels: 0 us -> 21.1 us
  matrix products: 13.3 us -> 0 us
  between operations: 14.8 us -> 1.61 us
  local copies, waits for them, and re-layouts: 0.02 us -> 7.58 us
    reduce_scatter x1 -> x0, waiting for transfers between devices: 124 us -> none  [on_device(): lax.psum_scatter(grad_x, 'col', scatter_dimension=0, tiled=True)]
    all_gather x1 -> x0, waiting for transfers between devices: 104 us -> none  [on_device(): block_rows = lax.all_gather(masked, ('dp', 'row'), axis=0, tiled=True)]
    ppermute x0 -> x16, starting transfers between devices: none -> 59.2 us  [the longest x8 21.1 us: over_x(): return lax.ppermute(array, 'x', flips(X, flip))]
    all_gather x1, blocking collectives: 54.3 us -> 2.74 us  [on_device(): both = lax.all_gather(masked, 'core', axis=0)]
    all_to_all x0 -> x3, waiting for transfers between devices: none -> 25.4 us  [the longest x1 20.9 us: on_device(): received = lax.all_to_all(coded, ('far', 'near'), 0, 0)]
    ppermute x0 -> x16, waiting for transfers between devices: none -> 23.4 us  [the longest x8 11.8 us: over_x(): return lax.ppermute(array, 'x', flips(X, flip))]
    pallas_call x0 -> x5, Pallas kernels: none -> 21.1 us  [the longest x2 11.6 us: partials(): pl.pallas_call(functools.partial(partial_kernel, live, chunk, counts), ou...]
    dot_general x2 -> x0, matrix products: 13.3 us -> none  [the longest x1 6.95 us: on_device(): lax.dot_general(block_rows, weight, (((1,), (1,)), ((), ())), preferred_e...]
  transfers between devices with their start and end apart: 2 -> 19, of which waited for: 2 -> 8; matrix products, arithmetic and copies ran while one was open for 2% -> 4% of each run, Pallas kernels for 0% -> 12%
where the time goes in v3:
time: 159 us; the launch traced here: 157 us
  starting transfers between devices  71.6 us (45%)
  waiting for transfers between devices  48.8 us (31%)
  Pallas kernels  21.1 us (13%)
  local copies, waits for them, and re-layouts  7.58 us (5%)
  other arithmetic  3.47 us (2%)
  blocking collectives  2.74 us (2%)
  between operations  1.61 us (1%)
    ppermute x8, starting transfers between devices, over_x(): return lax.ppermute(array, 'x', flips(X, flip))  21.1 us
    all_to_all x1, waiting for transfers between devices, on_device(): received = lax.all_to_all(coded, ('far', 'near'), 0, 0)  20.9 us
    ppermute x8, waiting for transfers between devices, over_x(): return lax.ppermute(array, 'x', flips(X, flip))  11.8 us
    pallas_call x2, Pallas kernels, partials(): pl.pallas_call(functools.partial(partial_kernel, live, chunk, counts), ou...  11.6 us
    ppermute x1, starting transfers between devices, on_device(): lax.ppermute(inputs, 'far', flips(FAR, 1))  11.5 us
    ppermute x2, starting transfers between devices, wider(): lax.ppermute(inputs, 'near', flips(NEAR, flip))  9.86 us
    ppermute x2, waiting for transfers between devices, wider(): lax.ppermute(inputs, 'near', flips(NEAR, flip))  8.38 us
    all_to_all x2, starting transfers between devices, over_row(): return lax.all_to_all(every, 'row', 0, 0).reshape(-1, hidden)  8.01 us
  transfers between devices with their start and end apart: 19, of which 8 were waited for; matrix products, arithmetic and copies ran while one was open for 4% of the time, Pallas kernels for 12%

profile of v3, /device:TPU:1, one launch (start us, length us, event | category | flops | bytes accessed | tf_op | source)
XLA Modules:
  0.0 156.9 jit_solution(8063803227095478989)
XLA Ops:
  0.6 11.5 %collective-permute-start = (bf16[1,232,128]{2,1,0:T(8,128)(2,1)}, bf16[1,232,128]{2,1,0:T(8,128)(2,1)S(1)}, u32[]{:S(2)}, u32[]{:S(2)}) collective-permute-start(bf16[1,232,128]{2,1,0:T(8,128)(2,1)} %bitcast.58), channel_id=1, source_target_pairs={{0,8},{8,0},{1,9},{9,1},{2,10},{10,2},{3,11},{11,3},{4,12},{12,4},... | collective-permute-start | bytes 178184 | tf_op jit(solution)/shard_map/ppermute | solution.py:190
  13.8 2.7 %all-gather = bf16[128,1856]{1,0:T(8,128)(2,1)S(1)} all-gather(bf16[64,1856]{1,0:T(8,128)(2,1)S(1)} %broadcast_select_fusion), channel_id=2, replica_groups=mesh['x'=4,'core'=2,'row'=4,'far'=2,'near'=8] {'core'}, dimensions={0}, use_global_device_ids=true | all-gather | bytes 712704 | tf_op jit(solution)/shard_map/all_gather | solution.py:195
  17.4 4.4 %collective-permute-start.2 = (bf16[16,1856]{1,0:T(8,128)(2,1)S(1)}, bf16[16,1856]{1,0:T(8,128)(2,1)S(1)}, u32[]{:S(2)}, u32[]{:S(2)}) collective-permute-start(bf16[16,1856]{1,0:T(8,128)(2,1)S(1)} %get-tuple-element.32), channel_id=1, source_target_pairs={{0,384},{128,256},{256,128},{384,0},{1,385},{129,257},{257,129},{3... | collective-permute-start | bytes 178184 | tf_op jit(solution)/shard_map/ppermute | solution.py:200
  21.8 1.9 %collective-permute-start.1 = (bf16[16,1856]{1,0:T(8,128)(2,1)S(1)}, bf16[16,1856]{1,0:T(8,128)(2,1)S(1)}, u32[]{:S(2)}, u32[]{:S(2)}) collective-permute-start(bf16[16,1856]{1,0:T(8,128)(2,1)S(1)} %get-tuple-element.33), channel_id=1, source_target_pairs={{0,128},{128,0},{256,384},{384,256},{1,129},{129,1},{257,385},{385... | collective-permute-start | bytes 178184 | tf_op jit(solution)/shard_map/ppermute | solution.py:200
  24.6 4.3 %all-to-all-start.1 = ((bf16[4,2,16,1856]{3,2,1,0:T(8,128)(2,1)}), bf16[4,2,16,1856]{3,2,1,0:T(8,128)(2,1)S(1)}, u32[]{:S(2)}, u32[]{:S(2)}) async-start(bf16[4,2,16,1856]{3,2,1,0:T(8,128)(2,1)} %broadcast_in_dim.32), calls=%async_computation.1 | async-start | bytes 983040 | tf_op jit(solution)/shard_map/all_to_all | solution.py:205
  28.9 2.7 %collective-permute-start.3 = (bf16[32,1856]{1,0:T(8,128)(2,1)S(1)}, bf16[32,1856]{1,0:T(8,128)(2,1)S(1)}, u32[]{:S(2)}, u32[]{:S(2)}) collective-permute-start(bf16[32,1856]{1,0:T(8,128)(2,1)S(1)} %pad_maximum_fusion.4), channel_id=1, source_target_pairs={{0,384},{128,256},{256,128},{384,0},{1,385},{129,257},{257,129},{3... | collective-permute-start | bytes 356360 | tf_op jit(solution)/shard_map/ppermute | solution.py:200
  31.6 2.6 %collective-permute-start.4 = (bf16[32,1856]{1,0:T(8,128)(2,1)S(1)}, bf16[32,1856]{1,0:T(8,128)(2,1)S(1)}, u32[]{:S(2)}, u32[]{:S(2)}) collective-permute-start(bf16[32,1856]{1,0:T(8,128)(2,1)S(1)} %pad_maximum_fusion.5), channel_id=1, source_target_pairs={{0,128},{128,0},{256,384},{384,256},{1,129},{129,1},{257,385},{385... | collective-permute-start | bytes 356360 | tf_op jit(solution)/shard_map/ppermute | solution.py:200
  34.2 1.8 %collective-permute-done.3 = bf16[32,1856]{1,0:T(8,128)(2,1)S(1)} collective-permute-done((bf16[32,1856]{1,0:T(8,128)(2,1)S(1)}, bf16[32,1856]{1,0:T(8,128)(2,1)S(1)}, u32[]{:S(2)}, u32[]{:S(2)}) %collective-permute-start.3) | collective-permute-done | bytes 118816 | tf_op jit(solution)/shard_map/ppermute | solution.py:200
  36.0 1.5 collective-permute-done.4
  37.6 4.6 %all-to-all-done.1 = bf16[4,2,16,1856]{3,2,1,0:T(8,128)(2,1)S(1)} async-done(((bf16[4,2,16,1856]{3,2,1,0:T(8,128)(2,1)}), bf16[4,2,16,1856]{3,2,1,0:T(8,128)(2,1)S(1)}, u32[]{:S(2)}, u32[]{:S(2)}) %all-to-all-start.1) | async-done | bytes 475168 | tf_op jit(solution)/shard_map/all_to_all | solution.py:205
  42.2 1.4 broadcast_in_dim.31
  43.6 3.7 %all-to-all-start = ((bf16[4,8,16,1856]{3,2,1,0:T(8,128)(2,1)}), bf16[4,8,16,1856]{3,2,1,0:T(8,128)(2,1)S(1)}, u32[]{:S(2)}, u32[]{:S(2)}) async-start(bf16[4,8,16,1856]{3,2,1,0:T(8,128)(2,1)} %broadcast_in_dim.31), calls=%async_computation | async-start | bytes 3932160 | tf_op jit(solution)/shard_map/all_to_all | solution.py:205
  47.4 3.4 %collective-permute-start.5 = (bf16[64,1856]{1,0:T(8,128)(2,1)S(1)}, bf16[64,1856]{1,0:T(8,128)(2,1)S(1)}, u32[]{:S(2)}, u32[]{:S(2)}) collective-permute-start(bf16[64,1856]{1,0:T(8,128)(2,1)S(1)} %bitcast.55), channel_id=1, source_target_pairs={{0,128},{128,0},{256,384},{384,256},{1,129},{129,1},{257,385},{385... | collective-permute-start | bytes 712712 | tf_op jit(solution)/shard_map/ppermute | solution.py:200
  50.7 7.5 %collective-permute-start.7 = (bf16[2,232,128]{2,1,0:T(8,128)(2,1)S(1)}, bf16[2,232,128]{2,1,0:T(8,128)(2,1)S(1)}, u32[]{:S(2)}, u32[]{:S(2)}) collective-permute-start(bf16[2,232,128]{2,1,0:T(8,128)(2,1)S(1)} %pad_maximum_fusion.6), channel_id=1, source_target_pairs={{0,4},{1,5},{2,6},{3,7},{4,0},{5,1},{6,2},{7,3},{8,12},{9,13},{10,... | collective-permute-start | bytes 356360 | tf_op jit(solution)/shard_map/ppermute | solution.py:217
  58.2 3.9 %collective-permute-start.12 = (bf16[232,1856]{1,0:T(8,128)(2,1)S(1)}, bf16[232,1856]{1,0:T(8,128)(2,1)}, u32[]{:S(2)}, u32[]{:S(2)}) collective-permute-start(bf16[232,1856]{1,0:T(8,128)(2,1)S(1)} %copy-done.2), channel_id=1, source_target_pairs={{0,64},{64,0},{1,65},{65,1},{2,66},{66,2},{3,67},{67,3},{4,68},{68... | collective-permute-start | bytes 2583560 | tf_op jit(solution)/shard_map/ppermute | solution.py:191
  62.1 2.1 %collective-permute-start.6 = (bf16[64,1856]{1,0:T(8,128)(2,1)S(1)}, bf16[64,1856]{1,0:T(8,128)(2,1)S(1)}, u32[]{:S(2)}, u32[]{:S(2)}) collective-permute-start(bf16[64,1856]{1,0:T(8,128)(2,1)S(1)} %bitcast.53), channel_id=1, source_target_pairs={{0,384},{128,256},{256,128},{384,0},{1,385},{129,257},{257,129},{3... | collective-permute-start | bytes 712712 | tf_op jit(solution)/shard_map/ppermute | solution.py:200
  64.4 8.5 %collective-permute-done.6 = bf16[64,1856]{1,0:T(8,128)(2,1)S(1)} collective-permute-done((bf16[64,1856]{1,0:T(8,128)(2,1)S(1)}, bf16[64,1856]{1,0:T(8,128)(2,1)S(1)}, u32[]{:S(2)}, u32[]{:S(2)}) %collective-permute-start.6) | collective-permute-done | bytes 237600 | tf_op jit(solution)/shard_map/ppermute | solution.py:200
  73.6 2.4 %collective-permute-start.8 = (bf16[4,232,128]{2,1,0:T(8,128)(2,1)S(1)}, bf16[4,232,128]{2,1,0:T(8,128)(2,1)S(1)}, u32[]{:S(2)}, u32[]{:S(2)}) collective-permute-start(bf16[4,232,128]{2,1,0:T(8,128)(2,1)S(1)} %pad_maximum_fusion.3), channel_id=1, source_target_pairs={{0,2},{1,3},{2,0},{3,1},{4,6},{5,7},{6,4},{7,5},{8,10},{9,11},{10,... | collective-permute-start | bytes 712712 | tf_op jit(solution)/shard_map/ppermute | solution.py:217
  76.0 2.1 %collective-permute-start.10 = (bf16[128,1856]{1,0:T(8,128)(2,1)S(1)}, bf16[128,1856]{1,0:T(8,128)(2,1)}, u32[]{:S(2)}, u32[]{:S(2)}) collective-permute-start(bf16[128,1856]{1,0:T(8,128)(2,1)S(1)} %pad_maximum_fusion.1.refs_0_), channel_id=1, source_target_pairs={{0,384},{128,256},{256,128},{384,0},{1,385},{129,257},{257,129},{3... | collective-permute-start | bytes 1425416 | tf_op jit(solution)/shard_map/ppermute | solution.py:200
  78.2 1.9 %collective-permute-start.11 = (bf16[128,1856]{1,0:T(8,128)(2,1)}, bf16[128,1856]{1,0:T(8,128)(2,1)}, u32[]{:S(2)}, u32[]{:S(2)}) collective-permute-start(bf16[128,1856]{1,0:T(8,128)(2,1)} %pad_maximum_fusion.2.refs_2_), channel_id=1, source_target_pairs={{0,128},{128,0},{256,384},{384,256},{1,129},{129,1},{257,385},{385... | collective-permute-start | bytes 1425416 | tf_op jit(solution)/shard_map/ppermute | solution.py:200
  80.8 8.4 %collective-permute-done.8 = bf16[4,232,128]{2,1,0:T(8,128)(2,1)S(1)} collective-permute-done((bf16[4,232,128]{2,1,0:T(8,128)(2,1)S(1)}, bf16[4,232,128]{2,1,0:T(8,128)(2,1)S(1)}, u32[]{:S(2)}, u32[]{:S(2)}) %collective-permute-start.8) | collective-permute-done | bytes 237600 | tf_op jit(solution)/shard_map/ppermute | solution.py:217
  89.9 1.9 %collective-permute-start.9 = (bf16[8,232,128]{2,1,0:T(8,128)(2,1)}, bf16[8,232,128]{2,1,0:T(8,128)(2,1)}, u32[]{:S(2)}, u32[]{:S(2)}) collective-permute-start(bf16[8,232,128]{2,1,0:T(8,128)(2,1)} %constant_dynamic-update-slice_fusion.inputs), channel_id=1, source_target_pairs={{0,1},{1,0},{2,3},{3,2},{4,5},{5,4},{6,7},{7,6},{8,9},{9,8},{10,11... | collective-permute-start | bytes 1425416 | tf_op jit(solution)/shard_map/ppermute | solution.py:235
  93.2 5.8 %shard_map.59 = (bf16[32,16,1856]{2,1,0:T(8,128)(2,1)}, bf16[16,2,2,32,256]{4,3,2,1,0:T(8,128)(2,1)}) custom-call(s32[32]{0:T(128)} %stack.174.where_ref, bf16[128,1856]{1,0:T(8,128)(2,1)} %copy-done.3, bf16[128,1856]{1,0:T(8,128)(2,1)} %collective-permute-done.10.refs_1_, bf16[128,1856]{1,0:T(8,128)(2,1)} %pad_maximum_fusion.2.refs_2_, ...), custom_call_target="tpu_custom_call" | custom-call | flops 881852416 | bytes 3801088 | tf_op jit(solution)/shard_map/pallas_call | solution.py:71
  99.0 2.7 %collective-permute-start.13 = (bf16[32,16,1856]{2,1,0:T(8,128)(2,1)}, bf16[32,16,1856]{2,1,0:T(8,128)(2,1)}, u32[]{:S(2)}, u32[]{:S(2)}) collective-permute-start(bf16[32,16,1856]{2,1,0:T(8,128)(2,1)} %get-tuple-element.26.refs_0_), channel_id=1, source_target_pairs={{0,64},{64,0},{1,65},{65,1},{2,66},{66,2},{3,67},{67,3},{4,68},{68... | collective-permute-start | bytes 5701640 | tf_op jit(solution)/shard_map/ppermute | solution.py:245
  101.7 2.3 %collective-permute-done.9.refs_1_.more = bf16[8,232,128]{2,1,0:T(8,128)(2,1)} collective-permute-done((bf16[8,232,128]{2,1,0:T(8,128)(2,1)}, bf16[8,232,128]{2,1,0:T(8,128)(2,1)}, u32[]{:S(2)}, u32[]{:S(2)}) %collective-permute-start.9) | collective-permute-done | bytes 475168 | tf_op jit(solution)/shard_map/ppermute | solution.py:235
  104.0 1.3 copy-done.1
  105.4 5.8 %shard_map.60 = (bf16[32,16,1856]{2,1,0:T(8,128)(2,1)}, bf16[16,2,2,32,256]{4,3,2,1,0:T(8,128)(2,1)}) custom-call(s32[32]{0:T(128)} %stack.173.where_ref, bf16[512,1856]{1,0:T(8,128)(2,1)} %bitcast.49, bf16[8,232,128]{2,1,0:T(8,128)(2,1)} %collective-permute-done.9.refs_1_.more, ...), custom_call_target="tpu_custom_call", output_to_operand_aliasing={{1}: (3, {})} | custom-call | flops 881852416 | bytes 3801088 | tf_op jit(solution)/shard_map/pallas_call | solution.py:71
  111.2 3.3 %collective-permute-start.14 = (bf16[32,16,1856]{2,1,0:T(8,128)(2,1)}, bf16[32,16,1856]{2,1,0:T(8,128)(2,1)}, u32[]{:S(2)}, u32[]{:S(2)}) collective-permute-start(bf16[32,16,1856]{2,1,0:T(8,128)(2,1)} %get-tuple-element.27.refs_1_), channel_id=1, source_target_pairs={{0,64},{64,0},{1,65},{65,1},{2,66},{66,2},{3,67},{67,3},{4,68},{68... | collective-permute-start | bytes 5701640 | tf_op jit(solution)/shard_map/ppermute | solution.py:245
  114.4 4.4 %all-to-all-start.2 = ((bf16[16,2,2,32,256]{4,3,2,1,0:T(8,128)(2,1)}), bf16[16,2,2,32,256]{4,3,2,1,0:T(8,128)(2,1)S(1)}, u32[]{:S(2)}, u32[]{:S(2)}) async-start(bf16[16,2,2,32,256]{4,3,2,1,0:T(8,128)(2,1)} %get-tuple-element.25), calls=%async_computation.2 | async-start | bytes 2097152 | tf_op jit(solution)/shard_map/all_to_all | solution.py:243
  119.5 7.9 %shard_map.61.after = bf16[232,1856]{1,0:T(8,128)(2,1)} custom-call(s32[2]{0:T(128)} %pad_add_fusion.core_ref, bf16[8,232,128]{2,1,0:T(8,128)(2,1)} %constant_dynamic-update-slice_fusion.inputs, bf16[8,232,128]{2,1,0:T(8,128)(2,1)} %collective-permute-done.9.refs_1_.more, bf16[32,16,1856]{2,1,0:T(8,128)(2,1)} %get-tuple-element.26.refs_0_, ...), custom_call_target="tpu_custom_call" | custom-call | flops 1763704832 | bytes 7602176 | tf_op jit(solution)/shard_map/pallas_call | solution.py:117
  127.4 20.9 %all-to-all-done.2.received = bf16[16,2,2,32,256]{4,3,2,1,0:T(8,128)(2,1)S(1)} async-done(((bf16[16,2,2,32,256]{4,3,2,1,0:T(8,128)(2,1)}), bf16[16,2,2,32,256]{4,3,2,1,0:T(8,128)(2,1)S(1)}, u32[]{:S(2)}, u32[]{:S(2)}) %all-to-all-start.2) | async-done | bytes 1048608 | tf_op jit(solution)/shard_map/all_to_all | solution.py:243
  150.3 4.9 %collective-permute-start.15 = (f32[64,232]{1,0:T(8,128)S(1)}, f32[64,232]{1,0:T(8,128)S(1)}, u32[]{:S(2)}, u32[]{:S(2)}) collective-permute-start(f32[64,232]{1,0:T(8,128)S(1)} %get-tuple-element.29), channel_id=1, source_target_pairs={{0,64},{64,0},{1,65},{65,1},{2,66},{66,2},{3,67},{67,3},{4,68},{68... | collective-permute-start | bytes 178184 | tf_op jit(solution)/shard_map/ppermute | solution.py:250
  (39 shorter events, 10.9 us)
Async XLA Ops:
  0.6 15.9 %collective-permute-start = (bf16[1,232,128]{2,1,0:T(8,128)(2,1)}, bf16[1,232,128]{2,1,0:T(8,128)(2,1)S(1)}, u32[]{:S(2)}, u32[]{:S(2)}) collective-permute-start(bf16[1,232,128]{2,1,0:T(8,128)(2,1)} %bitcast.58), channel_id=1, source_target_pairs={{0,8},{8,0},{1,9},{9,1},{2,10},{10,2},{3,11},{11,3},{4,12},{12,4},... | collective-permute-start | bytes 178184 | tf_op jit(solution)/shard_map/ppermute | solution.py:190
  17.4 11.4 %collective-permute-start.2 = (bf16[16,1856]{1,0:T(8,128)(2,1)S(1)}, bf16[16,1856]{1,0:T(8,128)(2,1)S(1)}, u32[]{:S(2)}, u32[]{:S(2)}) collective-permute-start(bf16[16,1856]{1,0:T(8,128)(2,1)S(1)} %get-tuple-element.32), channel_id=1, source_target_pairs={{0,384},{128,256},{256,128},{384,0},{1,385},{129,257},{257,129},{3... | collective-permute-start | bytes 178184 | tf_op jit(solution)/shard_map/ppermute | solution.py:200
  21.8 7.0 %collective-permute-start.1 = (bf16[16,1856]{1,0:T(8,128)(2,1)S(1)}, bf16[16,1856]{1,0:T(8,128)(2,1)S(1)}, u32[]{:S(2)}, u32[]{:S(2)}) collective-permute-start(bf16[16,1856]{1,0:T(8,128)(2,1)S(1)} %get-tuple-element.33), channel_id=1, source_target_pairs={{0,128},{128,0},{256,384},{384,256},{1,129},{129,1},{257,385},{385... | collective-permute-start | bytes 178184 | tf_op jit(solution)/shard_map/ppermute | solution.py:200
  24.6 17.6 %all-to-all-start.1 = ((bf16[4,2,16,1856]{3,2,1,0:T(8,128)(2,1)}), bf16[4,2,16,1856]{3,2,1,0:T(8,128)(2,1)S(1)}, u32[]{:S(2)}, u32[]{:S(2)}) async-start(bf16[4,2,16,1856]{3,2,1,0:T(8,128)(2,1)} %broadcast_in_dim.32), calls=%async_computation.1 | async-start | bytes 983040 | tf_op jit(solution)/shard_map/all_to_all | solution.py:205
  28.9 7.1 %collective-permute-start.3 = (bf16[32,1856]{1,0:T(8,128)(2,1)S(1)}, bf16[32,1856]{1,0:T(8,128)(2,1)S(1)}, u32[]{:S(2)}, u32[]{:S(2)}) collective-permute-start(bf16[32,1856]{1,0:T(8,128)(2,1)S(1)} %pad_maximum_fusion.4), channel_id=1, source_target_pairs={{0,384},{128,256},{256,128},{384,0},{1,385},{129,257},{257,129},{3... | collective-permute-start | bytes 356360 | tf_op jit(solution)/shard_map/ppermute | solution.py:200
  31.6 5.9 %collective-permute-start.4 = (bf16[32,1856]{1,0:T(8,128)(2,1)S(1)}, bf16[32,1856]{1,0:T(8,128)(2,1)S(1)}, u32[]{:S(2)}, u32[]{:S(2)}) collective-permute-start(bf16[32,1856]{1,0:T(8,128)(2,1)S(1)} %pad_maximum_fusion.5), channel_id=1, source_target_pairs={{0,128},{128,0},{256,384},{384,256},{1,129},{129,1},{257,385},{385... | collective-permute-start | bytes 356360 | tf_op jit(solution)/shard_map/ppermute | solution.py:200
  43.6 14.6 %copy-start.2 = (bf16[232,1856]{1,0:T(8,128)(2,1)S(1)}, bf16[232,1856]{1,0:T(8,128)(2,1)}, u32[]{:S(2)}) copy-start(bf16[232,1856]{1,0:T(8,128)(2,1)} %refs_3_.1) | copy-start | bytes 2583556
  43.6 60.5 %all-to-all-start = ((bf16[4,8,16,1856]{3,2,1,0:T(8,128)(2,1)}), bf16[4,8,16,1856]{3,2,1,0:T(8,128)(2,1)S(1)}, u32[]{:S(2)}, u32[]{:S(2)}) async-start(bf16[4,8,16,1856]{3,2,1,0:T(8,128)(2,1)} %broadcast_in_dim.31), calls=%async_computation | async-start | bytes 3932160 | tf_op jit(solution)/shard_map/all_to_all | solution.py:205
  47.4 16.9 %collective-permute-start.5 = (bf16[64,1856]{1,0:T(8,128)(2,1)S(1)}, bf16[64,1856]{1,0:T(8,128)(2,1)S(1)}, u32[]{:S(2)}, u32[]{:S(2)}) collective-permute-start(bf16[64,1856]{1,0:T(8,128)(2,1)S(1)} %bitcast.55), channel_id=1, source_target_pairs={{0,128},{128,0},{256,384},{384,256},{1,129},{129,1},{257,385},{385... | collective-permute-start | bytes 712712 | tf_op jit(solution)/shard_map/ppermute | solution.py:200
  50.7 13.5 %collective-permute-start.7 = (bf16[2,232,128]{2,1,0:T(8,128)(2,1)S(1)}, bf16[2,232,128]{2,1,0:T(8,128)(2,1)S(1)}, u32[]{:S(2)}, u32[]{:S(2)}) collective-permute-start(bf16[2,232,128]{2,1,0:T(8,128)(2,1)S(1)} %pad_maximum_fusion.6), channel_id=1, source_target_pairs={{0,4},{1,5},{2,6},{3,7},{4,0},{5,1},{6,2},{7,3},{8,12},{9,13},{10,... | collective-permute-start | bytes 356360 | tf_op jit(solution)/shard_map/ppermute | solution.py:217
  58.2 35.0 %collective-permute-start.12 = (bf16[232,1856]{1,0:T(8,128)(2,1)S(1)}, bf16[232,1856]{1,0:T(8,128)(2,1)}, u32[]{:S(2)}, u32[]{:S(2)}) collective-permute-start(bf16[232,1856]{1,0:T(8,128)(2,1)S(1)} %copy-done.2), channel_id=1, source_target_pairs={{0,64},{64,0},{1,65},{65,1},{2,66},{66,2},{3,67},{67,3},{4,68},{68... | collective-permute-start | bytes 2583560 | tf_op jit(solution)/shard_map/ppermute | solution.py:191
  62.1 10.7 %collective-permute-start.6 = (bf16[64,1856]{1,0:T(8,128)(2,1)S(1)}, bf16[64,1856]{1,0:T(8,128)(2,1)S(1)}, u32[]{:S(2)}, u32[]{:S(2)}) collective-permute-start(bf16[64,1856]{1,0:T(8,128)(2,1)S(1)} %bitcast.53), channel_id=1, source_target_pairs={{0,384},{128,256},{256,128},{384,0},{1,385},{129,257},{257,129},{3... | collective-permute-start | bytes 712712 | tf_op jit(solution)/shard_map/ppermute | solution.py:200
  64.3 28.9 %copy-start.3 = (bf16[128,1856]{1,0:T(8,128)(2,1)}, bf16[128,1856]{1,0:T(8,128)(2,1)S(1)}, u32[]{:S(2)}) copy-start(bf16[128,1856]{1,0:T(8,128)(2,1)S(1)} %pad_maximum_fusion.1.refs_0_) | copy-start | bytes 1425412
  73.6 15.6 %collective-permute-start.8 = (bf16[4,232,128]{2,1,0:T(8,128)(2,1)S(1)}, bf16[4,232,128]{2,1,0:T(8,128)(2,1)S(1)}, u32[]{:S(2)}, u32[]{:S(2)}) collective-permute-start(bf16[4,232,128]{2,1,0:T(8,128)(2,1)S(1)} %pad_maximum_fusion.3), channel_id=1, source_target_pairs={{0,2},{1,3},{2,0},{3,1},{4,6},{5,7},{6,4},{7,5},{8,10},{9,11},{10,... | collective-permute-start | bytes 712712 | tf_op jit(solution)/shard_map/ppermute | solution.py:217
  76.0 17.2 %collective-permute-start.10 = (bf16[128,1856]{1,0:T(8,128)(2,1)S(1)}, bf16[128,1856]{1,0:T(8,128)(2,1)}, u32[]{:S(2)}, u32[]{:S(2)}) collective-permute-start(bf16[128,1856]{1,0:T(8,128)(2,1)S(1)} %pad_maximum_fusion.1.refs_0_), channel_id=1, source_target_pairs={{0,384},{128,256},{256,128},{384,0},{1,385},{129,257},{257,129},{3... | collective-permute-start | bytes 1425416 | tf_op jit(solution)/shard_map/ppermute | solution.py:200
  78.2 15.0 %collective-permute-start.11 = (bf16[128,1856]{1,0:T(8,128)(2,1)}, bf16[128,1856]{1,0:T(8,128)(2,1)}, u32[]{:S(2)}, u32[]{:S(2)}) collective-permute-start(bf16[128,1856]{1,0:T(8,128)(2,1)} %pad_maximum_fusion.2.refs_2_), channel_id=1, source_target_pairs={{0,128},{128,0},{256,384},{384,256},{1,129},{129,1},{257,385},{385... | collective-permute-start | bytes 1425416 | tf_op jit(solution)/shard_map/ppermute | solution.py:200
  89.9 14.1 %collective-permute-start.9 = (bf16[8,232,128]{2,1,0:T(8,128)(2,1)}, bf16[8,232,128]{2,1,0:T(8,128)(2,1)}, u32[]{:S(2)}, u32[]{:S(2)}) collective-permute-start(bf16[8,232,128]{2,1,0:T(8,128)(2,1)} %constant_dynamic-update-slice_fusion.inputs), channel_id=1, source_target_pairs={{0,1},{1,0},{2,3},{3,2},{4,5},{5,4},{6,7},{7,6},{8,9},{9,8},{10,11... | collective-permute-start | bytes 1425416 | tf_op jit(solution)/shard_map/ppermute | solution.py:235
  99.0 20.5 %collective-permute-start.13 = (bf16[32,16,1856]{2,1,0:T(8,128)(2,1)}, bf16[32,16,1856]{2,1,0:T(8,128)(2,1)}, u32[]{:S(2)}, u32[]{:S(2)}) collective-permute-start(bf16[32,16,1856]{2,1,0:T(8,128)(2,1)} %get-tuple-element.26.refs_0_), channel_id=1, source_target_pairs={{0,64},{64,0},{1,65},{65,1},{2,66},{66,2},{3,67},{67,3},{4,68},{68... | collective-permute-start | bytes 5701640 | tf_op jit(solution)/shard_map/ppermute | solution.py:245
  104.0 1.3 copy-start.1
  111.2 8.3 %collective-permute-start.14 = (bf16[32,16,1856]{2,1,0:T(8,128)(2,1)}, bf16[32,16,1856]{2,1,0:T(8,128)(2,1)}, u32[]{:S(2)}, u32[]{:S(2)}) collective-permute-start(bf16[32,16,1856]{2,1,0:T(8,128)(2,1)} %get-tuple-element.27.refs_1_), channel_id=1, source_target_pairs={{0,64},{64,0},{1,65},{65,1},{2,66},{66,2},{3,67},{67,3},{4,68},{68... | collective-permute-start | bytes 5701640 | tf_op jit(solution)/shard_map/ppermute | solution.py:245
  114.4 33.8 %all-to-all-start.2 = ((bf16[16,2,2,32,256]{4,3,2,1,0:T(8,128)(2,1)}), bf16[16,2,2,32,256]{4,3,2,1,0:T(8,128)(2,1)S(1)}, u32[]{:S(2)}, u32[]{:S(2)}) async-start(bf16[16,2,2,32,256]{4,3,2,1,0:T(8,128)(2,1)} %get-tuple-element.25), calls=%async_computation.2 | async-start | bytes 2097152 | tf_op jit(solution)/shard_map/all_to_all | solution.py:243
  148.2 1.2 copy-start
  150.3 5.8 %collective-permute-start.15 = (f32[64,232]{1,0:T(8,128)S(1)}, f32[64,232]{1,0:T(8,128)S(1)}, u32[]{:S(2)}, u32[]{:S(2)}) collective-permute-start(f32[64,232]{1,0:T(8,128)S(1)} %get-tuple-element.29), channel_id=1, source_target_pairs={{0,64},{64,0},{1,65},{65,1},{2,66},{66,2},{3,67},{67,3},{4,68},{68... | collective-permute-start | bytes 178184 | tf_op jit(solution)/shard_map/ppermute | solution.py:250

commit v4 on v0

v4 whole, which is shorter than its diff:
```python
import jax
import jax.numpy as jnp
from jax import lax
from jax.experimental import pallas as pl
from jax.experimental.pallas import tpu as pltpu
from jax.sharding import Mesh
from jax.sharding import PartitionSpec as P

X, CORES, ROWS, FAR, NEAR = 4, 2, 4, 2, 8
BINS = X * CORES * ROWS
OWNERS = FAR * NEAR
VMEM = pl.BlockSpec(memory_space=pltpu.VMEM)
SMEM = pl.BlockSpec(memory_space=pltpu.SMEM)
ANY = pl.BlockSpec(memory_space=pl.ANY)
TINY = 2.0 ** -100
SHIFT = 7.5
LARGE = pltpu.CompilerParams(vmem_limit_bytes=60 << 20)
SMALL = pltpu.CompilerParams(vmem_limit_bytes=16 << 20)


def flips(size, flip):
    return [(i, i ^ flip) for i in range(size)]


def coded_of(result, lanes):
    rows, features = result.shape
    top = jnp.max(jnp.abs(result), axis=1, keepdims=True)
    power = jnp.ceil(jnp.log2(jnp.maximum(top, TINY)))
    raised = result * jnp.exp2(SHIFT - power)
    for _ in range(4):
        raised = raised * raised
    result = jnp.where(result < 0, -raised, raised)
    result = jnp.concatenate([result, jnp.zeros((rows, lanes - features), jnp.float32)], 1)
    lane = lax.broadcasted_iota(jnp.int32, (rows, lanes), 1)
    return jnp.where(lane < features, result, power).astype(jnp.bfloat16)


def partial_kernel(count, where_ref, *refs):
    pieces = refs[:count]
    own_ref, other_ref, out, sums, sems = refs[-5:]
    lanes = sums.shape[-1]
    copies = []
    for n, piece in enumerate(pieces):
        live, hidden = piece.shape[2:]
        tokens = piece[...].reshape(8 * live, hidden)
        for i, ref in enumerate((own_ref, other_ref)):
            coded = coded_of(lax.dot_general(
                tokens, ref[...], (((1,), (1,)), ((), ())), preferred_element_type=jnp.float32), lanes)
            for m in range(8):
                owner, slot = n * 4 + m // 4 * 2 + m % 2, m // 2 % 2
                sums[owner, i, slot * live:(slot + 1) * live] = coded[m * live:(m + 1) * live]
        for owner in range(n * 4, n * 4 + 4):
            copies.append(pltpu.make_async_copy(sums.at[owner], out.at[where_ref[owner]], sems.at[owner]))
            copies[-1].start()
    for copy in copies:
        copy.wait()


def partials(pieces, where, own, other, after, earlier):
    features, hidden = own.shape
    rows = sum(piece.size // hidden for piece in pieces)
    lanes = features // 128 * 128 + 128
    coded = jax.ShapeDtypeStruct((OWNERS, 2, rows // (4 * len(pieces)), lanes), jnp.bfloat16)
    after = after + ([] if earlier is None else [earlier])
    return pl.pallas_call(
        lambda *refs: partial_kernel(len(pieces), *refs),
        out_shape=coded,
        in_specs=[SMEM] + [VMEM] * len(pieces) + [ANY] * len(after) + [VMEM] * 2,
        out_specs=ANY,
        input_output_aliases={} if earlier is None else {len(pieces) + len(after): 0},
        scratch_shapes=[
            pltpu.VMEM((4 * len(pieces),) + coded.shape[1:], coded.dtype),
            pltpu.SemaphoreType.DMA((4 * len(pieces),))],
        compiler_params=LARGE,
        cost_estimate=pl.CostEstimate(
            flops=4 * rows * hidden * features, bytes_accessed=2 * rows * hidden, transcendentals=0),
    )(where, *pieces, *after, own, other)


def weight_grad_kernel(place_ref, where_ref, inputs, more, *refs):
    pieces, (out, held, tokens, sems) = refs[:-4], refs[-4:]
    core, owner = place_ref[0], place_ref[1]
    features, hidden = out.shape
    half = len(pieces) // 2
    copies = []
    for n, piece in enumerate(pieces):
        for m in range(8):
            copies.append(pltpu.make_async_copy(
                piece.at[m // 2, m % 2],
                tokens.at[where_ref[n % half * 8 + m], core if n < half else 1 - core],
                sems.at[len(copies)]))
    for copy in copies:
        copy.start()
    width = inputs.shape[2]
    for i in range(OWNERS):
        flip = (i & 1) * 4 + (i & 2) + (i >> 2 & 1) * NEAR + (i >> 3)
        first = pl.multiple_of((owner ^ flip) * width, width)
        held[:, pl.ds(first, width)] = inputs[i] if i < NEAR else more[i - NEAR]
    for copy in copies:
        copy.wait()
    for first in range(0, hidden, 256):
        last = min(first + 256, hidden)
        rows = tokens[:, :, :, first:last].reshape(held.shape[1], last - first)
        out[:, first:last] = lax.dot_general(
            held[...], rows, (((1,), (0,)), ((), ())), preferred_element_type=jnp.float32).astype(out.dtype)


def weight_grad(place, where, inputs, pieces):
    features, width = inputs[0].shape[1:]
    rows, hidden = OWNERS * width, pieces[0].shape[3]
    return pl.pallas_call(
        weight_grad_kernel,
        out_shape=jax.ShapeDtypeStruct((features, hidden), jnp.bfloat16),
        in_specs=[SMEM, SMEM, VMEM, VMEM] + [ANY] * len(pieces),
        out_specs=VMEM,
        scratch_shapes=[
            pltpu.VMEM((features, rows), jnp.bfloat16),
            pltpu.VMEM((BINS, CORES, rows // (BINS * CORES), hidden), jnp.bfloat16),
            pltpu.SemaphoreType.DMA((8 * len(pieces),))],
        compiler_params=LARGE,
        cost_estimate=pl.CostEstimate(
            flops=2 * rows * hidden * features, bytes_accessed=2 * rows * hidden, transcendentals=0),
    )(place, where, *inputs, *pieces)


def add_kernel(received, after, keep, send):
    del after
    features = keep.shape[1]
    for i, out in enumerate((keep, send)):
        total = None
        for n in range(OWNERS):
            coded = received[n, i].astype(jnp.float32)
            power = coded[:, features:features + 1] - SHIFT
            value = jnp.exp2(jnp.log2(jnp.abs(coded)) * 0.0625 + power)
            value = jnp.where(coded > 0, value, jnp.where(coded < 0, -value, 0.0))
            total = value if total is None else total + value
        out[...] = total[:, :features]


def add_up(received, features, after):
    return pl.pallas_call(
        add_kernel,
        out_shape=[jax.ShapeDtypeStruct((received.shape[2], features), jnp.float32)] * 2,
        in_specs=[VMEM, ANY],
        out_specs=[VMEM] * 2,
        compiler_params=SMALL,
    )(received, after)


def merge_kernel(place_ref, mine, theirs, out, whole):
    half, features = mine.shape[0] // 2, mine.shape[1]
    for slot in range(2):
        for ref, part in ((mine, place_ref[0]), (theirs, 1 - place_ref[0])):
            first = pl.multiple_of((slot * 2 + part) * half, half)
            whole[pl.ds(first, half), :features] = ref[slot * half:(slot + 1) * half]
    out[...] = whole[...].T[:features].astype(out.dtype)


def merge(place, mine, theirs):
    rows, features = mine.shape
    return pl.pallas_call(
        merge_kernel,
        out_shape=jax.ShapeDtypeStruct((features, 2 * rows), jnp.bfloat16),
        in_specs=[SMEM, VMEM, VMEM],
        out_specs=VMEM,
        scratch_shapes=[pltpu.VMEM((2 * rows, (features + 127) // 128 * 128), jnp.float32)],
        compiler_params=SMALL,
    )(place, mine, theirs)


def on_device(activations, upstream, weight, bin_fill):
    bin_len, hidden = upstream.shape
    features = activations.shape[1]
    live = bin_len // CORES
    x, core = lax.axis_index("x"), lax.axis_index("core")
    place = jnp.stack([core, lax.axis_index("far") * NEAR + lax.axis_index("near")]).astype(jnp.int32)

    def swap(array):
        return lax.ppermute(array, "core", flips(CORES, 1))

    def over_x(array, flip):
        return lax.ppermute(array, "x", flips(X, flip))

    def wider(inputs, axis, size, flip):
        return jnp.concatenate([inputs, lax.ppermute(inputs, axis, flips(size, flip))], 0)

    slot_index = jnp.arange(bin_len, dtype=jnp.int32)
    masked = jnp.where((slot_index < bin_fill[0])[:, None], upstream, jnp.zeros_like(upstream))
    both = lax.all_gather(masked, "core", axis=0)
    both = lax.dynamic_slice_in_dim(both, core * live, live, 1)
    both, inputs = lax.optimization_barrier((both, activations.T[None]))
    line = lax.all_to_all(jnp.broadcast_to(both[None], (ROWS,) + both.shape), "row", 0, 0)
    inputs = wider(wider(inputs, "near", NEAR, 4), "near", NEAR, 2)
    line, inputs = lax.optimization_barrier((line, inputs))

    other_weight = swap(weight)
    low, high = line[:ROWS // 2], line[ROWS // 2:]
    low = jnp.concatenate([low, over_x(low, 1)], 0)
    high = jnp.concatenate([high, over_x(high, 3)], 0)
    inputs = [wider(inputs, "far", FAR, 1)]
    high, inputs[0] = lax.optimization_barrier((high, inputs[0]))
    far_low, far_high = over_x(low, 3), over_x(high, 1)
    inputs.append(lax.ppermute(inputs[0], "near", flips(NEAR, 1)))

    x_1, x_2, x_3 = x ^ 1, x ^ 2, x ^ 3
    pieces = [low, high, far_low, far_high]
    origins = [((x, x_1), 0), ((x, x_3), 1), ((x_3, x_2), 0), ((x_1, x_2), 1)]
    owners = [(x_of * CORES + c) * 2 + pair for x_pair, pair in origins for x_of in x_pair for c in range(CORES)]
    bins = [(x_of * CORES + c) * ROWS + pair * 2 + r
            for x_pair, pair in origins for x_of in x_pair for r in range(2) for c in range(CORES)]
    owners, bins = (jnp.stack(table).astype(jnp.int32) for table in (owners, bins))

    coded = partials(pieces[:2], owners[:8], weight, other_weight, [], None)
    coded = partials(pieces[2:], owners[8:], weight, other_weight, inputs[1:], coded)
    received = lax.all_to_all(coded, ("far", "near"), 0, 0)
    d_weight = weight_grad(place, bins, inputs, pieces + [swap(piece) for piece in pieces])

    keep, send = add_up(received, features, d_weight)
    d_input = merge(place, keep, swap(send))
    return d_input.T, d_weight


def solution(mesh):
    fine = Mesh(mesh.devices.reshape(X, CORES, ROWS, FAR, NEAR), ("x", "core", "row", "far", "near"))
    tall, wide = ("x", "core", "row"), ("far", "near")
    return jax.shard_map(
        on_device, mesh=fine,
        in_specs=(P(wide, tall), P(tall, wide), P(tall, wide), P(tall)),
        out_specs=(P(wide, tall), P(tall, wide)), check_vma=False,
    )
```

time: 318 us -> 138 us (0.43); the launches traced: 314 us -> 137 us
  waiting for transfers between devices: 228 us -> 35.2 us
  starting transfers between devices: 0.08 us -> 65 us
  blocking collectives: 54.3 us -> 8.66 us
  Pallas kernels: 0 us -> 19.4 us
  matrix products: 13.3 us -> 0 us
  between operations: 14.8 us -> 1.65 us
  local copies, waits for them, and re-layouts: 0.02 us -> 5.15 us
    reduce_scatter x1 -> x0, waiting for transfers between devices: 124 us -> none  [on_device(): lax.psum_scatter(grad_x, 'col', scatter_dimension=0, tiled=True)]
    all_gather x1 -> x0, waiting for transfers between devices: 104 us -> none  [on_device(): block_rows = lax.all_gather(masked, ('dp', 'row'), axis=0, tiled=True)]
    ppermute x0 -> x14, starting transfers between devices: none -> 54.3 us  [the longest x6 25.5 us: swap(): return lax.ppermute(array, 'core', flips(CORES, 1))]
    all_gather x1, blocking collectives: 54.3 us -> 8.66 us  [on_device(): both = lax.all_gather(masked, 'core', axis=0)]
    ppermute x0 -> x14, waiting for transfers between devices: none -> 26.3 us  [the longest x3 15 us: wider(): lax.ppermute(inputs, axis, flips(size, flip))]
    pallas_call x0 -> x5, Pallas kernels: none -> 19.4 us  [the longest x2 8.93 us: partials(): pl.pallas_call(lambda *refs: partial_kernel(len(pieces), *refs), out_shap...]
    dot_general x2 -> x0, matrix products: 13.3 us -> none  [the longest x1 6.95 us: on_device(): lax.dot_general(block_rows, weight, (((1,), (1,)), ((), ())), preferred_e...]
    all_to_all x0 -> x2, starting transfers between devices: none -> 10.7 us  [the longest x1 7.02 us: on_device(): received = lax.all_to_all(coded, ('far', 'near'), 0, 0)]
  transfers between devices with their start and end apart: 2 -> 16, of which waited for: 2 -> 9; matrix products, arithmetic and copies ran while one was open for 2% -> 2% of each run, Pallas kernels for 0% -> 9%
where the time goes in v4:
time: 138 us; the launch traced here: 137 us
  starting transfers between devices  65 us (47%)
  waiting for transfers between devices  35.2 us (26%)
  Pallas kernels  19.4 us (14%)
  blocking collectives  8.66 us (6%)
  local copies, waits for them, and re-layouts  5.15 us (4%)
  other arithmetic  2.01 us (1%)
  between operations  1.65 us (1%)
    ppermute x6, starting transfers between devices, swap(): return lax.ppermute(array, 'core', flips(CORES, 1))  25.5 us
    ppermute x3, starting transfers between devices, wider(): lax.ppermute(inputs, axis, flips(size, flip))  15.7 us
    ppermute x3, waiting for transfers between devices, wider(): lax.ppermute(inputs, axis, flips(size, flip))  15 us
    ppermute x4, starting transfers between devices, over_x(): return lax.ppermute(array, 'x', flips(X, flip))  9.45 us
    pallas_call x2, Pallas kernels, partials(): pl.pallas_call(lambda *refs: partial_kernel(len(pieces), *refs), out_shap...  8.93 us
    all_gather x1, blocking collectives, on_device(): both = lax.all_gather(masked, 'core', axis=0)  8.66 us
    pallas_call x1, Pallas kernels, weight_grad(): pl.pallas_call(weight_grad_kernel, out_shape=jax.ShapeDtypeStruct((featur...  8.26 us
    all_to_all x1, starting transfers between devices, on_device(): received = lax.all_to_all(coded, ('far', 'near'), 0, 0)  7.02 us
  transfers between devices with their start and end apart: 16, of which 9 were waited for; matrix products, arithmetic and copies ran while one was open for 2% of the time, Pallas kernels for 9%

profile of v4, /device:TPU:1, one launch (start us, length us, event | category | flops | bytes accessed | tf_op | source)
XLA Modules:
  0.0 137.1 jit_solution(10354972084221813469)
XLA Ops:
  1.3 1.0 broadcast_select_fusion
  2.3 8.7 %all-gather = bf16[128,1856]{1,0:T(8,128)(2,1)S(1)} all-gather(bf16[64,1856]{1,0:T(8,128)(2,1)S(1)} %broadcast_select_fusion), channel_id=2, replica_groups=mesh['x'=4,'core'=2,'row'=4,'far'=2,'near'=8] {'core'}, dimensions={0}, use_global_device_ids=true | all-gather | bytes 712704 | tf_op jit(solution)/shard_map/all_gather | solution.py:189
  11.0 1.1 broadcast_in_dim.24
  12.1 3.6 %all-to-all-start = ((bf16[4,2,32,1856]{3,2,1,0:T(8,128)(2,1)}), bf16[4,2,32,1856]{3,2,1,0:T(8,128)(2,1)S(1)}, u32[]{:S(2)}, u32[]{:S(2)}) async-start(bf16[4,2,32,1856]{3,2,1,0:T(8,128)(2,1)} %broadcast_in_dim.24), calls=%async_computation | async-start | bytes 1966080 | tf_op jit(solution)/shard_map/all_to_all | solution.py:192
  15.7 5.5 %collective-permute-start = (bf16[1,232,128]{2,1,0:T(8,128)(2,1)S(1)}, bf16[1,232,128]{2,1,0:T(8,128)(2,1)S(1)}, u32[]{:S(2)}, u32[]{:S(2)}) collective-permute-start(bf16[1,232,128]{2,1,0:T(8,128)(2,1)S(1)} %bitcast.58), channel_id=1, source_target_pairs={{0,4},{1,5},{2,6},{3,7},{4,0},{5,1},{6,2},{7,3},{8,12},{9,13},{10,... | collective-permute-start | bytes 178184 | tf_op jit(solution)/shard_map/ppermute | solution.py:185
  21.3 3.4 %collective-permute-done = bf16[1,232,128]{2,1,0:T(8,128)(2,1)S(1)} collective-permute-done((bf16[1,232,128]{2,1,0:T(8,128)(2,1)S(1)}, bf16[1,232,128]{2,1,0:T(8,128)(2,1)S(1)}, u32[]{:S(2)}, u32[]{:S(2)}) %collective-permute-start) | collective-permute-done | bytes 59424 | tf_op jit(solution)/shard_map/ppermute | solution.py:185
  24.7 2.3 %collective-permute-start.1 = (bf16[2,232,128]{2,1,0:T(8,128)(2,1)S(1)}, bf16[2,232,128]{2,1,0:T(8,128)(2,1)S(1)}, u32[]{:S(2)}, u32[]{:S(2)}) collective-permute-start(bf16[2,232,128]{2,1,0:T(8,128)(2,1)S(1)} %pad_maximum_fusion.4), channel_id=1, source_target_pairs={{0,2},{1,3},{2,0},{3,1},{4,6},{5,7},{6,4},{7,5},{8,10},{9,11},{10,... | collective-permute-start | bytes 356360 | tf_op jit(solution)/shard_map/ppermute | solution.py:185
  26.9 6.4 %collective-permute-done.1 = bf16[2,232,128]{2,1,0:T(8,128)(2,1)S(1)} collective-permute-done((bf16[2,232,128]{2,1,0:T(8,128)(2,1)S(1)}, bf16[2,232,128]{2,1,0:T(8,128)(2,1)S(1)}, u32[]{:S(2)}, u32[]{:S(2)}) %collective-permute-start.1) | collective-permute-done | bytes 118816 | tf_op jit(solution)/shard_map/ppermute | solution.py:185
  33.4 6.4 %all-to-all-done = bf16[4,2,32,1856]{3,2,1,0:T(8,128)(2,1)S(1)} async-done(((bf16[4,2,32,1856]{3,2,1,0:T(8,128)(2,1)}), bf16[4,2,32,1856]{3,2,1,0:T(8,128)(2,1)S(1)}, u32[]{:S(2)}, u32[]{:S(2)}) %all-to-all-start) | async-done | bytes 950304 | tf_op jit(solution)/shard_map/all_to_all | solution.py:192
  39.9 2.3 %collective-permute-start.4 = (bf16[2,2,32,1856]{3,2,1,0:T(8,128)(2,1)S(1)}, bf16[2,2,32,1856]{3,2,1,0:T(8,128)(2,1)S(1)}, u32[]{:S(2)}, u32[]{:S(2)}) collective-permute-start(bf16[2,2,32,1856]{3,2,1,0:T(8,128)(2,1)S(1)} %get-tuple-element.18), channel_id=1, source_target_pairs={{0,384},{128,256},{256,128},{384,0},{1,385},{129,257},{257,129},{3... | collective-permute-start | bytes 1425416 | tf_op jit(solution)/shard_map/ppermute | solution.py:182
  42.2 7.9 %collective-permute-start.5 = (bf16[4,232,128]{2,1,0:T(8,128)(2,1)S(1)}, bf16[4,232,128]{2,1,0:T(8,128)(2,1)S(1)}, u32[]{:S(2)}, u32[]{:S(2)}) collective-permute-start(bf16[4,232,128]{2,1,0:T(8,128)(2,1)S(1)} %pad_maximum_fusion.3), channel_id=1, source_target_pairs={{0,8},{8,0},{1,9},{9,1},{2,10},{10,2},{3,11},{11,3},{4,12},{12,4},... | collective-permute-start | bytes 712712 | tf_op jit(solution)/shard_map/ppermute | solution.py:185
  50.1 1.9 %collective-permute-start.2 = (bf16[2,2,32,1856]{3,2,1,0:T(8,128)(2,1)S(1)}, bf16[2,2,32,1856]{3,2,1,0:T(8,128)(2,1)S(1)}, u32[]{:S(2)}, u32[]{:S(2)}) collective-permute-start(bf16[2,2,32,1856]{3,2,1,0:T(8,128)(2,1)S(1)} %get-tuple-element.19), channel_id=1, source_target_pairs={{0,128},{128,0},{256,384},{384,256},{1,129},{129,1},{257,385},{385... | collective-permute-start | bytes 1425416 | tf_op jit(solution)/shard_map/ppermute | solution.py:182
  52.0 5.3 %collective-permute-done.5 = bf16[4,232,128]{2,1,0:T(8,128)(2,1)S(1)} collective-permute-done((bf16[4,232,128]{2,1,0:T(8,128)(2,1)S(1)}, bf16[4,232,128]{2,1,0:T(8,128)(2,1)S(1)}, u32[]{:S(2)}, u32[]{:S(2)}) %collective-permute-start.5) | collective-permute-done | bytes 237600 | tf_op jit(solution)/shard_map/ppermute | solution.py:185
  57.5 1.9 %collective-permute-start.6 = (bf16[4,2,32,1856]{3,2,1,0:T(8,128)(2,1)S(1)}, bf16[4,2,32,1856]{3,2,1,0:T(8,128)(2,1)S(1)}, u32[]{:S(2)}, u32[]{:S(2)}) collective-permute-start(bf16[4,2,32,1856]{3,2,1,0:T(8,128)(2,1)S(1)} %pad_maximum_fusion.1.refs_2_.refs_1_), channel_id=1, source_target_pairs={{0,128},{128,0},{256,384},{384,256},{1,129},{129,1},{257,385},{385... | collective-permute-start | bytes 2850824 | tf_op jit(solution)/shard_map/ppermute | solution.py:182
  59.4 3.3 %collective-permute-done.2 = bf16[2,2,32,1856]{3,2,1,0:T(8,128)(2,1)S(1)} collective-permute-done((bf16[2,2,32,1856]{3,2,1,0:T(8,128)(2,1)S(1)}, bf16[2,2,32,1856]{3,2,1,0:T(8,128)(2,1)S(1)}, u32[]{:S(2)}, u32[]{:S(2)}) %collective-permute-start.2) | collective-permute-done | bytes 475168 | tf_op jit(solution)/shard_map/ppermute | solution.py:182
  62.9 3.3 %collective-permute-start.3 = (bf16[4,2,32,1856]{3,2,1,0:T(8,128)(2,1)S(1)}, bf16[4,2,32,1856]{3,2,1,0:T(8,128)(2,1)}, u32[]{:S(2)}, u32[]{:S(2)}) collective-permute-start(bf16[4,2,32,1856]{3,2,1,0:T(8,128)(2,1)S(1)} %pad_maximum_fusion.refs_1_.refs_0_), channel_id=1, source_target_pairs={{0,384},{128,256},{256,128},{384,0},{1,385},{129,257},{257,129},{3... | collective-permute-start | bytes 2850824 | tf_op jit(solution)/shard_map/ppermute | solution.py:182
  66.2 5.9 %collective-permute-start.8 = (bf16[232,1856]{1,0:T(8,128)(2,1)}, bf16[232,1856]{1,0:T(8,128)(2,1)}, u32[]{:S(2)}, u32[]{:S(2)}) collective-permute-start(bf16[232,1856]{1,0:T(8,128)(2,1)} %refs_5_.1), channel_id=1, source_target_pairs={{0,64},{64,0},{1,65},{65,1},{2,66},{66,2},{3,67},{67,3},{4,68},{68... | collective-permute-start | bytes 2583560 | tf_op jit(solution)/shard_map/ppermute | solution.py:179
  72.1 3.7 %collective-permute-start.7 = (bf16[8,232,128]{2,1,0:T(8,128)(2,1)S(1)}, bf16[8,232,128]{2,1,0:T(8,128)(2,1)}, u32[]{:S(2)}, u32[]{:S(2)}) collective-permute-start(bf16[8,232,128]{2,1,0:T(8,128)(2,1)S(1)} %pad_maximum_fusion.2.inputs), channel_id=1, source_target_pairs={{0,1},{1,0},{2,3},{3,2},{4,5},{5,4},{6,7},{7,6},{8,9},{9,8},{10,11... | collective-permute-start | bytes 1425416 | tf_op jit(solution)/shard_map/ppermute | solution.py:203
  77.0 4.5 %shard_map.59.refs_4_ = bf16[16,2,64,256]{3,2,1,0:T(8,128)(2,1)} custom-call(s32[8]{0:T(128)} %stack.181.refs_0_, bf16[4,2,32,1856]{3,2,1,0:T(8,128)(2,1)} %copy-done.4, bf16[4,2,32,1856]{3,2,1,0:T(8,128)(2,1)} %copy-done.2, bf16[232,1856]{1,0:T(8,128)(2,1)} %refs_5_.1, bf16[232,1856]{1,0:T(8,128)(2,1)} %collective-permute-done.8.refs_4_.refs_6_), custom_call_target="tpu_custom_call" | custom-call | flops 881852416 | bytes 1900544 | tf_op jit(solution)/shard_map/pallas_call | solution.py:65
  81.5 5.6 %collective-permute-done.7.refs_3_.more = bf16[8,232,128]{2,1,0:T(8,128)(2,1)} collective-permute-done((bf16[8,232,128]{2,1,0:T(8,128)(2,1)S(1)}, bf16[8,232,128]{2,1,0:T(8,128)(2,1)}, u32[]{:S(2)}, u32[]{:S(2)}) %collective-permute-start.7) | collective-permute-done | bytes 475168 | tf_op jit(solution)/shard_map/ppermute | solution.py:203
  88.1 4.5 %shard_map.60 = bf16[16,2,64,256]{3,2,1,0:T(8,128)(2,1)} custom-call(s32[8]{0:T(128)} %stack.172.refs_0_, bf16[4,2,32,1856]{3,2,1,0:T(8,128)(2,1)} %collective-permute-done.3.refs_1_.refs_2_, bf16[4,2,32,1856]{3,2,1,0:T(8,128)(2,1)} %copy-done.6, bf16[8,232,128]{2,1,0:T(8,128)(2,1)} %collective-permute-done.7.refs_3_.more, ...), custom_call_target="tpu_custom_call", output_to_operand_aliasing={{}: (4, {})} | custom-call | flops 881852416 | bytes 1900544 | tf_op jit(solution)/shard_map/pallas_call | solution.py:65
  92.5 7.0 %all-to-all-start.1 = ((bf16[16,2,64,256]{3,2,1,0:T(8,128)(2,1)}), bf16[16,2,64,256]{3,2,1,0:T(8,128)(2,1)S(1)}, u32[]{:S(2)}, u32[]{:S(2)}) async-start(bf16[16,2,64,256]{3,2,1,0:T(8,128)(2,1)} %shard_map.60), calls=%async_computation.1 | async-start | bytes 2097152 | tf_op jit(solution)/shard_map/all_to_all | solution.py:215
  99.6 5.4 %collective-permute-start.10 = (bf16[4,2,32,1856]{3,2,1,0:T(8,128)(2,1)S(1)}, bf16[4,2,32,1856]{3,2,1,0:T(8,128)(2,1)}, u32[]{:S(2)}, u32[]{:S(2)}) collective-permute-start(bf16[4,2,32,1856]{3,2,1,0:T(8,128)(2,1)S(1)} %copy-done.3), channel_id=1, source_target_pairs={{0,64},{64,0},{1,65},{65,1},{2,66},{66,2},{3,67},{67,3},{4,68},{68... | collective-permute-start | bytes 2850824 | tf_op jit(solution)/shard_map/ppermute | solution.py:179
  105.0 1.9 %collective-permute-start.9 = (bf16[4,2,32,1856]{3,2,1,0:T(8,128)(2,1)S(1)}, bf16[4,2,32,1856]{3,2,1,0:T(8,128)(2,1)}, u32[]{:S(2)}, u32[]{:S(2)}) collective-permute-start(bf16[4,2,32,1856]{3,2,1,0:T(8,128)(2,1)S(1)} %copy-done.5), channel_id=1, source_target_pairs={{0,64},{64,0},{1,65},{65,1},{2,66},{66,2},{3,67},{67,3},{4,68},{68... | collective-permute-start | bytes 2850824 | tf_op jit(solution)/shard_map/ppermute | solution.py:179
  106.9 2.4 %collective-permute-start.12 = (bf16[4,2,32,1856]{3,2,1,0:T(8,128)(2,1)}, bf16[4,2,32,1856]{3,2,1,0:T(8,128)(2,1)}, u32[]{:S(2)}, u32[]{:S(2)}) collective-permute-start(bf16[4,2,32,1856]{3,2,1,0:T(8,128)(2,1)} %copy-done.6), channel_id=1, source_target_pairs={{0,64},{64,0},{1,65},{65,1},{2,66},{66,2},{3,67},{67,3},{4,68},{68... | collective-permute-start | bytes 2850824 | tf_op jit(solution)/shard_map/ppermute | solution.py:179
  109.3 1.9 %collective-permute-start.11 = (bf16[4,2,32,1856]{3,2,1,0:T(8,128)(2,1)}, bf16[4,2,32,1856]{3,2,1,0:T(8,128)(2,1)}, u32[]{:S(2)}, u32[]{:S(2)}) collective-permute-start(bf16[4,2,32,1856]{3,2,1,0:T(8,128)(2,1)} %collective-permute-done.3.refs_1_.refs_2_), channel_id=1, source_target_pairs={{0,64},{64,0},{1,65},{65,1},{2,66},{66,2},{3,67},{67,3},{4,68},{68... | collective-permute-start | bytes 2850824 | tf_op jit(solution)/shard_map/ppermute | solution.py:179
  112.6 1.5 %collective-permute-done.11.refs_6_ = bf16[4,2,32,1856]{3,2,1,0:T(8,128)(2,1)} collective-permute-done((bf16[4,2,32,1856]{3,2,1,0:T(8,128)(2,1)}, bf16[4,2,32,1856]{3,2,1,0:T(8,128)(2,1)}, u32[]{:S(2)}, u32[]{:S(2)}) %collective-permute-start.11) | collective-permute-done | bytes 950304 | tf_op jit(solution)/shard_map/ppermute | solution.py:179
  114.1 8.3 %shard_map.61.after = bf16[232,1856]{1,0:T(8,128)(2,1)} custom-call(s32[2]{0:T(128)} %pad_add_fusion.place_ref, s32[32]{0:T(128)} %stack.214.where_ref, bf16[8,232,128]{2,1,0:T(8,128)(2,1)} %copy-done.7, bf16[8,232,128]{2,1,0:T(8,128)(2,1)} %collective-permute-done.7.refs_3_.more, bf16[4,2,32,1856]{3,2,1,0:T(8,128)(2,1)} %copy-done.4, ...), custom_call_target="tpu_custom_call" | custom-call | flops 1763704832 | bytes 7602176 | tf_op jit(solution)/shard_map/pallas_call | solution.py:111
  122.4 2.5 %all-to-all-done.1.received = bf16[16,2,64,256]{3,2,1,0:T(8,128)(2,1)S(1)} async-done(((bf16[16,2,64,256]{3,2,1,0:T(8,128)(2,1)}), bf16[16,2,64,256]{3,2,1,0:T(8,128)(2,1)S(1)}, u32[]{:S(2)}, u32[]{:S(2)}) %all-to-all-start.1) | async-done | bytes 1048608 | tf_op jit(solution)/shard_map/all_to_all | solution.py:215
  124.9 1.2 copy-done
  127.0 7.9 %collective-permute-start.13 = (f32[64,232]{1,0:T(8,128)S(1)}, f32[64,232]{1,0:T(8,128)S(1)}, u32[]{:S(2)}, u32[]{:S(2)}) collective-permute-start(f32[64,232]{1,0:T(8,128)S(1)} %get-tuple-element.17), channel_id=1, source_target_pairs={{0,64},{64,0},{1,65},{65,1},{2,66},{66,2},{3,67},{67,3},{4,68},{68... | collective-permute-start | bytes 178184 | tf_op jit(solution)/shard_map/ppermute | solution.py:179
  135.8 1.3 shard_map.63
  (38 shorter events, 5.7 us)
Async XLA Ops:
  12.1 3.7 %copy-start.8 = (bf16[128,232]{0,1:T(8,128)(2,1)S(1)}, bf16[128,232]{0,1:T(8,128)(2,1)}, u32[]{:S(2)}) copy-start(bf16[128,232]{0,1:T(8,128)(2,1)} %param.4) | copy-start | bytes 178180
  12.1 27.7 %all-to-all-start = ((bf16[4,2,32,1856]{3,2,1,0:T(8,128)(2,1)}), bf16[4,2,32,1856]{3,2,1,0:T(8,128)(2,1)S(1)}, u32[]{:S(2)}, u32[]{:S(2)}) async-start(bf16[4,2,32,1856]{3,2,1,0:T(8,128)(2,1)} %broadcast_in_dim.24), calls=%async_computation | async-start | bytes 1966080 | tf_op jit(solution)/shard_map/all_to_all | solution.py:192
  15.7 8.9 %collective-permute-start = (bf16[1,232,128]{2,1,0:T(8,128)(2,1)S(1)}, bf16[1,232,128]{2,1,0:T(8,128)(2,1)S(1)}, u32[]{:S(2)}, u32[]{:S(2)}) collective-permute-start(bf16[1,232,128]{2,1,0:T(8,128)(2,1)S(1)} %bitcast.58), channel_id=1, source_target_pairs={{0,4},{1,5},{2,6},{3,7},{4,0},{5,1},{6,2},{7,3},{8,12},{9,13},{10,... | collective-permute-start | bytes 178184 | tf_op jit(solution)/shard_map/ppermute | solution.py:185
  24.7 8.7 %collective-permute-start.1 = (bf16[2,232,128]{2,1,0:T(8,128)(2,1)S(1)}, bf16[2,232,128]{2,1,0:T(8,128)(2,1)S(1)}, u32[]{:S(2)}, u32[]{:S(2)}) collective-permute-start(bf16[2,232,128]{2,1,0:T(8,128)(2,1)S(1)} %pad_maximum_fusion.4), channel_id=1, source_target_pairs={{0,2},{1,3},{2,0},{3,1},{4,6},{5,7},{6,4},{7,5},{8,10},{9,11},{10,... | collective-permute-start | bytes 356360 | tf_op jit(solution)/shard_map/ppermute | solution.py:185
  39.9 17.5 %collective-permute-start.4 = (bf16[2,2,32,1856]{3,2,1,0:T(8,128)(2,1)S(1)}, bf16[2,2,32,1856]{3,2,1,0:T(8,128)(2,1)S(1)}, u32[]{:S(2)}, u32[]{:S(2)}) collective-permute-start(bf16[2,2,32,1856]{3,2,1,0:T(8,128)(2,1)S(1)} %get-tuple-element.18), channel_id=1, source_target_pairs={{0,384},{128,256},{256,128},{384,0},{1,385},{129,257},{257,129},{3... | collective-permute-start | bytes 1425416 | tf_op jit(solution)/shard_map/ppermute | solution.py:182
  42.2 15.2 %collective-permute-start.5 = (bf16[4,232,128]{2,1,0:T(8,128)(2,1)S(1)}, bf16[4,232,128]{2,1,0:T(8,128)(2,1)S(1)}, u32[]{:S(2)}, u32[]{:S(2)}) collective-permute-start(bf16[4,232,128]{2,1,0:T(8,128)(2,1)S(1)} %pad_maximum_fusion.3), channel_id=1, source_target_pairs={{0,8},{8,0},{1,9},{9,1},{2,10},{10,2},{3,11},{11,3},{4,12},{12,4},... | collective-permute-start | bytes 712712 | tf_op jit(solution)/shard_map/ppermute | solution.py:185
  50.1 12.6 %collective-permute-start.2 = (bf16[2,2,32,1856]{3,2,1,0:T(8,128)(2,1)S(1)}, bf16[2,2,32,1856]{3,2,1,0:T(8,128)(2,1)S(1)}, u32[]{:S(2)}, u32[]{:S(2)}) collective-permute-start(bf16[2,2,32,1856]{3,2,1,0:T(8,128)(2,1)S(1)} %get-tuple-element.19), channel_id=1, source_target_pairs={{0,128},{128,0},{256,384},{384,256},{1,129},{129,1},{257,385},{385... | collective-permute-start | bytes 1425416 | tf_op jit(solution)/shard_map/ppermute | solution.py:182
  57.4 14.7 %copy-start.7 = (bf16[8,232,128]{2,1,0:T(8,128)(2,1)}, bf16[8,232,128]{2,1,0:T(8,128)(2,1)S(1)}, u32[]{:S(2)}) copy-start(bf16[8,232,128]{2,1,0:T(8,128)(2,1)S(1)} %pad_maximum_fusion.2.inputs) | copy-start | bytes 1425412
  57.5 18.3 %copy-start.2 = (bf16[4,2,32,1856]{3,2,1,0:T(8,128)(2,1)}, bf16[4,2,32,1856]{3,2,1,0:T(8,128)(2,1)S(1)}, u32[]{:S(2)}) copy-start(bf16[4,2,32,1856]{3,2,1,0:T(8,128)(2,1)S(1)} %pad_maximum_fusion.1.refs_2_.refs_1_) | copy-start | bytes 2850820
  57.5 29.6 %collective-permute-start.6 = (bf16[4,2,32,1856]{3,2,1,0:T(8,128)(2,1)S(1)}, bf16[4,2,32,1856]{3,2,1,0:T(8,128)(2,1)S(1)}, u32[]{:S(2)}, u32[]{:S(2)}) collective-permute-start(bf16[4,2,32,1856]{3,2,1,0:T(8,128)(2,1)S(1)} %pad_maximum_fusion.1.refs_2_.refs_1_), channel_id=1, source_target_pairs={{0,128},{128,0},{256,384},{384,256},{1,129},{129,1},{257,385},{385... | collective-permute-start | bytes 2850824 | tf_op jit(solution)/shard_map/ppermute | solution.py:182
  62.9 14.2 %copy-start.4 = (bf16[4,2,32,1856]{3,2,1,0:T(8,128)(2,1)}, bf16[4,2,32,1856]{3,2,1,0:T(8,128)(2,1)S(1)}, u32[]{:S(2)}) copy-start(bf16[4,2,32,1856]{3,2,1,0:T(8,128)(2,1)S(1)} %pad_maximum_fusion.refs_1_.refs_0_) | copy-start | bytes 2850820
  62.9 24.2 %collective-permute-start.3 = (bf16[4,2,32,1856]{3,2,1,0:T(8,128)(2,1)S(1)}, bf16[4,2,32,1856]{3,2,1,0:T(8,128)(2,1)}, u32[]{:S(2)}, u32[]{:S(2)}) collective-permute-start(bf16[4,2,32,1856]{3,2,1,0:T(8,128)(2,1)S(1)} %pad_maximum_fusion.refs_1_.refs_0_), channel_id=1, source_target_pairs={{0,384},{128,256},{256,128},{384,0},{1,385},{129,257},{257,129},{3... | collective-permute-start | bytes 2850824 | tf_op jit(solution)/shard_map/ppermute | solution.py:182
  66.2 10.8 %collective-permute-start.8 = (bf16[232,1856]{1,0:T(8,128)(2,1)}, bf16[232,1856]{1,0:T(8,128)(2,1)}, u32[]{:S(2)}, u32[]{:S(2)}) collective-permute-start(bf16[232,1856]{1,0:T(8,128)(2,1)} %refs_5_.1), channel_id=1, source_target_pairs={{0,64},{64,0},{1,65},{65,1},{2,66},{66,2},{3,67},{67,3},{4,68},{68... | collective-permute-start | bytes 2583560 | tf_op jit(solution)/shard_map/ppermute | solution.py:179
  72.1 15.0 %collective-permute-start.7 = (bf16[8,232,128]{2,1,0:T(8,128)(2,1)S(1)}, bf16[8,232,128]{2,1,0:T(8,128)(2,1)}, u32[]{:S(2)}, u32[]{:S(2)}) collective-permute-start(bf16[8,232,128]{2,1,0:T(8,128)(2,1)S(1)} %pad_maximum_fusion.2.inputs), channel_id=1, source_target_pairs={{0,1},{1,0},{2,3},{3,2},{4,5},{5,4},{6,7},{7,6},{8,9},{9,8},{10,11... | collective-permute-start | bytes 1425416 | tf_op jit(solution)/shard_map/ppermute | solution.py:203
  87.1 0.9 copy-start.6
  92.5 7.1 %copy-start.3 = (bf16[4,2,32,1856]{3,2,1,0:T(8,128)(2,1)S(1)}, bf16[4,2,32,1856]{3,2,1,0:T(8,128)(2,1)}, u32[]{:S(2)}) copy-start(bf16[4,2,32,1856]{3,2,1,0:T(8,128)(2,1)} %copy-done.2) | copy-start | bytes 2850820
  92.5 12.5 %copy-start.5 = (bf16[4,2,32,1856]{3,2,1,0:T(8,128)(2,1)S(1)}, bf16[4,2,32,1856]{3,2,1,0:T(8,128)(2,1)}, u32[]{:S(2)}) copy-start(bf16[4,2,32,1856]{3,2,1,0:T(8,128)(2,1)} %copy-done.4) | copy-start | bytes 2850820
  92.5 32.4 %all-to-all-start.1 = ((bf16[16,2,64,256]{3,2,1,0:T(8,128)(2,1)}), bf16[16,2,64,256]{3,2,1,0:T(8,128)(2,1)S(1)}, u32[]{:S(2)}, u32[]{:S(2)}) async-start(bf16[16,2,64,256]{3,2,1,0:T(8,128)(2,1)} %shard_map.60), calls=%async_computation.1 | async-start | bytes 2097152 | tf_op jit(solution)/shard_map/all_to_all | solution.py:215
  99.6 13.0 %collective-permute-start.10 = (bf16[4,2,32,1856]{3,2,1,0:T(8,128)(2,1)S(1)}, bf16[4,2,32,1856]{3,2,1,0:T(8,128)(2,1)}, u32[]{:S(2)}, u32[]{:S(2)}) collective-permute-start(bf16[4,2,32,1856]{3,2,1,0:T(8,128)(2,1)S(1)} %copy-done.3), channel_id=1, source_target_pairs={{0,64},{64,0},{1,65},{65,1},{2,66},{66,2},{3,67},{67,3},{4,68},{68... | collective-permute-start | bytes 2850824 | tf_op jit(solution)/shard_map/ppermute | solution.py:179
  105.0 7.6 %collective-permute-start.9 = (bf16[4,2,32,1856]{3,2,1,0:T(8,128)(2,1)S(1)}, bf16[4,2,32,1856]{3,2,1,0:T(8,128)(2,1)}, u32[]{:S(2)}, u32[]{:S(2)}) collective-permute-start(bf16[4,2,32,1856]{3,2,1,0:T(8,128)(2,1)S(1)} %copy-done.5), channel_id=1, source_target_pairs={{0,64},{64,0},{1,65},{65,1},{2,66},{66,2},{3,67},{67,3},{4,68},{68... | collective-permute-start | bytes 2850824 | tf_op jit(solution)/shard_map/ppermute | solution.py:179
  106.9 5.7 %collective-permute-start.12 = (bf16[4,2,32,1856]{3,2,1,0:T(8,128)(2,1)}, bf16[4,2,32,1856]{3,2,1,0:T(8,128)(2,1)}, u32[]{:S(2)}, u32[]{:S(2)}) collective-permute-start(bf16[4,2,32,1856]{3,2,1,0:T(8,128)(2,1)} %copy-done.6), channel_id=1, source_target_pairs={{0,64},{64,0},{1,65},{65,1},{2,66},{66,2},{3,67},{67,3},{4,68},{68... | collective-permute-start | bytes 2850824 | tf_op jit(solution)/shard_map/ppermute | solution.py:179
  109.3 4.8 %collective-permute-start.11 = (bf16[4,2,32,1856]{3,2,1,0:T(8,128)(2,1)}, bf16[4,2,32,1856]{3,2,1,0:T(8,128)(2,1)}, u32[]{:S(2)}, u32[]{:S(2)}) collective-permute-start(bf16[4,2,32,1856]{3,2,1,0:T(8,128)(2,1)} %collective-permute-done.3.refs_1_.refs_2_), channel_id=1, source_target_pairs={{0,64},{64,0},{1,65},{65,1},{2,66},{66,2},{3,67},{67,3},{4,68},{68... | collective-permute-start | bytes 2850824 | tf_op jit(solution)/shard_map/ppermute | solution.py:179
  124.9 1.2 copy-start
  127.0 8.8 %copy-start.1 = (s32[2]{0:T(128)S(1)}, s32[2]{0:T(128)}, u32[]{:S(2)}) copy-start(s32[2]{0:T(128)} %pad_add_fusion.place_ref) | copy-start | bytes 28
  127.0 8.8 %collective-permute-start.13 = (f32[64,232]{1,0:T(8,128)S(1)}, f32[64,232]{1,0:T(8,128)S(1)}, u32[]{:S(2)}, u32[]{:S(2)}) collective-permute-start(f32[64,232]{1,0:T(8,128)S(1)} %get-tuple-element.17), channel_id=1, source_target_pairs={{0,64},{64,0},{1,65},{65,1},{2,66},{66,2},{3,67},{67,3},{4,68},{68... | collective-permute-start | bytes 178184 | tf_op jit(solution)/shard_map/ppermute | solution.py:179

commit v5 on v4

--- a/solution.py
+++ b/solution.py
@@ -50,8 +50,12 @@
                 owner, slot = n * 4 + m // 4 * 2 + m % 2, m // 2 % 2
                 sums[owner, i, slot * live:(slot + 1) * live] = coded[m * live:(m + 1) * live]
         for owner in range(n * 4, n * 4 + 4):
-            copies.append(pltpu.make_async_copy(sums.at[owner], out.at[where_ref[owner]], sems.at[owner]))
-            copies[-1].start()
+            for u in range(2):
+                slot = pl.multiple_of((where_ref[4 * count] ^ u) * live, live)
+                copies.append(pltpu.make_async_copy(
+                    sums.at[owner, :, pl.ds(u * live, live)],
+                    out.at[where_ref[owner], :, pl.ds(slot, live)], sems.at[len(copies)]))
+                copies[-1].start()
     for copy in copies:
         copy.wait()
 
@@ -70,7 +74,7 @@
         input_output_aliases={} if earlier is None else {len(pieces) + len(after): 0},
         scratch_shapes=[
             pltpu.VMEM((4 * len(pieces),) + coded.shape[1:], coded.dtype),
-            pltpu.SemaphoreType.DMA((4 * len(pieces),))],
+            pltpu.SemaphoreType.DMA((8 * len(pieces),))],
         compiler_params=LARGE,
         cost_estimate=pl.CostEstimate(
             flops=4 * rows * hidden * features, bytes_accessed=2 * rows * hidden, transcendentals=0),
@@ -189,31 +193,33 @@
     both = lax.all_gather(masked, "core", axis=0)
     both = lax.dynamic_slice_in_dim(both, core * live, live, 1)
     both, inputs = lax.optimization_barrier((both, activations.T[None]))
-    line = lax.all_to_all(jnp.broadcast_to(both[None], (ROWS,) + both.shape), "row", 0, 0)
+    rows = [both] + [lax.ppermute(both, "row", flips(ROWS, flip)) for flip in (1, 2, 3)]
     inputs = wider(wider(inputs, "near", NEAR, 4), "near", NEAR, 2)
-    line, inputs = lax.optimization_barrier((line, inputs))
 
     other_weight = swap(weight)
-    low, high = line[:ROWS // 2], line[ROWS // 2:]
+    low, high = jnp.stack(rows[:2]), jnp.stack(rows[2:])
     low = jnp.concatenate([low, over_x(low, 1)], 0)
     high = jnp.concatenate([high, over_x(high, 3)], 0)
+    low, inputs = lax.optimization_barrier((low, inputs))
     inputs = [wider(inputs, "far", FAR, 1)]
     high, inputs[0] = lax.optimization_barrier((high, inputs[0]))
     far_low, far_high = over_x(low, 3), over_x(high, 1)
     inputs.append(lax.ppermute(inputs[0], "near", flips(NEAR, 1)))
 
     x_1, x_2, x_3 = x ^ 1, x ^ 2, x ^ 3
+    row = lax.axis_index("row")
     pieces = [low, high, far_low, far_high]
-    origins = [((x, x_1), 0), ((x, x_3), 1), ((x_3, x_2), 0), ((x_1, x_2), 1)]
-    owners = [(x_of * CORES + c) * 2 + pair for x_pair, pair in origins for x_of in x_pair for c in range(CORES)]
-    bins = [(x_of * CORES + c) * ROWS + pair * 2 + r
-            for x_pair, pair in origins for x_of in x_pair for r in range(2) for c in range(CORES)]
-    owners, bins = (jnp.stack(table).astype(jnp.int32) for table in (owners, bins))
-
-    coded = partials(pieces[:2], owners[:8], weight, other_weight, [], None)
-    coded = partials(pieces[2:], owners[8:], weight, other_weight, inputs[1:], coded)
+    origins = [((x, x_1), 0), ((x, x_3), 2), ((x_3, x_2), 0), ((x_1, x_2), 2)]
+    owners = [(x_of * CORES + c) * 2 + (row ^ flip) // 2
+              for x_pair, flip in origins for x_of in x_pair for c in range(CORES)]
+    bins = [(x_of * CORES + c) * ROWS + (row ^ flip ^ u)
+            for x_pair, flip in origins for x_of in x_pair for u in range(2) for c in range(CORES)]
+    tables = [jnp.stack(table).astype(jnp.int32) for table in (owners[:8] + [row % 2], owners[8:] + [row % 2], bins)]
+
+    coded = partials(pieces[:2], tables[0], weight, other_weight, [], None)
+    coded = partials(pieces[2:], tables[1], weight, other_weight, inputs[1:], coded)
     received = lax.all_to_all(coded, ("far", "near"), 0, 0)
-    d_weight = weight_grad(place, bins, inputs, pieces + [swap(piece) for piece in pieces])
+    d_weight = weight_grad(place, tables[2], inputs, pieces + [swap(piece) for piece in pieces])
 
     keep, send = add_up(received, features, d_weight)
     d_input = merge(place, keep, swap(send))

time: 138 us -> 135 us (0.978)
  the two profiles are of different devices: /device:TPU:1 before, /device:TPU:73 now
where the time goes in v5:
time: 135 us; the launch traced here: 134 us
  starting transfers between devices  71.8 us (53%)
  waiting for transfers between devices  33.7 us (25%)
  Pallas kernels  19.5 us (14%)
  local copies, waits for them, and re-layouts  3.07 us (2%)
  blocking collectives  2.46 us (2%)
  other arithmetic  2.18 us (2%)
  between operations  1.76 us (1%)
    ppermute x6, starting transfers between devices, swap(): return lax.ppermute(array, 'core', flips(CORES, 1))  18.6 us
    ppermute x3, starting transfers between devices, wider(): lax.ppermute(inputs, axis, flips(size, flip))  17.8 us
    ppermute x4, starting transfers between devices, over_x(): return lax.ppermute(array, 'x', flips(X, flip))  12.7 us
    all_to_all x1, starting transfers between devices, on_device(): received = lax.all_to_all(coded, ('far', 'near'), 0, 0)  10.6 us
    ppermute x3, starting transfers between devices, on_device(): lax.ppermute(both, 'row', flips(ROWS, flip))  9.92 us
    pallas_call x2, Pallas kernels, partials(): pl.pallas_call(lambda *refs: partial_kernel(len(pieces), *refs), out_shap...  9.08 us
    pallas_call x1, Pallas kernels, weight_grad(): pl.pallas_call(weight_grad_kernel, out_shape=jax.ShapeDtypeStruct((featur...  8.26 us
    ppermute x3, waiting for transfers between devices, wider(): lax.ppermute(inputs, axis, flips(size, flip))  7.68 us
  transfers between devices with their start and end apart: 18, of which 8 were waited for; matrix products, arithmetic and copies ran while one was open for 2% of the time, Pallas kernels for 10%

profile of v5, /device:TPU:73, one launch (start us, length us, event | category | flops | bytes accessed | tf_op | source)
XLA Modules:
  0.0 134.5 jit_solution(632594070797255974)
XLA Ops:
  1.3 1.0 broadcast_select_fusion
  2.3 2.5 %all-gather = bf16[128,1856]{1,0:T(8,128)(2,1)S(1)} all-gather(bf16[64,1856]{1,0:T(8,128)(2,1)S(1)} %broadcast_select_fusion), channel_id=2, replica_groups=mesh['x'=4,'core'=2,'row'=4,'far'=2,'near'=8] {'core'}, dimensions={0}, use_global_device_ids=true | all-gather | bytes 712704 | tf_op jit(solution)/shard_map/all_gather | solution.py:193
  4.8 1.9 %collective-permute-start = (bf16[2,32,1856]{2,1,0:T(8,128)(2,1)S(1)}, bf16[2,32,1856]{2,1,0:T(8,128)(2,1)S(1)}, u32[]{:S(2)}, u32[]{:S(2)}) collective-permute-start(bf16[2,32,1856]{2,1,0:T(8,128)(2,1)S(1)} %constant_dynamic-slice_fusion), channel_id=1, source_target_pairs={{0,16},{16,0},{32,48},{48,32},{1,17},{17,1},{33,49},{49,33},{2,18}... | collective-permute-start | bytes 712712 | tf_op jit(solution)/shard_map/ppermute | solution.py:196
  6.8 5.8 %collective-permute-start.5 = (bf16[2,32,1856]{2,1,0:T(8,128)(2,1)S(1)}, bf16[2,32,1856]{2,1,0:T(8,128)(2,1)S(1)}, u32[]{:S(2)}, u32[]{:S(2)}) collective-permute-start(bf16[2,32,1856]{2,1,0:T(8,128)(2,1)S(1)} %constant_dynamic-slice_fusion), channel_id=1, source_target_pairs={{0,32},{16,48},{32,0},{48,16},{1,33},{17,49},{33,1},{49,17},{2,34}... | collective-permute-start | bytes 712712 | tf_op jit(solution)/shard_map/ppermute | solution.py:196
  12.6 2.2 %collective-permute-start.6 = (bf16[2,32,1856]{2,1,0:T(8,128)(2,1)S(1)}, bf16[2,32,1856]{2,1,0:T(8,128)(2,1)S(1)}, u32[]{:S(2)}, u32[]{:S(2)}) collective-permute-start(bf16[2,32,1856]{2,1,0:T(8,128)(2,1)S(1)} %constant_dynamic-slice_fusion), channel_id=1, source_target_pairs={{0,48},{16,32},{32,16},{48,0},{1,49},{17,33},{33,17},{49,1},{2,50}... | collective-permute-start | bytes 712712 | tf_op jit(solution)/shard_map/ppermute | solution.py:196
  14.8 6.6 %collective-permute-start.2 = (bf16[1,232,128]{2,1,0:T(8,128)(2,1)S(1)}, bf16[1,232,128]{2,1,0:T(8,128)(2,1)S(1)}, u32[]{:S(2)}, u32[]{:S(2)}) collective-permute-start(bf16[1,232,128]{2,1,0:T(8,128)(2,1)S(1)} %bitcast.71), channel_id=1, source_target_pairs={{0,4},{1,5},{2,6},{3,7},{4,0},{5,1},{6,2},{7,3},{8,12},{9,13},{10,... | collective-permute-start | bytes 178184 | tf_op jit(solution)/shard_map/ppermute | solution.py:189
  21.4 3.1 %collective-permute-start.1 = (bf16[2,2,32,1856]{3,2,1,0:T(8,128)(2,1)S(1)}, bf16[2,2,32,1856]{3,2,1,0:T(8,128)(2,1)S(1)}, u32[]{:S(2)}, u32[]{:S(2)}) collective-permute-start(bf16[2,2,32,1856]{3,2,1,0:T(8,128)(2,1)S(1)} %pad_maximum_fusion.2), channel_id=1, source_target_pairs={{0,128},{128,0},{256,384},{384,256},{1,129},{129,1},{257,385},{385... | collective-permute-start | bytes 1425416 | tf_op jit(solution)/shard_map/ppermute | solution.py:186
  24.6 3.3 %collective-permute-start.3 = (bf16[2,232,128]{2,1,0:T(8,128)(2,1)S(1)}, bf16[2,232,128]{2,1,0:T(8,128)(2,1)S(1)}, u32[]{:S(2)}, u32[]{:S(2)}) collective-permute-start(bf16[2,232,128]{2,1,0:T(8,128)(2,1)S(1)} %pad_maximum_fusion.6), channel_id=1, source_target_pairs={{0,2},{1,3},{2,0},{3,1},{4,6},{5,7},{6,4},{7,5},{8,10},{9,11},{10,... | collective-permute-start | bytes 356360 | tf_op jit(solution)/shard_map/ppermute | solution.py:189
  28.1 6.2 %collective-permute-done.6 = bf16[2,32,1856]{2,1,0:T(8,128)(2,1)S(1)} collective-permute-done((bf16[2,32,1856]{2,1,0:T(8,128)(2,1)S(1)}, bf16[2,32,1856]{2,1,0:T(8,128)(2,1)S(1)}, u32[]{:S(2)}, u32[]{:S(2)}) %collective-permute-start.6) | collective-permute-done | bytes 237600 | tf_op jit(solution)/shard_map/ppermute | solution.py:196
  34.4 4.4 %collective-permute-start.7 = (bf16[2,2,32,1856]{3,2,1,0:T(8,128)(2,1)S(1)}, bf16[2,2,32,1856]{3,2,1,0:T(8,128)(2,1)S(1)}, u32[]{:S(2)}, u32[]{:S(2)}) collective-permute-start(bf16[2,2,32,1856]{3,2,1,0:T(8,128)(2,1)S(1)} %pad_maximum_fusion.3), channel_id=1, source_target_pairs={{0,384},{128,256},{256,128},{384,0},{1,385},{129,257},{257,129},{3... | collective-permute-start | bytes 1425416 | tf_op jit(solution)/shard_map/ppermute | solution.py:186
  39.0 8.0 %collective-permute-start.8 = (bf16[4,232,128]{2,1,0:T(8,128)(2,1)S(1)}, bf16[4,232,128]{2,1,0:T(8,128)(2,1)S(1)}, u32[]{:S(2)}, u32[]{:S(2)}) collective-permute-start(bf16[4,232,128]{2,1,0:T(8,128)(2,1)S(1)} %pad_maximum_fusion.5), channel_id=1, source_target_pairs={{0,8},{8,0},{1,9},{9,1},{2,10},{10,2},{3,11},{11,3},{4,12},{12,4},... | collective-permute-start | bytes 712712 | tf_op jit(solution)/shard_map/ppermute | solution.py:189
  47.0 2.1 %collective-permute-start.4 = (bf16[4,2,32,1856]{3,2,1,0:T(8,128)(2,1)S(1)}, bf16[4,2,32,1856]{3,2,1,0:T(8,128)(2,1)S(1)}, u32[]{:S(2)}, u32[]{:S(2)}) collective-permute-start(bf16[4,2,32,1856]{3,2,1,0:T(8,128)(2,1)S(1)} %pad_maximum_fusion.refs_1_.refs_0_), channel_id=1, source_target_pairs={{0,384},{128,256},{256,128},{384,0},{1,385},{129,257},{257,129},{3... | collective-permute-start | bytes 2850824 | tf_op jit(solution)/shard_map/ppermute | solution.py:186
  49.2 7.7 %collective-permute-done.8 = bf16[4,232,128]{2,1,0:T(8,128)(2,1)S(1)} collective-permute-done((bf16[4,232,128]{2,1,0:T(8,128)(2,1)S(1)}, bf16[4,232,128]{2,1,0:T(8,128)(2,1)S(1)}, u32[]{:S(2)}, u32[]{:S(2)}) %collective-permute-start.8) | collective-permute-done | bytes 237600 | tf_op jit(solution)/shard_map/ppermute | solution.py:189
  57.0 3.1 %collective-permute-start.9 = (bf16[4,2,32,1856]{3,2,1,0:T(8,128)(2,1)S(1)}, bf16[4,2,32,1856]{3,2,1,0:T(8,128)(2,1)}, u32[]{:S(2)}, u32[]{:S(2)}) collective-permute-start(bf16[4,2,32,1856]{3,2,1,0:T(8,128)(2,1)S(1)} %pad_maximum_fusion.1.refs_2_.refs_1_), channel_id=1, source_target_pairs={{0,128},{128,0},{256,384},{384,256},{1,129},{129,1},{257,385},{385... | collective-permute-start | bytes 2850824 | tf_op jit(solution)/shard_map/ppermute | solution.py:186
  60.1 2.8 %collective-permute-start.11 = (bf16[232,1856]{1,0:T(8,128)(2,1)}, bf16[232,1856]{1,0:T(8,128)(2,1)}, u32[]{:S(2)}, u32[]{:S(2)}) collective-permute-start(bf16[232,1856]{1,0:T(8,128)(2,1)} %refs_5_.1), channel_id=1, source_target_pairs={{0,64},{64,0},{1,65},{65,1},{2,66},{66,2},{3,67},{67,3},{4,68},{68... | collective-permute-start | bytes 2583560 | tf_op jit(solution)/shard_map/ppermute | solution.py:183
  62.9 2.2 %collective-permute-start.10 = (bf16[8,232,128]{2,1,0:T(8,128)(2,1)S(1)}, bf16[8,232,128]{2,1,0:T(8,128)(2,1)}, u32[]{:S(2)}, u32[]{:S(2)}) collective-permute-start(bf16[8,232,128]{2,1,0:T(8,128)(2,1)S(1)} %pad_maximum_fusion.4.inputs), channel_id=1, source_target_pairs={{0,1},{1,0},{2,3},{3,2},{4,5},{5,4},{6,7},{7,6},{8,9},{9,8},{10,11... | collective-permute-start | bytes 1425416 | tf_op jit(solution)/shard_map/ppermute | solution.py:207
  66.4 4.6 %shard_map.59.refs_4_ = bf16[16,2,64,256]{3,2,1,0:T(8,128)(2,1)} custom-call(s32[9]{0:T(128)} %stack.211.refs_0_, bf16[4,2,32,1856]{3,2,1,0:T(8,128)(2,1)} %copy-done.2, bf16[4,2,32,1856]{3,2,1,0:T(8,128)(2,1)} %copy-done.4, bf16[232,1856]{1,0:T(8,128)(2,1)} %refs_5_.1, bf16[232,1856]{1,0:T(8,128)(2,1)} %collective-permute-done.11.refs_4_.refs_6_), custom_call_target="tpu_custom_call" | custom-call | flops 881852416 | bytes 1900544 | tf_op jit(solution)/shard_map/pallas_call | solution.py:69
  70.9 6.4 %collective-permute-done.10.refs_3_.more = bf16[8,232,128]{2,1,0:T(8,128)(2,1)} collective-permute-done((bf16[8,232,128]{2,1,0:T(8,128)(2,1)S(1)}, bf16[8,232,128]{2,1,0:T(8,128)(2,1)}, u32[]{:S(2)}, u32[]{:S(2)}) %collective-permute-start.10) | collective-permute-done | bytes 475168 | tf_op jit(solution)/shard_map/ppermute | solution.py:207
  77.4 4.3 %collective-permute-done.9.refs_2_.refs_3_ = bf16[4,2,32,1856]{3,2,1,0:T(8,128)(2,1)} collective-permute-done((bf16[4,2,32,1856]{3,2,1,0:T(8,128)(2,1)S(1)}, bf16[4,2,32,1856]{3,2,1,0:T(8,128)(2,1)}, u32[]{:S(2)}, u32[]{:S(2)}) %collective-permute-start.9) | collective-permute-done | bytes 950304 | tf_op jit(solution)/shard_map/ppermute | solution.py:186
  81.7 4.5 %shard_map.60 = bf16[16,2,64,256]{3,2,1,0:T(8,128)(2,1)} custom-call(s32[9]{0:T(128)} %stack.196.refs_0_, bf16[4,2,32,1856]{3,2,1,0:T(8,128)(2,1)} %copy-done.6, bf16[4,2,32,1856]{3,2,1,0:T(8,128)(2,1)} %collective-permute-done.9.refs_2_.refs_3_, bf16[8,232,128]{2,1,0:T(8,128)(2,1)} %collective-permute-done.10.refs_3_.more, ...), custom_call_target="tpu_custom_call", output_to_operand_aliasing={{}: (4, {})} | custom-call | flops 881852416 | bytes 1900544 | tf_op jit(solution)/shard_map/pallas_call | solution.py:69
  86.2 10.6 %all-to-all-start = ((bf16[16,2,64,256]{3,2,1,0:T(8,128)(2,1)}), bf16[16,2,64,256]{3,2,1,0:T(8,128)(2,1)S(1)}, u32[]{:S(2)}, u32[]{:S(2)}) async-start(bf16[16,2,64,256]{3,2,1,0:T(8,128)(2,1)} %shard_map.60), calls=%async_computation | async-start | bytes 2097152 | tf_op jit(solution)/shard_map/all_to_all | solution.py:221
  96.8 3.9 %collective-permute-start.12 = (bf16[4,2,32,1856]{3,2,1,0:T(8,128)(2,1)S(1)}, bf16[4,2,32,1856]{3,2,1,0:T(8,128)(2,1)}, u32[]{:S(2)}, u32[]{:S(2)}) collective-permute-start(bf16[4,2,32,1856]{3,2,1,0:T(8,128)(2,1)S(1)} %copy-done.3), channel_id=1, source_target_pairs={{0,64},{64,0},{1,65},{65,1},{2,66},{66,2},{3,67},{67,3},{4,68},{68... | collective-permute-start | bytes 2850824 | tf_op jit(solution)/shard_map/ppermute | solution.py:183
  100.7 1.9 %collective-permute-start.13 = (bf16[4,2,32,1856]{3,2,1,0:T(8,128)(2,1)S(1)}, bf16[4,2,32,1856]{3,2,1,0:T(8,128)(2,1)}, u32[]{:S(2)}, u32[]{:S(2)}) collective-permute-start(bf16[4,2,32,1856]{3,2,1,0:T(8,128)(2,1)S(1)} %copy-done.5), channel_id=1, source_target_pairs={{0,64},{64,0},{1,65},{65,1},{2,66},{66,2},{3,67},{67,3},{4,68},{68... | collective-permute-start | bytes 2850824 | tf_op jit(solution)/shard_map/ppermute | solution.py:183
  102.6 2.4 %collective-permute-start.14 = (bf16[4,2,32,1856]{3,2,1,0:T(8,128)(2,1)}, bf16[4,2,32,1856]{3,2,1,0:T(8,128)(2,1)}, u32[]{:S(2)}, u32[]{:S(2)}) collective-permute-start(bf16[4,2,32,1856]{3,2,1,0:T(8,128)(2,1)} %copy-done.6), channel_id=1, source_target_pairs={{0,64},{64,0},{1,65},{65,1},{2,66},{66,2},{3,67},{67,3},{4,68},{68... | collective-permute-start | bytes 2850824 | tf_op jit(solution)/shard_map/ppermute | solution.py:183
  105.0 1.9 %collective-permute-start.15 = (bf16[4,2,32,1856]{3,2,1,0:T(8,128)(2,1)}, bf16[4,2,32,1856]{3,2,1,0:T(8,128)(2,1)}, u32[]{:S(2)}, u32[]{:S(2)}) collective-permute-start(bf16[4,2,32,1856]{3,2,1,0:T(8,128)(2,1)} %collective-permute-done.9.refs_2_.refs_3_), channel_id=1, source_target_pairs={{0,64},{64,0},{1,65},{65,1},{2,66},{66,2},{3,67},{67,3},{4,68},{68... | collective-permute-start | bytes 2850824 | tf_op jit(solution)/shard_map/ppermute | solution.py:183
  108.4 1.5 %collective-permute-done.15.refs_7_ = bf16[4,2,32,1856]{3,2,1,0:T(8,128)(2,1)} collective-permute-done((bf16[4,2,32,1856]{3,2,1,0:T(8,128)(2,1)}, bf16[4,2,32,1856]{3,2,1,0:T(8,128)(2,1)}, u32[]{:S(2)}, u32[]{:S(2)}) %collective-permute-start.15) | collective-permute-done | bytes 950304 | tf_op jit(solution)/shard_map/ppermute | solution.py:183
  109.9 8.3 %shard_map.61.after = bf16[232,1856]{1,0:T(8,128)(2,1)} custom-call(s32[2]{0:T(128)} %pad_add_fusion.place_ref, s32[32]{0:T(128)} %stack.244.where_ref, bf16[8,232,128]{2,1,0:T(8,128)(2,1)} %copy-done.7, bf16[8,232,128]{2,1,0:T(8,128)(2,1)} %collective-permute-done.10.refs_3_.more, bf16[4,2,32,1856]{3,2,1,0:T(8,128)(2,1)} %copy-done.2, ...), custom_call_target="tpu_custom_call" | custom-call | flops 1763704832 | bytes 7602176 | tf_op jit(solution)/shard_map/pallas_call | solution.py:115
  118.1 6.4 %all-to-all-done.received = bf16[16,2,64,256]{3,2,1,0:T(8,128)(2,1)S(1)} async-done(((bf16[16,2,64,256]{3,2,1,0:T(8,128)(2,1)}), bf16[16,2,64,256]{3,2,1,0:T(8,128)(2,1)S(1)}, u32[]{:S(2)}, u32[]{:S(2)}) %all-to-all-start) | async-done | bytes 1048608 | tf_op jit(solution)/shard_map/all_to_all | solution.py:221
  124.5 1.2 copy-done
  125.7 0.9 shard_map.62
  126.6 5.7 %collective-permute-start.16 = (f32[64,232]{1,0:T(8,128)S(1)}, f32[64,232]{1,0:T(8,128)S(1)}, u32[]{:S(2)}, u32[]{:S(2)}) collective-permute-start(f32[64,232]{1,0:T(8,128)S(1)} %get-tuple-element.17), channel_id=1, source_target_pairs={{0,64},{64,0},{1,65},{65,1},{2,66},{66,2},{3,67},{67,3},{4,68},{68... | collective-permute-start | bytes 178184 | tf_op jit(solution)/shard_map/ppermute | solution.py:183
  133.2 1.3 shard_map.63
  (42 shorter events, 4.2 us)
Async XLA Ops:
  4.8 10.0 %copy-start.8 = (bf16[128,232]{0,1:T(8,128)(2,1)S(1)}, bf16[128,232]{0,1:T(8,128)(2,1)}, u32[]{:S(2)}) copy-start(bf16[128,232]{0,1:T(8,128)(2,1)} %param.4) | copy-start | bytes 178180
  4.8 16.5 %collective-permute-start = (bf16[2,32,1856]{2,1,0:T(8,128)(2,1)S(1)}, bf16[2,32,1856]{2,1,0:T(8,128)(2,1)S(1)}, u32[]{:S(2)}, u32[]{:S(2)}) collective-permute-start(bf16[2,32,1856]{2,1,0:T(8,128)(2,1)S(1)} %constant_dynamic-slice_fusion), channel_id=1, source_target_pairs={{0,16},{16,0},{32,48},{48,32},{1,17},{17,1},{33,49},{49,33},{2,18}... | collective-permute-start | bytes 712712 | tf_op jit(solution)/shard_map/ppermute | solution.py:196
  6.8 21.3 %collective-permute-start.5 = (bf16[2,32,1856]{2,1,0:T(8,128)(2,1)S(1)}, bf16[2,32,1856]{2,1,0:T(8,128)(2,1)S(1)}, u32[]{:S(2)}, u32[]{:S(2)}) collective-permute-start(bf16[2,32,1856]{2,1,0:T(8,128)(2,1)S(1)} %constant_dynamic-slice_fusion), channel_id=1, source_target_pairs={{0,32},{16,48},{32,0},{48,16},{1,33},{17,49},{33,1},{49,17},{2,34}... | collective-permute-start | bytes 712712 | tf_op jit(solution)/shard_map/ppermute | solution.py:196
  12.6 21.8 %collective-permute-start.6 = (bf16[2,32,1856]{2,1,0:T(8,128)(2,1)S(1)}, bf16[2,32,1856]{2,1,0:T(8,128)(2,1)S(1)}, u32[]{:S(2)}, u32[]{:S(2)}) collective-permute-start(bf16[2,32,1856]{2,1,0:T(8,128)(2,1)S(1)} %constant_dynamic-slice_fusion), channel_id=1, source_target_pairs={{0,48},{16,32},{32,16},{48,0},{1,49},{17,33},{33,17},{49,1},{2,50}... | collective-permute-start | bytes 712712 | tf_op jit(solution)/shard_map/ppermute | solution.py:196
  14.8 9.8 %collective-permute-start.2 = (bf16[1,232,128]{2,1,0:T(8,128)(2,1)S(1)}, bf16[1,232,128]{2,1,0:T(8,128)(2,1)S(1)}, u32[]{:S(2)}, u32[]{:S(2)}) collective-permute-start(bf16[1,232,128]{2,1,0:T(8,128)(2,1)S(1)} %bitcast.71), channel_id=1, source_target_pairs={{0,4},{1,5},{2,6},{3,7},{4,0},{5,1},{6,2},{7,3},{8,12},{9,13},{10,... | collective-permute-start | bytes 178184 | tf_op jit(solution)/shard_map/ppermute | solution.py:189
  21.4 17.4 %collective-permute-start.1 = (bf16[2,2,32,1856]{3,2,1,0:T(8,128)(2,1)S(1)}, bf16[2,2,32,1856]{3,2,1,0:T(8,128)(2,1)S(1)}, u32[]{:S(2)}, u32[]{:S(2)}) collective-permute-start(bf16[2,2,32,1856]{3,2,1,0:T(8,128)(2,1)S(1)} %pad_maximum_fusion.2), channel_id=1, source_target_pairs={{0,128},{128,0},{256,384},{384,256},{1,129},{129,1},{257,385},{385... | collective-permute-start | bytes 1425416 | tf_op jit(solution)/shard_map/ppermute | solution.py:186
  24.6 14.2 %collective-permute-start.3 = (bf16[2,232,128]{2,1,0:T(8,128)(2,1)S(1)}, bf16[2,232,128]{2,1,0:T(8,128)(2,1)S(1)}, u32[]{:S(2)}, u32[]{:S(2)}) collective-permute-start(bf16[2,232,128]{2,1,0:T(8,128)(2,1)S(1)} %pad_maximum_fusion.6), channel_id=1, source_target_pairs={{0,2},{1,3},{2,0},{3,1},{4,6},{5,7},{6,4},{7,5},{8,10},{9,11},{10,... | collective-permute-start | bytes 356360 | tf_op jit(solution)/shard_map/ppermute | solution.py:189
  34.4 14.7 %collective-permute-start.7 = (bf16[2,2,32,1856]{3,2,1,0:T(8,128)(2,1)S(1)}, bf16[2,2,32,1856]{3,2,1,0:T(8,128)(2,1)S(1)}, u32[]{:S(2)}, u32[]{:S(2)}) collective-permute-start(bf16[2,2,32,1856]{3,2,1,0:T(8,128)(2,1)S(1)} %pad_maximum_fusion.3), channel_id=1, source_target_pairs={{0,384},{128,256},{256,128},{384,0},{1,385},{129,257},{257,129},{3... | collective-permute-start | bytes 1425416 | tf_op jit(solution)/shard_map/ppermute | solution.py:186
  39.0 18.0 %copy-start.2 = (bf16[4,2,32,1856]{3,2,1,0:T(8,128)(2,1)}, bf16[4,2,32,1856]{3,2,1,0:T(8,128)(2,1)S(1)}, u32[]{:S(2)}) copy-start(bf16[4,2,32,1856]{3,2,1,0:T(8,128)(2,1)S(1)} %pad_maximum_fusion.refs_1_.refs_0_) | copy-start | bytes 2850820
  39.0 17.9 %collective-permute-start.8 = (bf16[4,232,128]{2,1,0:T(8,128)(2,1)S(1)}, bf16[4,232,128]{2,1,0:T(8,128)(2,1)S(1)}, u32[]{:S(2)}, u32[]{:S(2)}) collective-permute-start(bf16[4,232,128]{2,1,0:T(8,128)(2,1)S(1)} %pad_maximum_fusion.5), channel_id=1, source_target_pairs={{0,8},{8,0},{1,9},{9,1},{2,10},{10,2},{3,11},{11,3},{4,12},{12,4},... | collective-permute-start | bytes 712712 | tf_op jit(solution)/shard_map/ppermute | solution.py:189
  47.0 30.4 %collective-permute-start.4 = (bf16[4,2,32,1856]{3,2,1,0:T(8,128)(2,1)S(1)}, bf16[4,2,32,1856]{3,2,1,0:T(8,128)(2,1)S(1)}, u32[]{:S(2)}, u32[]{:S(2)}) collective-permute-start(bf16[4,2,32,1856]{3,2,1,0:T(8,128)(2,1)S(1)} %pad_maximum_fusion.refs_1_.refs_0_), channel_id=1, source_target_pairs={{0,384},{128,256},{256,128},{384,0},{1,385},{129,257},{257,129},{3... | collective-permute-start | bytes 2850824 | tf_op jit(solution)/shard_map/ppermute | solution.py:186
  49.2 17.2 %copy-start.4 = (bf16[4,2,32,1856]{3,2,1,0:T(8,128)(2,1)}, bf16[4,2,32,1856]{3,2,1,0:T(8,128)(2,1)S(1)}, u32[]{:S(2)}) copy-start(bf16[4,2,32,1856]{3,2,1,0:T(8,128)(2,1)S(1)} %pad_maximum_fusion.1.refs_2_.refs_1_) | copy-start | bytes 2850820
  57.0 14.0 %copy-start.7 = (bf16[8,232,128]{2,1,0:T(8,128)(2,1)}, bf16[8,232,128]{2,1,0:T(8,128)(2,1)S(1)}, u32[]{:S(2)}) copy-start(bf16[8,232,128]{2,1,0:T(8,128)(2,1)S(1)} %pad_maximum_fusion.4.inputs) | copy-start | bytes 1425412
  57.0 24.7 %collective-permute-start.9 = (bf16[4,2,32,1856]{3,2,1,0:T(8,128)(2,1)S(1)}, bf16[4,2,32,1856]{3,2,1,0:T(8,128)(2,1)}, u32[]{:S(2)}, u32[]{:S(2)}) collective-permute-start(bf16[4,2,32,1856]{3,2,1,0:T(8,128)(2,1)S(1)} %pad_maximum_fusion.1.refs_2_.refs_1_), channel_id=1, source_target_pairs={{0,128},{128,0},{256,384},{384,256},{1,129},{129,1},{257,385},{385... | collective-permute-start | bytes 2850824 | tf_op jit(solution)/shard_map/ppermute | solution.py:186
  60.1 6.3 %collective-permute-start.11 = (bf16[232,1856]{1,0:T(8,128)(2,1)}, bf16[232,1856]{1,0:T(8,128)(2,1)}, u32[]{:S(2)}, u32[]{:S(2)}) collective-permute-start(bf16[232,1856]{1,0:T(8,128)(2,1)} %refs_5_.1), channel_id=1, source_target_pairs={{0,64},{64,0},{1,65},{65,1},{2,66},{66,2},{3,67},{67,3},{4,68},{68... | collective-permute-start | bytes 2583560 | tf_op jit(solution)/shard_map/ppermute | solution.py:183
  62.9 14.5 %collective-permute-start.10 = (bf16[8,232,128]{2,1,0:T(8,128)(2,1)S(1)}, bf16[8,232,128]{2,1,0:T(8,128)(2,1)}, u32[]{:S(2)}, u32[]{:S(2)}) collective-permute-start(bf16[8,232,128]{2,1,0:T(8,128)(2,1)S(1)} %pad_maximum_fusion.4.inputs), channel_id=1, source_target_pairs={{0,1},{1,0},{2,3},{3,2},{4,5},{5,4},{6,7},{7,6},{8,9},{9,8},{10,11... | collective-permute-start | bytes 1425416 | tf_op jit(solution)/shard_map/ppermute | solution.py:207
  77.4 4.3 %copy-start.6 = (bf16[4,2,32,1856]{3,2,1,0:T(8,128)(2,1)}, bf16[4,2,32,1856]{3,2,1,0:T(8,128)(2,1)S(1)}, u32[]{:S(2)}) copy-start(bf16[4,2,32,1856]{3,2,1,0:T(8,128)(2,1)S(1)} %collective-permute-done.4.refs_1_.refs_2_) | copy-start | bytes 2850820
  86.2 10.6 %copy-start.3 = (bf16[4,2,32,1856]{3,2,1,0:T(8,128)(2,1)S(1)}, bf16[4,2,32,1856]{3,2,1,0:T(8,128)(2,1)}, u32[]{:S(2)}) copy-start(bf16[4,2,32,1856]{3,2,1,0:T(8,128)(2,1)} %copy-done.2) | copy-start | bytes 2850820
  86.2 14.5 %copy-start.5 = (bf16[4,2,32,1856]{3,2,1,0:T(8,128)(2,1)S(1)}, bf16[4,2,32,1856]{3,2,1,0:T(8,128)(2,1)}, u32[]{:S(2)}) copy-start(bf16[4,2,32,1856]{3,2,1,0:T(8,128)(2,1)} %copy-done.4) | copy-start | bytes 2850820
  86.2 38.3 %all-to-all-start = ((bf16[16,2,64,256]{3,2,1,0:T(8,128)(2,1)}), bf16[16,2,64,256]{3,2,1,0:T(8,128)(2,1)S(1)}, u32[]{:S(2)}, u32[]{:S(2)}) async-start(bf16[16,2,64,256]{3,2,1,0:T(8,128)(2,1)} %shard_map.60), calls=%async_computation | async-start | bytes 2097152 | tf_op jit(solution)/shard_map/all_to_all | solution.py:221
  96.8 11.5 %collective-permute-start.12 = (bf16[4,2,32,1856]{3,2,1,0:T(8,128)(2,1)S(1)}, bf16[4,2,32,1856]{3,2,1,0:T(8,128)(2,1)}, u32[]{:S(2)}, u32[]{:S(2)}) collective-permute-start(bf16[4,2,32,1856]{3,2,1,0:T(8,128)(2,1)S(1)} %copy-done.3), channel_id=1, source_target_pairs={{0,64},{64,0},{1,65},{65,1},{2,66},{66,2},{3,67},{67,3},{4,68},{68... | collective-permute-start | bytes 2850824 | tf_op jit(solution)/shard_map/ppermute | solution.py:183
  100.7 7.6 %collective-permute-start.13 = (bf16[4,2,32,1856]{3,2,1,0:T(8,128)(2,1)S(1)}, bf16[4,2,32,1856]{3,2,1,0:T(8,128)(2,1)}, u32[]{:S(2)}, u32[]{:S(2)}) collective-permute-start(bf16[4,2,32,1856]{3,2,1,0:T(8,128)(2,1)S(1)} %copy-done.5), channel_id=1, source_target_pairs={{0,64},{64,0},{1,65},{65,1},{2,66},{66,2},{3,67},{67,3},{4,68},{68... | collective-permute-start | bytes 2850824 | tf_op jit(solution)/shard_map/ppermute | solution.py:183
  102.6 5.7 %collective-permute-start.14 = (bf16[4,2,32,1856]{3,2,1,0:T(8,128)(2,1)}, bf16[4,2,32,1856]{3,2,1,0:T(8,128)(2,1)}, u32[]{:S(2)}, u32[]{:S(2)}) collective-permute-start(bf16[4,2,32,1856]{3,2,1,0:T(8,128)(2,1)} %copy-done.6), channel_id=1, source_target_pairs={{0,64},{64,0},{1,65},{65,1},{2,66},{66,2},{3,67},{67,3},{4,68},{68... | collective-permute-start | bytes 2850824 | tf_op jit(solution)/shard_map/ppermute | solution.py:183
  105.0 4.8 %collective-permute-start.15 = (bf16[4,2,32,1856]{3,2,1,0:T(8,128)(2,1)}, bf16[4,2,32,1856]{3,2,1,0:T(8,128)(2,1)}, u32[]{:S(2)}, u32[]{:S(2)}) collective-permute-start(bf16[4,2,32,1856]{3,2,1,0:T(8,128)(2,1)} %collective-permute-done.9.refs_2_.refs_3_), channel_id=1, source_target_pairs={{0,64},{64,0},{1,65},{65,1},{2,66},{66,2},{3,67},{67,3},{4,68},{68... | collective-permute-start | bytes 2850824 | tf_op jit(solution)/shard_map/ppermute | solution.py:183
  124.5 1.2 copy-start
  126.6 6.6 %copy-start.1 = (s32[2]{0:T(128)S(1)}, s32[2]{0:T(128)}, u32[]{:S(2)}) copy-start(s32[2]{0:T(128)} %pad_add_fusion.place_ref) | copy-start | bytes 28
  126.6 6.6 %collective-permute-start.16 = (f32[64,232]{1,0:T(8,128)S(1)}, f32[64,232]{1,0:T(8,128)S(1)}, u32[]{:S(2)}, u32[]{:S(2)}) collective-permute-start(f32[64,232]{1,0:T(8,128)S(1)} %get-tuple-element.17), channel_id=1, source_target_pairs={{0,64},{64,0},{1,65},{65,1},{2,66},{66,2},{3,67},{67,3},{4,68},{68... | collective-permute-start | bytes 178184 | tf_op jit(solution)/shard_map/ppermute | solution.py:183

commit v6 on v4

--- a/solution.py
+++ b/solution.py
@@ -38,19 +38,20 @@
 def partial_kernel(count, where_ref, *refs):
     pieces = refs[:count]
     own_ref, other_ref, out, sums, sems = refs[-5:]
-    lanes = sums.shape[-1]
     copies = []
     for n, piece in enumerate(pieces):
-        live, hidden = piece.shape[2:]
-        tokens = piece[...].reshape(8 * live, hidden)
+        places, cores, live, hidden = piece.shape
+        blocks = places * cores
+        tokens = piece[...].reshape(blocks * live, hidden)
         for i, ref in enumerate((own_ref, other_ref)):
             coded = coded_of(lax.dot_general(
-                tokens, ref[...], (((1,), (1,)), ((), ())), preferred_element_type=jnp.float32), lanes)
-            for m in range(8):
-                owner, slot = n * 4 + m // 4 * 2 + m % 2, m // 2 % 2
-                sums[owner, i, slot * live:(slot + 1) * live] = coded[m * live:(m + 1) * live]
-        for owner in range(n * 4, n * 4 + 4):
-            copies.append(pltpu.make_async_copy(sums.at[owner], out.at[where_ref[owner]], sems.at[owner]))
+                tokens, ref[...], (((1,), (1,)), ((), ())), preferred_element_type=jnp.float32), sums.shape[-1])
+            for m in range(blocks):
+                sums[n * blocks + m, i] = coded[m * live:(m + 1) * live]
+        for m in range(n * blocks, (n + 1) * blocks):
+            slot = pl.multiple_of(where_ref[m] % 2 * live, live)
+            copies.append(pltpu.make_async_copy(
+                sums.at[m], out.at[where_ref[m] // 2, :, pl.ds(slot, live)], sems.at[m]))
             copies[-1].start()
     for copy in copies:
         copy.wait()
@@ -69,8 +70,8 @@
         out_specs=ANY,
         input_output_aliases={} if earlier is None else {len(pieces) + len(after): 0},
         scratch_shapes=[
-            pltpu.VMEM((4 * len(pieces),) + coded.shape[1:], coded.dtype),
-            pltpu.SemaphoreType.DMA((4 * len(pieces),))],
+            pltpu.VMEM((8 * len(pieces), 2, coded.shape[2] // 2, lanes), coded.dtype),
+            pltpu.SemaphoreType.DMA((8 * len(pieces),))],
         compiler_params=LARGE,
         cost_estimate=pl.CostEstimate(
             flops=4 * rows * hidden * features, bytes_accessed=2 * rows * hidden, transcendentals=0),
@@ -189,29 +190,29 @@
     both = lax.all_gather(masked, "core", axis=0)
     both = lax.dynamic_slice_in_dim(both, core * live, live, 1)
     both, inputs = lax.optimization_barrier((both, activations.T[None]))
-    line = lax.all_to_all(jnp.broadcast_to(both[None], (ROWS,) + both.shape), "row", 0, 0)
+    rows = [both] + [lax.ppermute(both, "row", flips(ROWS, flip)) for flip in (2, 3, 1)]
     inputs = wider(wider(inputs, "near", NEAR, 4), "near", NEAR, 2)
-    line, inputs = lax.optimization_barrier((line, inputs))
 
     other_weight = swap(weight)
-    low, high = line[:ROWS // 2], line[ROWS // 2:]
+    low, high = jnp.stack(rows[:2]), jnp.stack(rows[2:])
     low = jnp.concatenate([low, over_x(low, 1)], 0)
     high = jnp.concatenate([high, over_x(high, 3)], 0)
+    low, inputs = lax.optimization_barrier((low, inputs))
     inputs = [wider(inputs, "far", FAR, 1)]
     high, inputs[0] = lax.optimization_barrier((high, inputs[0]))
     far_low, far_high = over_x(low, 3), over_x(high, 1)
     inputs.append(lax.ppermute(inputs[0], "near", flips(NEAR, 1)))
 
     x_1, x_2, x_3 = x ^ 1, x ^ 2, x ^ 3
+    row = lax.axis_index("row")
     pieces = [low, high, far_low, far_high]
-    origins = [((x, x_1), 0), ((x, x_3), 1), ((x_3, x_2), 0), ((x_1, x_2), 1)]
-    owners = [(x_of * CORES + c) * 2 + pair for x_pair, pair in origins for x_of in x_pair for c in range(CORES)]
-    bins = [(x_of * CORES + c) * ROWS + pair * 2 + r
-            for x_pair, pair in origins for x_of in x_pair for r in range(2) for c in range(CORES)]
-    owners, bins = (jnp.stack(table).astype(jnp.int32) for table in (owners, bins))
-
-    coded = partials(pieces[:2], owners[:8], weight, other_weight, [], None)
-    coded = partials(pieces[2:], owners[8:], weight, other_weight, inputs[1:], coded)
+    origins = [((x, x_1), (0, 2)), ((x, x_3), (3, 1)), ((x_3, x_2), (0, 2)), ((x_1, x_2), (3, 1))]
+    bins = jnp.stack([
+        (x_of * CORES + c) * ROWS + (row ^ flip)
+        for x_pair, pair in origins for x_of in x_pair for flip in pair for c in range(CORES)]).astype(jnp.int32)
+
+    coded = partials(pieces[:2], bins[:16], weight, other_weight, [], None)
+    coded = partials(pieces[2:], bins[16:], weight, other_weight, inputs[1:], coded)
     received = lax.all_to_all(coded, ("far", "near"), 0, 0)
     d_weight = weight_grad(place, bins, inputs, pieces + [swap(piece) for piece in pieces])
 

time: 138 us -> 135 us (0.978)
  local copies, waits for them, and re-layouts: 5.15 us -> 3.23 us
  waiting for transfers between devices: 35.2 us -> 33.5 us
    ppermute x0 -> x3, starting transfers between devices: none -> 8.37 us  [on_device(): lax.ppermute(both, 'row', flips(ROWS, flip))]
    all_to_all x1 -> x0, waiting for transfers between devices: 6.41 us -> none  [on_device(): lax.all_to_all(jnp.broadcast_to(both[None], (ROWS,) + both.shape), 'row',...]
    ppermute x0 -> x3, waiting for transfers between devices: none -> 5.4 us  [on_device(): lax.ppermute(both, 'row', flips(ROWS, flip))]
    all_to_all x1 -> x0, starting transfers between devices: 3.64 us -> none  [on_device(): lax.all_to_all(jnp.broadcast_to(both[None], (ROWS,) + both.shape), 'row',...]
    ppermute x3, waiting for transfers between devices: 15 us -> 11.7 us  [wider(): lax.ppermute(inputs, axis, flips(size, flip))]
    ppermute x4, starting transfers between devices: 9.45 us -> 12 us  [over_x(): return lax.ppermute(array, 'x', flips(X, flip))]
    all_to_all x1, starting transfers between devices: 7.02 us -> 4.6 us  [on_device(): received = lax.all_to_all(coded, ('far', 'near'), 0, 0)]
    ppermute x4, waiting for transfers between devices: 3.32 us -> 5.42 us  [over_x(): return lax.ppermute(array, 'x', flips(X, flip))]
  transfers between devices with their start and end apart: 16 -> 18, of which waited for: 9 -> 9; matrix products, arithmetic and copies ran while one was open for 2% -> 2% of each run, Pallas kernels for 9% -> 10%
where the time goes in v6:
time: 135 us; the launch traced here: 133 us
  starting transfers between devices  64.7 us (48%)
  waiting for transfers between devices  33.5 us (25%)
  Pallas kernels  19.5 us (14%)
  blocking collectives  8.66 us (6%)
  local copies, waits for them, and re-layouts  3.23 us (2%)
  other arithmetic  2.12 us (2%)
  between operations  1.7 us (1%)
    ppermute x6, starting transfers between devices, swap(): return lax.ppermute(array, 'core', flips(CORES, 1))  24.1 us
    ppermute x3, starting transfers between devices, wider(): lax.ppermute(inputs, axis, flips(size, flip))  13.7 us
    ppermute x4, starting transfers between devices, over_x(): return lax.ppermute(array, 'x', flips(X, flip))  12 us
    ppermute x3, waiting for transfers between devices, wider(): lax.ppermute(inputs, axis, flips(size, flip))  11.7 us
    pallas_call x2, Pallas kernels, partials(): pl.pallas_call(lambda *refs: partial_kernel(len(pieces), *refs), out_shap...  9.07 us
    all_gather x1, blocking collectives, on_device(): both = lax.all_gather(masked, 'core', axis=0)  8.66 us
    ppermute x3, starting transfers between devices, on_device(): lax.ppermute(both, 'row', flips(ROWS, flip))  8.37 us
    pallas_call x1, Pallas kernels, weight_grad(): pl.pallas_call(weight_grad_kernel, out_shape=jax.ShapeDtypeStruct((featur...  8.26 us
  transfers between devices with their start and end apart: 18, of which 9 were waited for; matrix products, arithmetic and copies ran while one was open for 2% of the time, Pallas kernels for 10%

profile of v6, /device:TPU:1, one launch (start us, length us, event | category | flops | bytes accessed | tf_op | source)
XLA Modules:
  0.0 133.4 jit_solution(3384962120006530255)
XLA Ops:
  2.3 8.7 %all-gather = bf16[128,1856]{1,0:T(8,128)(2,1)S(1)} all-gather(bf16[64,1856]{1,0:T(8,128)(2,1)S(1)} %broadcast_select_fusion), channel_id=2, replica_groups=mesh['x'=4,'core'=2,'row'=4,'far'=2,'near'=8] {'core'}, dimensions={0}, use_global_device_ids=true | all-gather | bytes 712704 | tf_op jit(solution)/shard_map/all_gather | solution.py:190
  11.0 1.9 %collective-permute-start = (bf16[2,32,1856]{2,1,0:T(8,128)(2,1)S(1)}, bf16[2,32,1856]{2,1,0:T(8,128)(2,1)S(1)}, u32[]{:S(2)}, u32[]{:S(2)}) collective-permute-start(bf16[2,32,1856]{2,1,0:T(8,128)(2,1)S(1)} %constant_dynamic-slice_fusion), channel_id=1, source_target_pairs={{0,32},{16,48},{32,0},{48,16},{1,33},{17,49},{33,1},{49,17},{2,34}... | collective-permute-start | bytes 712712 | tf_op jit(solution)/shard_map/ppermute | solution.py:193
  13.0 2.2 %collective-permute-start.5 = (bf16[2,32,1856]{2,1,0:T(8,128)(2,1)S(1)}, bf16[2,32,1856]{2,1,0:T(8,128)(2,1)S(1)}, u32[]{:S(2)}, u32[]{:S(2)}) collective-permute-start(bf16[2,32,1856]{2,1,0:T(8,128)(2,1)S(1)} %constant_dynamic-slice_fusion), channel_id=1, source_target_pairs={{0,48},{16,32},{32,16},{48,0},{1,49},{17,33},{33,17},{49,1},{2,50}... | collective-permute-start | bytes 712712 | tf_op jit(solution)/shard_map/ppermute | solution.py:193
  15.2 4.2 %collective-permute-start.6 = (bf16[2,32,1856]{2,1,0:T(8,128)(2,1)S(1)}, bf16[2,32,1856]{2,1,0:T(8,128)(2,1)S(1)}, u32[]{:S(2)}, u32[]{:S(2)}) collective-permute-start(bf16[2,32,1856]{2,1,0:T(8,128)(2,1)S(1)} %constant_dynamic-slice_fusion), channel_id=1, source_target_pairs={{0,16},{16,0},{32,48},{48,32},{1,17},{17,1},{33,49},{49,33},{2,18}... | collective-permute-start | bytes 712712 | tf_op jit(solution)/shard_map/ppermute | solution.py:193
  19.4 5.4 %collective-permute-start.2 = (bf16[1,232,128]{2,1,0:T(8,128)(2,1)S(1)}, bf16[1,232,128]{2,1,0:T(8,128)(2,1)S(1)}, u32[]{:S(2)}, u32[]{:S(2)}) collective-permute-start(bf16[1,232,128]{2,1,0:T(8,128)(2,1)S(1)} %bitcast.54), channel_id=1, source_target_pairs={{0,4},{1,5},{2,6},{3,7},{4,0},{5,1},{6,2},{7,3},{8,12},{9,13},{10,... | collective-permute-start | bytes 178184 | tf_op jit(solution)/shard_map/ppermute | solution.py:186
  24.9 5.4 %collective-permute-done = bf16[2,32,1856]{2,1,0:T(8,128)(2,1)S(1)} collective-permute-done((bf16[2,32,1856]{2,1,0:T(8,128)(2,1)S(1)}, bf16[2,32,1856]{2,1,0:T(8,128)(2,1)S(1)}, u32[]{:S(2)}, u32[]{:S(2)}) %collective-permute-start) | collective-permute-done | bytes 237600 | tf_op jit(solution)/shard_map/ppermute | solution.py:193
  30.3 1.9 %collective-permute-start.1 = (bf16[2,2,32,1856]{3,2,1,0:T(8,128)(2,1)S(1)}, bf16[2,2,32,1856]{3,2,1,0:T(8,128)(2,1)S(1)}, u32[]{:S(2)}, u32[]{:S(2)}) collective-permute-start(bf16[2,2,32,1856]{3,2,1,0:T(8,128)(2,1)S(1)} %pad_maximum_fusion.2), channel_id=1, source_target_pairs={{0,128},{128,0},{256,384},{384,256},{1,129},{129,1},{257,385},{385... | collective-permute-start | bytes 1425416 | tf_op jit(solution)/shard_map/ppermute | solution.py:183
  32.3 3.2 %collective-permute-start.3 = (bf16[2,232,128]{2,1,0:T(8,128)(2,1)S(1)}, bf16[2,232,128]{2,1,0:T(8,128)(2,1)S(1)}, u32[]{:S(2)}, u32[]{:S(2)}) collective-permute-start(bf16[2,232,128]{2,1,0:T(8,128)(2,1)S(1)} %pad_maximum_fusion.6), channel_id=1, source_target_pairs={{0,2},{1,3},{2,0},{3,1},{4,6},{5,7},{6,4},{7,5},{8,10},{9,11},{10,... | collective-permute-start | bytes 356360 | tf_op jit(solution)/shard_map/ppermute | solution.py:186
  35.6 3.7 %collective-permute-start.7 = (bf16[2,2,32,1856]{3,2,1,0:T(8,128)(2,1)S(1)}, bf16[2,2,32,1856]{3,2,1,0:T(8,128)(2,1)S(1)}, u32[]{:S(2)}, u32[]{:S(2)}) collective-permute-start(bf16[2,2,32,1856]{3,2,1,0:T(8,128)(2,1)S(1)} %pad_maximum_fusion.3), channel_id=1, source_target_pairs={{0,384},{128,256},{256,128},{384,0},{1,385},{129,257},{257,129},{3... | collective-permute-start | bytes 1425416 | tf_op jit(solution)/shard_map/ppermute | solution.py:183
  39.3 3.5 %collective-permute-done.3 = bf16[2,232,128]{2,1,0:T(8,128)(2,1)S(1)} collective-permute-done((bf16[2,232,128]{2,1,0:T(8,128)(2,1)S(1)}, bf16[2,232,128]{2,1,0:T(8,128)(2,1)S(1)}, u32[]{:S(2)}, u32[]{:S(2)}) %collective-permute-start.3) | collective-permute-done | bytes 118816 | tf_op jit(solution)/shard_map/ppermute | solution.py:186
  42.8 1.6 %collective-permute-done.1 = bf16[2,2,32,1856]{3,2,1,0:T(8,128)(2,1)S(1)} collective-permute-done((bf16[2,2,32,1856]{3,2,1,0:T(8,128)(2,1)S(1)}, bf16[2,2,32,1856]{3,2,1,0:T(8,128)(2,1)S(1)}, u32[]{:S(2)}, u32[]{:S(2)}) %collective-permute-start.1) | collective-permute-done | bytes 475168 | tf_op jit(solution)/shard_map/ppermute | solution.py:183
  44.6 5.0 %collective-permute-start.8 = (bf16[4,232,128]{2,1,0:T(8,128)(2,1)S(1)}, bf16[4,232,128]{2,1,0:T(8,128)(2,1)S(1)}, u32[]{:S(2)}, u32[]{:S(2)}) collective-permute-start(bf16[4,232,128]{2,1,0:T(8,128)(2,1)S(1)} %pad_maximum_fusion.5), channel_id=1, source_target_pairs={{0,8},{8,0},{1,9},{9,1},{2,10},{10,2},{3,11},{11,3},{4,12},{12,4},... | collective-permute-start | bytes 712712 | tf_op jit(solution)/shard_map/ppermute | solution.py:186
  49.6 4.4 %collective-permute-start.4 = (bf16[4,2,32,1856]{3,2,1,0:T(8,128)(2,1)S(1)}, bf16[4,2,32,1856]{3,2,1,0:T(8,128)(2,1)}, u32[]{:S(2)}, u32[]{:S(2)}) collective-permute-start(bf16[4,2,32,1856]{3,2,1,0:T(8,128)(2,1)S(1)} %pad_maximum_fusion.refs_1_.refs_0_), channel_id=1, source_target_pairs={{0,384},{128,256},{256,128},{384,0},{1,385},{129,257},{257,129},{3... | collective-permute-start | bytes 2850824 | tf_op jit(solution)/shard_map/ppermute | solution.py:183
  54.2 8.2 %collective-permute-done.8 = bf16[4,232,128]{2,1,0:T(8,128)(2,1)S(1)} collective-permute-done((bf16[4,232,128]{2,1,0:T(8,128)(2,1)S(1)}, bf16[4,232,128]{2,1,0:T(8,128)(2,1)S(1)}, u32[]{:S(2)}, u32[]{:S(2)}) %collective-permute-start.8) | collective-permute-done | bytes 237600 | tf_op jit(solution)/shard_map/ppermute | solution.py:186
  62.5 1.9 %collective-permute-start.9 = (bf16[4,2,32,1856]{3,2,1,0:T(8,128)(2,1)S(1)}, bf16[4,2,32,1856]{3,2,1,0:T(8,128)(2,1)}, u32[]{:S(2)}, u32[]{:S(2)}) collective-permute-start(bf16[4,2,32,1856]{3,2,1,0:T(8,128)(2,1)S(1)} %pad_maximum_fusion.1.refs_2_.refs_1_), channel_id=1, source_target_pairs={{0,128},{128,0},{256,384},{384,256},{1,129},{129,1},{257,385},{385... | collective-permute-start | bytes 2850824 | tf_op jit(solution)/shard_map/ppermute | solution.py:183
  64.4 3.7 %collective-permute-start.11 = (bf16[232,1856]{1,0:T(8,128)(2,1)S(1)}, bf16[232,1856]{1,0:T(8,128)(2,1)}, u32[]{:S(2)}, u32[]{:S(2)}) collective-permute-start(bf16[232,1856]{1,0:T(8,128)(2,1)S(1)} %copy-done.6), channel_id=1, source_target_pairs={{0,64},{64,0},{1,65},{65,1},{2,66},{66,2},{3,67},{67,3},{4,68},{68... | collective-permute-start | bytes 2583560 | tf_op jit(solution)/shard_map/ppermute | solution.py:180
  68.2 2.0 %collective-permute-start.10 = (bf16[8,232,128]{2,1,0:T(8,128)(2,1)S(1)}, bf16[8,232,128]{2,1,0:T(8,128)(2,1)}, u32[]{:S(2)}, u32[]{:S(2)}) collective-permute-start(bf16[8,232,128]{2,1,0:T(8,128)(2,1)S(1)} %pad_maximum_fusion.4.inputs), channel_id=1, source_target_pairs={{0,1},{1,0},{2,3},{3,2},{4,5},{5,4},{6,7},{7,6},{8,9},{9,8},{10,11... | collective-permute-start | bytes 1425416 | tf_op jit(solution)/shard_map/ppermute | solution.py:204
  71.5 4.5 %shard_map.59.refs_4_ = bf16[16,2,64,256]{3,2,1,0:T(8,128)(2,1)} custom-call(s32[16]{0:T(128)} %stack.174.refs_0_, bf16[4,2,32,1856]{3,2,1,0:T(8,128)(2,1)} %copy-done.2, bf16[4,2,32,1856]{3,2,1,0:T(8,128)(2,1)} %copy-done.4, bf16[232,1856]{1,0:T(8,128)(2,1)} %refs_5_.1, bf16[232,1856]{1,0:T(8,128)(2,1)} %collective-permute-done.11.refs_4_.refs_6_), custom_call_target="tpu_custom_call" | custom-call | flops 881852416 | bytes 1900544 | tf_op jit(solution)/shard_map/pallas_call | solution.py:66
  76.0 6.6 %collective-permute-done.10.refs_3_.more = bf16[8,232,128]{2,1,0:T(8,128)(2,1)} collective-permute-done((bf16[8,232,128]{2,1,0:T(8,128)(2,1)S(1)}, bf16[8,232,128]{2,1,0:T(8,128)(2,1)}, u32[]{:S(2)}, u32[]{:S(2)}) %collective-permute-start.10) | collective-permute-done | bytes 475168 | tf_op jit(solution)/shard_map/ppermute | solution.py:204
  82.7 3.8 %collective-permute-done.9.refs_2_.refs_3_ = bf16[4,2,32,1856]{3,2,1,0:T(8,128)(2,1)} collective-permute-done((bf16[4,2,32,1856]{3,2,1,0:T(8,128)(2,1)S(1)}, bf16[4,2,32,1856]{3,2,1,0:T(8,128)(2,1)}, u32[]{:S(2)}, u32[]{:S(2)}) %collective-permute-start.9) | collective-permute-done | bytes 950304 | tf_op jit(solution)/shard_map/ppermute | solution.py:183
  86.4 4.5 %shard_map.60 = bf16[16,2,64,256]{3,2,1,0:T(8,128)(2,1)} custom-call(s32[16]{0:T(128)} %stack.151.refs_0_, bf16[4,2,32,1856]{3,2,1,0:T(8,128)(2,1)} %collective-permute-done.4.refs_1_.refs_2_, bf16[4,2,32,1856]{3,2,1,0:T(8,128)(2,1)} %collective-permute-done.9.refs_2_.refs_3_, ...), custom_call_target="tpu_custom_call", output_to_operand_aliasing={{}: (4, {})} | custom-call | flops 881852416 | bytes 1900544 | tf_op jit(solution)/shard_map/pallas_call | solution.py:66
  91.0 4.6 %all-to-all-start = ((bf16[16,2,64,256]{3,2,1,0:T(8,128)(2,1)}), bf16[16,2,64,256]{3,2,1,0:T(8,128)(2,1)S(1)}, u32[]{:S(2)}, u32[]{:S(2)}) async-start(bf16[16,2,64,256]{3,2,1,0:T(8,128)(2,1)} %shard_map.60), calls=%async_computation | async-start | bytes 2097152 | tf_op jit(solution)/shard_map/all_to_all | solution.py:216
  95.6 5.6 %collective-permute-start.12 = (bf16[4,2,32,1856]{3,2,1,0:T(8,128)(2,1)S(1)}, bf16[4,2,32,1856]{3,2,1,0:T(8,128)(2,1)}, u32[]{:S(2)}, u32[]{:S(2)}) collective-permute-start(bf16[4,2,32,1856]{3,2,1,0:T(8,128)(2,1)S(1)} %copy-done.3), channel_id=1, source_target_pairs={{0,64},{64,0},{1,65},{65,1},{2,66},{66,2},{3,67},{67,3},{4,68},{68... | collective-permute-start | bytes 2850824 | tf_op jit(solution)/shard_map/ppermute | solution.py:180
  101.2 1.9 %collective-permute-start.13 = (bf16[4,2,32,1856]{3,2,1,0:T(8,128)(2,1)S(1)}, bf16[4,2,32,1856]{3,2,1,0:T(8,128)(2,1)}, u32[]{:S(2)}, u32[]{:S(2)}) collective-permute-start(bf16[4,2,32,1856]{3,2,1,0:T(8,128)(2,1)S(1)} %copy-done.5), channel_id=1, source_target_pairs={{0,64},{64,0},{1,65},{65,1},{2,66},{66,2},{3,67},{67,3},{4,68},{68... | collective-permute-start | bytes 2850824 | tf_op jit(solution)/shard_map/ppermute | solution.py:180
  103.2 2.4 %collective-permute-start.14 = (bf16[4,2,32,1856]{3,2,1,0:T(8,128)(2,1)}, bf16[4,2,32,1856]{3,2,1,0:T(8,128)(2,1)}, u32[]{:S(2)}, u32[]{:S(2)}) collective-permute-start(bf16[4,2,32,1856]{3,2,1,0:T(8,128)(2,1)} %collective-permute-done.4.refs_1_.refs_2_), channel_id=1, source_target_pairs={{0,64},{64,0},{1,65},{65,1},{2,66},{66,2},{3,67},{67,3},{4,68},{68... | collective-permute-start | bytes 2850824 | tf_op jit(solution)/shard_map/ppermute | solution.py:180
  105.6 1.9 %collective-permute-start.15 = (bf16[4,2,32,1856]{3,2,1,0:T(8,128)(2,1)}, bf16[4,2,32,1856]{3,2,1,0:T(8,128)(2,1)}, u32[]{:S(2)}, u32[]{:S(2)}) collective-permute-start(bf16[4,2,32,1856]{3,2,1,0:T(8,128)(2,1)} %collective-permute-done.9.refs_2_.refs_3_), channel_id=1, source_target_pairs={{0,64},{64,0},{1,65},{65,1},{2,66},{66,2},{3,67},{67,3},{4,68},{68... | collective-permute-start | bytes 2850824 | tf_op jit(solution)/shard_map/ppermute | solution.py:180
  108.9 1.5 %collective-permute-done.15.refs_7_ = bf16[4,2,32,1856]{3,2,1,0:T(8,128)(2,1)} collective-permute-done((bf16[4,2,32,1856]{3,2,1,0:T(8,128)(2,1)}, bf16[4,2,32,1856]{3,2,1,0:T(8,128)(2,1)}, u32[]{:S(2)}, u32[]{:S(2)}) %collective-permute-start.15) | collective-permute-done | bytes 950304 | tf_op jit(solution)/shard_map/ppermute | solution.py:180
  110.4 8.3 %shard_map.61.after = bf16[232,1856]{1,0:T(8,128)(2,1)} custom-call(s32[2]{0:T(128)} %pad_add_fusion.place_ref, s32[32]{0:T(128)} %stack.175.where_ref, bf16[8,232,128]{2,1,0:T(8,128)(2,1)} %copy-done.7, bf16[8,232,128]{2,1,0:T(8,128)(2,1)} %collective-permute-done.10.refs_3_.more, bf16[4,2,32,1856]{3,2,1,0:T(8,128)(2,1)} %copy-done.2, ...), custom_call_target="tpu_custom_call" | custom-call | flops 1763704832 | bytes 7602176 | tf_op jit(solution)/shard_map/pallas_call | solution.py:112
  118.7 2.0 %all-to-all-done.received = bf16[16,2,64,256]{3,2,1,0:T(8,128)(2,1)S(1)} async-done(((bf16[16,2,64,256]{3,2,1,0:T(8,128)(2,1)}), bf16[16,2,64,256]{3,2,1,0:T(8,128)(2,1)S(1)}, u32[]{:S(2)}, u32[]{:S(2)}) %all-to-all-start) | async-done | bytes 1048608 | tf_op jit(solution)/shard_map/all_to_all | solution.py:216
  120.6 1.2 copy-done
  122.7 8.5 %collective-permute-start.16 = (f32[64,232]{1,0:T(8,128)S(1)}, f32[64,232]{1,0:T(8,128)S(1)}, u32[]{:S(2)}, u32[]{:S(2)}) collective-permute-start(f32[64,232]{1,0:T(8,128)S(1)} %get-tuple-element.17), channel_id=1, source_target_pairs={{0,64},{64,0},{1,65},{65,1},{2,66},{66,2},{3,67},{67,3},{4,68},{68... | collective-permute-start | bytes 178184 | tf_op jit(solution)/shard_map/ppermute | solution.py:180
  132.1 1.3 shard_map.63
  (42 shorter events, 6.0 us)
Async XLA Ops:
  11.0 8.4 %copy-start.8 = (bf16[128,232]{0,1:T(8,128)(2,1)S(1)}, bf16[128,232]{0,1:T(8,128)(2,1)}, u32[]{:S(2)}) copy-start(bf16[128,232]{0,1:T(8,128)(2,1)} %param.4) | copy-start | bytes 178180
  11.0 19.2 %collective-permute-start = (bf16[2,32,1856]{2,1,0:T(8,128)(2,1)S(1)}, bf16[2,32,1856]{2,1,0:T(8,128)(2,1)S(1)}, u32[]{:S(2)}, u32[]{:S(2)}) collective-permute-start(bf16[2,32,1856]{2,1,0:T(8,128)(2,1)S(1)} %constant_dynamic-slice_fusion), channel_id=1, source_target_pairs={{0,32},{16,48},{32,0},{48,16},{1,33},{17,49},{33,1},{49,17},{2,34}... | collective-permute-start | bytes 712712 | tf_op jit(solution)/shard_map/ppermute | solution.py:193
  13.0 22.6 %collective-permute-start.5 = (bf16[2,32,1856]{2,1,0:T(8,128)(2,1)S(1)}, bf16[2,32,1856]{2,1,0:T(8,128)(2,1)S(1)}, u32[]{:S(2)}, u32[]{:S(2)}) collective-permute-start(bf16[2,32,1856]{2,1,0:T(8,128)(2,1)S(1)} %constant_dynamic-slice_fusion), channel_id=1, source_target_pairs={{0,48},{16,32},{32,16},{48,0},{1,49},{17,33},{33,17},{49,1},{2,50}... | collective-permute-start | bytes 712712 | tf_op jit(solution)/shard_map/ppermute | solution.py:193
  15.2 20.3 %collective-permute-start.6 = (bf16[2,32,1856]{2,1,0:T(8,128)(2,1)S(1)}, bf16[2,32,1856]{2,1,0:T(8,128)(2,1)S(1)}, u32[]{:S(2)}, u32[]{:S(2)}) collective-permute-start(bf16[2,32,1856]{2,1,0:T(8,128)(2,1)S(1)} %constant_dynamic-slice_fusion), channel_id=1, source_target_pairs={{0,16},{16,0},{32,48},{48,32},{1,17},{17,1},{33,49},{49,33},{2,18}... | collective-permute-start | bytes 712712 | tf_op jit(solution)/shard_map/ppermute | solution.py:193
  19.4 12.8 %collective-permute-start.2 = (bf16[1,232,128]{2,1,0:T(8,128)(2,1)S(1)}, bf16[1,232,128]{2,1,0:T(8,128)(2,1)S(1)}, u32[]{:S(2)}, u32[]{:S(2)}) collective-permute-start(bf16[1,232,128]{2,1,0:T(8,128)(2,1)S(1)} %bitcast.54), channel_id=1, source_target_pairs={{0,4},{1,5},{2,6},{3,7},{4,0},{5,1},{6,2},{7,3},{8,12},{9,13},{10,... | collective-permute-start | bytes 178184 | tf_op jit(solution)/shard_map/ppermute | solution.py:186
  30.3 14.1 %collective-permute-start.1 = (bf16[2,2,32,1856]{3,2,1,0:T(8,128)(2,1)S(1)}, bf16[2,2,32,1856]{3,2,1,0:T(8,128)(2,1)S(1)}, u32[]{:S(2)}, u32[]{:S(2)}) collective-permute-start(bf16[2,2,32,1856]{3,2,1,0:T(8,128)(2,1)S(1)} %pad_maximum_fusion.2), channel_id=1, source_target_pairs={{0,128},{128,0},{256,384},{384,256},{1,129},{129,1},{257,385},{385... | collective-permute-start | bytes 1425416 | tf_op jit(solution)/shard_map/ppermute | solution.py:183
  32.3 10.5 %collective-permute-start.3 = (bf16[2,232,128]{2,1,0:T(8,128)(2,1)S(1)}, bf16[2,232,128]{2,1,0:T(8,128)(2,1)S(1)}, u32[]{:S(2)}, u32[]{:S(2)}) collective-permute-start(bf16[2,232,128]{2,1,0:T(8,128)(2,1)S(1)} %pad_maximum_fusion.6), channel_id=1, source_target_pairs={{0,2},{1,3},{2,0},{3,1},{4,6},{5,7},{6,4},{7,5},{8,10},{9,11},{10,... | collective-permute-start | bytes 356360 | tf_op jit(solution)/shard_map/ppermute | solution.py:186
  35.6 18.5 %collective-permute-start.7 = (bf16[2,2,32,1856]{3,2,1,0:T(8,128)(2,1)S(1)}, bf16[2,2,32,1856]{3,2,1,0:T(8,128)(2,1)S(1)}, u32[]{:S(2)}, u32[]{:S(2)}) collective-permute-start(bf16[2,2,32,1856]{3,2,1,0:T(8,128)(2,1)S(1)} %pad_maximum_fusion.3), channel_id=1, source_target_pairs={{0,384},{128,256},{256,128},{384,0},{1,385},{129,257},{257,129},{3... | collective-permute-start | bytes 1425416 | tf_op jit(solution)/shard_map/ppermute | solution.py:183
  44.6 17.9 %copy-start.2 = (bf16[4,2,32,1856]{3,2,1,0:T(8,128)(2,1)}, bf16[4,2,32,1856]{3,2,1,0:T(8,128)(2,1)S(1)}, u32[]{:S(2)}) copy-start(bf16[4,2,32,1856]{3,2,1,0:T(8,128)(2,1)S(1)} %pad_maximum_fusion.refs_1_.refs_0_) | copy-start | bytes 2850820
  44.6 17.8 %collective-permute-start.8 = (bf16[4,232,128]{2,1,0:T(8,128)(2,1)S(1)}, bf16[4,232,128]{2,1,0:T(8,128)(2,1)S(1)}, u32[]{:S(2)}, u32[]{:S(2)}) collective-permute-start(bf16[4,232,128]{2,1,0:T(8,128)(2,1)S(1)} %pad_maximum_fusion.5), channel_id=1, source_target_pairs={{0,8},{8,0},{1,9},{9,1},{2,10},{10,2},{3,11},{11,3},{4,12},{12,4},... | collective-permute-start | bytes 712712 | tf_op jit(solution)/shard_map/ppermute | solution.py:186
  49.6 33.0 %collective-permute-start.4 = (bf16[4,2,32,1856]{3,2,1,0:T(8,128)(2,1)S(1)}, bf16[4,2,32,1856]{3,2,1,0:T(8,128)(2,1)}, u32[]{:S(2)}, u32[]{:S(2)}) collective-permute-start(bf16[4,2,32,1856]{3,2,1,0:T(8,128)(2,1)S(1)} %pad_maximum_fusion.refs_1_.refs_0_), channel_id=1, source_target_pairs={{0,384},{128,256},{256,128},{384,0},{1,385},{129,257},{257,129},{3... | collective-permute-start | bytes 2850824 | tf_op jit(solution)/shard_map/ppermute | solution.py:183
  54.2 17.3 %copy-start.4 = (bf16[4,2,32,1856]{3,2,1,0:T(8,128)(2,1)}, bf16[4,2,32,1856]{3,2,1,0:T(8,128)(2,1)S(1)}, u32[]{:S(2)}) copy-start(bf16[4,2,32,1856]{3,2,1,0:T(8,128)(2,1)S(1)} %pad_maximum_fusion.1.refs_2_.refs_1_) | copy-start | bytes 2850820
  54.2 10.2 %copy-start.6 = (bf16[232,1856]{1,0:T(8,128)(2,1)S(1)}, bf16[232,1856]{1,0:T(8,128)(2,1)}, u32[]{:S(2)}) copy-start(bf16[232,1856]{1,0:T(8,128)(2,1)} %refs_5_.1) | copy-start | bytes 2583556
  62.5 13.6 %copy-start.7 = (bf16[8,232,128]{2,1,0:T(8,128)(2,1)}, bf16[8,232,128]{2,1,0:T(8,128)(2,1)S(1)}, u32[]{:S(2)}) copy-start(bf16[8,232,128]{2,1,0:T(8,128)(2,1)S(1)} %pad_maximum_fusion.4.inputs) | copy-start | bytes 1425412
  62.5 24.0 %collective-permute-start.9 = (bf16[4,2,32,1856]{3,2,1,0:T(8,128)(2,1)S(1)}, bf16[4,2,32,1856]{3,2,1,0:T(8,128)(2,1)}, u32[]{:S(2)}, u32[]{:S(2)}) collective-permute-start(bf16[4,2,32,1856]{3,2,1,0:T(8,128)(2,1)S(1)} %pad_maximum_fusion.1.refs_2_.refs_1_), channel_id=1, source_target_pairs={{0,128},{128,0},{256,384},{384,256},{1,129},{129,1},{257,385},{385... | collective-permute-start | bytes 2850824 | tf_op jit(solution)/shard_map/ppermute | solution.py:183
  64.4 7.1 %collective-permute-start.11 = (bf16[232,1856]{1,0:T(8,128)(2,1)S(1)}, bf16[232,1856]{1,0:T(8,128)(2,1)}, u32[]{:S(2)}, u32[]{:S(2)}) collective-permute-start(bf16[232,1856]{1,0:T(8,128)(2,1)S(1)} %copy-done.6), channel_id=1, source_target_pairs={{0,64},{64,0},{1,65},{65,1},{2,66},{66,2},{3,67},{67,3},{4,68},{68... | collective-permute-start | bytes 2583560 | tf_op jit(solution)/shard_map/ppermute | solution.py:180
  68.2 14.5 %collective-permute-start.10 = (bf16[8,232,128]{2,1,0:T(8,128)(2,1)S(1)}, bf16[8,232,128]{2,1,0:T(8,128)(2,1)}, u32[]{:S(2)}, u32[]{:S(2)}) collective-permute-start(bf16[8,232,128]{2,1,0:T(8,128)(2,1)S(1)} %pad_maximum_fusion.4.inputs), channel_id=1, source_target_pairs={{0,1},{1,0},{2,3},{3,2},{4,5},{5,4},{6,7},{7,6},{8,9},{9,8},{10,11... | collective-permute-start | bytes 1425416 | tf_op jit(solution)/shard_map/ppermute | solution.py:204
  91.0 4.6 %copy-start.3 = (bf16[4,2,32,1856]{3,2,1,0:T(8,128)(2,1)S(1)}, bf16[4,2,32,1856]{3,2,1,0:T(8,128)(2,1)}, u32[]{:S(2)}) copy-start(bf16[4,2,32,1856]{3,2,1,0:T(8,128)(2,1)} %copy-done.2) | copy-start | bytes 2850820
  91.0 10.2 %copy-start.5 = (bf16[4,2,32,1856]{3,2,1,0:T(8,128)(2,1)S(1)}, bf16[4,2,32,1856]{3,2,1,0:T(8,128)(2,1)}, u32[]{:S(2)}) copy-start(bf16[4,2,32,1856]{3,2,1,0:T(8,128)(2,1)} %copy-done.4) | copy-start | bytes 2850820
  91.0 29.6 %all-to-all-start = ((bf16[16,2,64,256]{3,2,1,0:T(8,128)(2,1)}), bf16[16,2,64,256]{3,2,1,0:T(8,128)(2,1)S(1)}, u32[]{:S(2)}, u32[]{:S(2)}) async-start(bf16[16,2,64,256]{3,2,1,0:T(8,128)(2,1)} %shard_map.60), calls=%async_computation | async-start | bytes 2097152 | tf_op jit(solution)/shard_map/all_to_all | solution.py:216
  95.6 13.2 %collective-permute-start.12 = (bf16[4,2,32,1856]{3,2,1,0:T(8,128)(2,1)S(1)}, bf16[4,2,32,1856]{3,2,1,0:T(8,128)(2,1)}, u32[]{:S(2)}, u32[]{:S(2)}) collective-permute-start(bf16[4,2,32,1856]{3,2,1,0:T(8,128)(2,1)S(1)} %copy-done.3), channel_id=1, source_target_pairs={{0,64},{64,0},{1,65},{65,1},{2,66},{66,2},{3,67},{67,3},{4,68},{68... | collective-permute-start | bytes 2850824 | tf_op jit(solution)/shard_map/ppermute | solution.py:180
  101.2 7.6 %collective-permute-start.13 = (bf16[4,2,32,1856]{3,2,1,0:T(8,128)(2,1)S(1)}, bf16[4,2,32,1856]{3,2,1,0:T(8,128)(2,1)}, u32[]{:S(2)}, u32[]{:S(2)}) collective-permute-start(bf16[4,2,32,1856]{3,2,1,0:T(8,128)(2,1)S(1)} %copy-done.5), channel_id=1, source_target_pairs={{0,64},{64,0},{1,65},{65,1},{2,66},{66,2},{3,67},{67,3},{4,68},{68... | collective-permute-start | bytes 2850824 | tf_op jit(solution)/shard_map/ppermute | solution.py:180
  103.2 5.7 %collective-permute-start.14 = (bf16[4,2,32,1856]{3,2,1,0:T(8,128)(2,1)}, bf16[4,2,32,1856]{3,2,1,0:T(8,128)(2,1)}, u32[]{:S(2)}, u32[]{:S(2)}) collective-permute-start(bf16[4,2,32,1856]{3,2,1,0:T(8,128)(2,1)} %collective-permute-done.4.refs_1_.refs_2_), channel_id=1, source_target_pairs={{0,64},{64,0},{1,65},{65,1},{2,66},{66,2},{3,67},{67,3},{4,68},{68... | collective-permute-start | bytes 2850824 | tf_op jit(solution)/shard_map/ppermute | solution.py:180
  105.6 4.8 %collective-permute-start.15 = (bf16[4,2,32,1856]{3,2,1,0:T(8,128)(2,1)}, bf16[4,2,32,1856]{3,2,1,0:T(8,128)(2,1)}, u32[]{:S(2)}, u32[]{:S(2)}) collective-permute-start(bf16[4,2,32,1856]{3,2,1,0:T(8,128)(2,1)} %collective-permute-done.9.refs_2_.refs_3_), channel_id=1, source_target_pairs={{0,64},{64,0},{1,65},{65,1},{2,66},{66,2},{3,67},{67,3},{4,68},{68... | collective-permute-start | bytes 2850824 | tf_op jit(solution)/shard_map/ppermute | solution.py:180
  120.6 1.2 copy-start
  122.7 9.4 %copy-start.1 = (s32[2]{0:T(128)S(1)}, s32[2]{0:T(128)}, u32[]{:S(2)}) copy-start(s32[2]{0:T(128)} %pad_add_fusion.place_ref) | copy-start | bytes 28
  122.7 9.4 %collective-permute-start.16 = (f32[64,232]{1,0:T(8,128)S(1)}, f32[64,232]{1,0:T(8,128)S(1)}, u32[]{:S(2)}, u32[]{:S(2)}) collective-permute-start(f32[64,232]{1,0:T(8,128)S(1)} %get-tuple-element.17), channel_id=1, source_target_pairs={{0,64},{64,0},{1,65},{65,1},{2,66},{66,2},{3,67},{67,3},{4,68},{68... | collective-permute-start | bytes 178184 | tf_op jit(solution)/shard_map/ppermute | solution.py:180

commit v7 on v6

--- a/solution.py
+++ b/solution.py
@@ -151,9 +151,12 @@
 def merge_kernel(place_ref, mine, theirs, out, whole):
     half, features = mine.shape[0] // 2, mine.shape[1]
     for slot in range(2):
-        for ref, part in ((mine, place_ref[0]), (theirs, 1 - place_ref[0])):
+        other = 1 - place_ref[0]
+        for block, part in (
+                (mine[slot * half:(slot + 1) * half], place_ref[0]),
+                (theirs[other, slot * half:(slot + 1) * half], other)):
             first = pl.multiple_of((slot * 2 + part) * half, half)
-            whole[pl.ds(first, half), :features] = ref[slot * half:(slot + 1) * half]
+            whole[pl.ds(first, half), :features] = block
     out[...] = whole[...].T[:features].astype(out.dtype)
 
 
@@ -217,7 +220,7 @@
     d_weight = weight_grad(place, bins, inputs, pieces + [swap(piece) for piece in pieces])
 
     keep, send = add_up(received, features, d_weight)
-    d_input = merge(place, keep, swap(send))
+    d_input = merge(place, keep, lax.all_gather(send, "core", axis=0))
     return d_input.T, d_weight
 
 

time: 135 us -> 134 us (level)
  starting transfers between devices: 64.7 us -> 56.2 us
  blocking collectives: 8.66 us -> 16.8 us
    ppermute x6 -> x5, starting transfers between devices: 24.1 us -> 15.6 us  [swap(): return lax.ppermute(array, 'core', flips(CORES, 1))]
    all_gather x0 -> x1, blocking collectives: none -> 8.1 us  [on_device(): d_input = merge(place, keep, lax.all_gather(send, 'core', axis=0))]
  transfers between devices with their start and end apart: 18 -> 17, of which waited for: 9 -> 8; matrix products, arithmetic and copies ran while one was open for 2% -> 2% of each run, Pallas kernels for 10% -> 10%
where the time goes in v7:
time: 134 us; the launch traced here: 133 us
  starting transfers between devices  56.2 us (42%)
  waiting for transfers between devices  32.8 us (24%)
  Pallas kernels  19.5 us (15%)
  blocking collectives  16.8 us (13%)
  local copies, waits for them, and re-layouts  3.69 us (3%)
  other arithmetic  2.06 us (2%)
  between operations  1.68 us (1%)
    ppermute x5, starting transfers between devices, swap(): return lax.ppermute(array, 'core', flips(CORES, 1))  15.6 us
    ppermute x3, starting transfers between devices, wider(): lax.ppermute(inputs, axis, flips(size, flip))  13.7 us
    ppermute x4, starting transfers between devices, over_x(): return lax.ppermute(array, 'x', flips(X, flip))  12 us
    ppermute x3, waiting for transfers between devices, wider(): lax.ppermute(inputs, axis, flips(size, flip))  11.7 us
    pallas_call x2, Pallas kernels, partials(): pl.pallas_call(lambda *refs: partial_kernel(len(pieces), *refs), out_shap...  9.06 us
    all_gather x1, blocking collectives, on_device(): both = lax.all_gather(masked, 'core', axis=0)  8.66 us
    ppermute x3, starting transfers between devices, on_device(): lax.ppermute(both, 'row', flips(ROWS, flip))  8.37 us
    pallas_call x1, Pallas kernels, weight_grad(): pl.pallas_call(weight_grad_kernel, out_shape=jax.ShapeDtypeStruct((featur...  8.26 us
  transfers between devices with their start and end apart: 17, of which 8 were waited for; matrix products, arithmetic and copies ran while one was open for 2% of the time, Pallas kernels for 10%

profile of v7, /device:TPU:1, one launch (start us, length us, event | category | flops | bytes accessed | tf_op | source)
XLA Modules:
  0.0 132.6 jit_solution(17186255231959005941)
XLA Ops:
  2.3 8.7 %all-gather = bf16[128,1856]{1,0:T(8,128)(2,1)S(1)} all-gather(bf16[64,1856]{1,0:T(8,128)(2,1)S(1)} %broadcast_select_fusion), channel_id=2, replica_groups=mesh['x'=4,'core'=2,'row'=4,'far'=2,'near'=8] {'core'}, dimensions={0}, use_global_device_ids=true | all-gather | bytes 712704 | tf_op jit(solution)/shard_map/all_gather | solution.py:193
  11.0 1.9 %collective-permute-start = (bf16[2,32,1856]{2,1,0:T(8,128)(2,1)S(1)}, bf16[2,32,1856]{2,1,0:T(8,128)(2,1)S(1)}, u32[]{:S(2)}, u32[]{:S(2)}) collective-permute-start(bf16[2,32,1856]{2,1,0:T(8,128)(2,1)S(1)} %constant_dynamic-slice_fusion), channel_id=1, source_target_pairs={{0,32},{16,48},{32,0},{48,16},{1,33},{17,49},{33,1},{49,17},{2,34}... | collective-permute-start | bytes 712712 | tf_op jit(solution)/shard_map/ppermute | solution.py:196
  13.0 2.2 %collective-permute-start.5 = (bf16[2,32,1856]{2,1,0:T(8,128)(2,1)S(1)}, bf16[2,32,1856]{2,1,0:T(8,128)(2,1)S(1)}, u32[]{:S(2)}, u32[]{:S(2)}) collective-permute-start(bf16[2,32,1856]{2,1,0:T(8,128)(2,1)S(1)} %constant_dynamic-slice_fusion), channel_id=1, source_target_pairs={{0,48},{16,32},{32,16},{48,0},{1,49},{17,33},{33,17},{49,1},{2,50}... | collective-permute-start | bytes 712712 | tf_op jit(solution)/shard_map/ppermute | solution.py:196
  15.2 4.2 %collective-permute-start.6 = (bf16[2,32,1856]{2,1,0:T(8,128)(2,1)S(1)}, bf16[2,32,1856]{2,1,0:T(8,128)(2,1)S(1)}, u32[]{:S(2)}, u32[]{:S(2)}) collective-permute-start(bf16[2,32,1856]{2,1,0:T(8,128)(2,1)S(1)} %constant_dynamic-slice_fusion), channel_id=1, source_target_pairs={{0,16},{16,0},{32,48},{48,32},{1,17},{17,1},{33,49},{49,33},{2,18}... | collective-permute-start | bytes 712712 | tf_op jit(solution)/shard_map/ppermute | solution.py:196
  19.4 5.4 %collective-permute-start.2 = (bf16[1,232,128]{2,1,0:T(8,128)(2,1)S(1)}, bf16[1,232,128]{2,1,0:T(8,128)(2,1)S(1)}, u32[]{:S(2)}, u32[]{:S(2)}) collective-permute-start(bf16[1,232,128]{2,1,0:T(8,128)(2,1)S(1)} %bitcast.56), channel_id=1, source_target_pairs={{0,4},{1,5},{2,6},{3,7},{4,0},{5,1},{6,2},{7,3},{8,12},{9,13},{10,... | collective-permute-start | bytes 178184 | tf_op jit(solution)/shard_map/ppermute | solution.py:189
  24.9 5.4 %collective-permute-done = bf16[2,32,1856]{2,1,0:T(8,128)(2,1)S(1)} collective-permute-done((bf16[2,32,1856]{2,1,0:T(8,128)(2,1)S(1)}, bf16[2,32,1856]{2,1,0:T(8,128)(2,1)S(1)}, u32[]{:S(2)}, u32[]{:S(2)}) %collective-permute-start) | collective-permute-done | bytes 237600 | tf_op jit(solution)/shard_map/ppermute | solution.py:196
  30.3 1.9 %collective-permute-start.1 = (bf16[2,2,32,1856]{3,2,1,0:T(8,128)(2,1)S(1)}, bf16[2,2,32,1856]{3,2,1,0:T(8,128)(2,1)S(1)}, u32[]{:S(2)}, u32[]{:S(2)}) collective-permute-start(bf16[2,2,32,1856]{3,2,1,0:T(8,128)(2,1)S(1)} %pad_maximum_fusion.2), channel_id=1, source_target_pairs={{0,128},{128,0},{256,384},{384,256},{1,129},{129,1},{257,385},{385... | collective-permute-start | bytes 1425416 | tf_op jit(solution)/shard_map/ppermute | solution.py:186
  32.3 3.2 %collective-permute-start.3 = (bf16[2,232,128]{2,1,0:T(8,128)(2,1)S(1)}, bf16[2,232,128]{2,1,0:T(8,128)(2,1)S(1)}, u32[]{:S(2)}, u32[]{:S(2)}) collective-permute-start(bf16[2,232,128]{2,1,0:T(8,128)(2,1)S(1)} %pad_maximum_fusion.6), channel_id=1, source_target_pairs={{0,2},{1,3},{2,0},{3,1},{4,6},{5,7},{6,4},{7,5},{8,10},{9,11},{10,... | collective-permute-start | bytes 356360 | tf_op jit(solution)/shard_map/ppermute | solution.py:189
  35.6 3.7 %collective-permute-start.7 = (bf16[2,2,32,1856]{3,2,1,0:T(8,128)(2,1)S(1)}, bf16[2,2,32,1856]{3,2,1,0:T(8,128)(2,1)S(1)}, u32[]{:S(2)}, u32[]{:S(2)}) collective-permute-start(bf16[2,2,32,1856]{3,2,1,0:T(8,128)(2,1)S(1)} %pad_maximum_fusion.3), channel_id=1, source_target_pairs={{0,384},{128,256},{256,128},{384,0},{1,385},{129,257},{257,129},{3... | collective-permute-start | bytes 1425416 | tf_op jit(solution)/shard_map/ppermute | solution.py:186
  39.3 3.5 %collective-permute-done.3 = bf16[2,232,128]{2,1,0:T(8,128)(2,1)S(1)} collective-permute-done((bf16[2,232,128]{2,1,0:T(8,128)(2,1)S(1)}, bf16[2,232,128]{2,1,0:T(8,128)(2,1)S(1)}, u32[]{:S(2)}, u32[]{:S(2)}) %collective-permute-start.3) | collective-permute-done | bytes 118816 | tf_op jit(solution)/shard_map/ppermute | solution.py:189
  42.8 1.6 %collective-permute-done.1 = bf16[2,2,32,1856]{3,2,1,0:T(8,128)(2,1)S(1)} collective-permute-done((bf16[2,2,32,1856]{3,2,1,0:T(8,128)(2,1)S(1)}, bf16[2,2,32,1856]{3,2,1,0:T(8,128)(2,1)S(1)}, u32[]{:S(2)}, u32[]{:S(2)}) %collective-permute-start.1) | collective-permute-done | bytes 475168 | tf_op jit(solution)/shard_map/ppermute | solution.py:186
  44.6 5.0 %collective-permute-start.8 = (bf16[4,232,128]{2,1,0:T(8,128)(2,1)S(1)}, bf16[4,232,128]{2,1,0:T(8,128)(2,1)S(1)}, u32[]{:S(2)}, u32[]{:S(2)}) collective-permute-start(bf16[4,232,128]{2,1,0:T(8,128)(2,1)S(1)} %pad_maximum_fusion.5), channel_id=1, source_target_pairs={{0,8},{8,0},{1,9},{9,1},{2,10},{10,2},{3,11},{11,3},{4,12},{12,4},... | collective-permute-start | bytes 712712 | tf_op jit(solution)/shard_map/ppermute | solution.py:189
  49.6 4.4 %collective-permute-start.4 = (bf16[4,2,32,1856]{3,2,1,0:T(8,128)(2,1)S(1)}, bf16[4,2,32,1856]{3,2,1,0:T(8,128)(2,1)}, u32[]{:S(2)}, u32[]{:S(2)}) collective-permute-start(bf16[4,2,32,1856]{3,2,1,0:T(8,128)(2,1)S(1)} %pad_maximum_fusion.refs_1_.refs_0_), channel_id=1, source_target_pairs={{0,384},{128,256},{256,128},{384,0},{1,385},{129,257},{257,129},{3... | collective-permute-start | bytes 2850824 | tf_op jit(solution)/shard_map/ppermute | solution.py:186
  54.2 8.2 %collective-permute-done.8 = bf16[4,232,128]{2,1,0:T(8,128)(2,1)S(1)} collective-permute-done((bf16[4,232,128]{2,1,0:T(8,128)(2,1)S(1)}, bf16[4,232,128]{2,1,0:T(8,128)(2,1)S(1)}, u32[]{:S(2)}, u32[]{:S(2)}) %collective-permute-start.8) | collective-permute-done | bytes 237600 | tf_op jit(solution)/shard_map/ppermute | solution.py:189
  62.5 1.9 %collective-permute-start.9 = (bf16[4,2,32,1856]{3,2,1,0:T(8,128)(2,1)S(1)}, bf16[4,2,32,1856]{3,2,1,0:T(8,128)(2,1)}, u32[]{:S(2)}, u32[]{:S(2)}) collective-permute-start(bf16[4,2,32,1856]{3,2,1,0:T(8,128)(2,1)S(1)} %pad_maximum_fusion.1.refs_2_.refs_1_), channel_id=1, source_target_pairs={{0,128},{128,0},{256,384},{384,256},{1,129},{129,1},{257,385},{385... | collective-permute-start | bytes 2850824 | tf_op jit(solution)/shard_map/ppermute | solution.py:186
  64.4 3.7 %collective-permute-start.11 = (bf16[232,1856]{1,0:T(8,128)(2,1)S(1)}, bf16[232,1856]{1,0:T(8,128)(2,1)}, u32[]{:S(2)}, u32[]{:S(2)}) collective-permute-start(bf16[232,1856]{1,0:T(8,128)(2,1)S(1)} %copy-done.6), channel_id=1, source_target_pairs={{0,64},{64,0},{1,65},{65,1},{2,66},{66,2},{3,67},{67,3},{4,68},{68... | collective-permute-start | bytes 2583560 | tf_op jit(solution)/shard_map/ppermute | solution.py:183
  68.2 2.0 %collective-permute-start.10 = (bf16[8,232,128]{2,1,0:T(8,128)(2,1)S(1)}, bf16[8,232,128]{2,1,0:T(8,128)(2,1)}, u32[]{:S(2)}, u32[]{:S(2)}) collective-permute-start(bf16[8,232,128]{2,1,0:T(8,128)(2,1)S(1)} %pad_maximum_fusion.4.inputs), channel_id=1, source_target_pairs={{0,1},{1,0},{2,3},{3,2},{4,5},{5,4},{6,7},{7,6},{8,9},{9,8},{10,11... | collective-permute-start | bytes 1425416 | tf_op jit(solution)/shard_map/ppermute | solution.py:207
  71.4 4.5 %shard_map.59.refs_4_ = bf16[16,2,64,256]{3,2,1,0:T(8,128)(2,1)} custom-call(s32[16]{0:T(128)} %stack.174.refs_0_, bf16[4,2,32,1856]{3,2,1,0:T(8,128)(2,1)} %copy-done.2, bf16[4,2,32,1856]{3,2,1,0:T(8,128)(2,1)} %copy-done.4, bf16[232,1856]{1,0:T(8,128)(2,1)} %refs_5_.1, bf16[232,1856]{1,0:T(8,128)(2,1)} %collective-permute-done.11.refs_4_.refs_6_), custom_call_target="tpu_custom_call" | custom-call | flops 881852416 | bytes 1900544 | tf_op jit(solution)/shard_map/pallas_call | solution.py:66
  76.0 6.7 %collective-permute-done.10.refs_3_.more = bf16[8,232,128]{2,1,0:T(8,128)(2,1)} collective-permute-done((bf16[8,232,128]{2,1,0:T(8,128)(2,1)S(1)}, bf16[8,232,128]{2,1,0:T(8,128)(2,1)}, u32[]{:S(2)}, u32[]{:S(2)}) %collective-permute-start.10) | collective-permute-done | bytes 475168 | tf_op jit(solution)/shard_map/ppermute | solution.py:207
  82.7 3.8 %collective-permute-done.9.refs_2_.refs_3_ = bf16[4,2,32,1856]{3,2,1,0:T(8,128)(2,1)} collective-permute-done((bf16[4,2,32,1856]{3,2,1,0:T(8,128)(2,1)S(1)}, bf16[4,2,32,1856]{3,2,1,0:T(8,128)(2,1)}, u32[]{:S(2)}, u32[]{:S(2)}) %collective-permute-start.9) | collective-permute-done | bytes 950304 | tf_op jit(solution)/shard_map/ppermute | solution.py:186
  86.4 4.5 %shard_map.60 = bf16[16,2,64,256]{3,2,1,0:T(8,128)(2,1)} custom-call(s32[16]{0:T(128)} %stack.151.refs_0_, bf16[4,2,32,1856]{3,2,1,0:T(8,128)(2,1)} %collective-permute-done.4.refs_1_.refs_2_, bf16[4,2,32,1856]{3,2,1,0:T(8,128)(2,1)} %collective-permute-done.9.refs_2_.refs_3_, ...), custom_call_target="tpu_custom_call", output_to_operand_aliasing={{}: (4, {})} | custom-call | flops 881852416 | bytes 1900544 | tf_op jit(solution)/shard_map/pallas_call | solution.py:66
  91.0 4.6 %all-to-all-start = ((bf16[16,2,64,256]{3,2,1,0:T(8,128)(2,1)}), bf16[16,2,64,256]{3,2,1,0:T(8,128)(2,1)S(1)}, u32[]{:S(2)}, u32[]{:S(2)}) async-start(bf16[16,2,64,256]{3,2,1,0:T(8,128)(2,1)} %shard_map.60), calls=%async_computation | async-start | bytes 2097152 | tf_op jit(solution)/shard_map/all_to_all | solution.py:219
  95.6 5.6 %collective-permute-start.12 = (bf16[4,2,32,1856]{3,2,1,0:T(8,128)(2,1)S(1)}, bf16[4,2,32,1856]{3,2,1,0:T(8,128)(2,1)}, u32[]{:S(2)}, u32[]{:S(2)}) collective-permute-start(bf16[4,2,32,1856]{3,2,1,0:T(8,128)(2,1)S(1)} %copy-done.3), channel_id=1, source_target_pairs={{0,64},{64,0},{1,65},{65,1},{2,66},{66,2},{3,67},{67,3},{4,68},{68... | collective-permute-start | bytes 2850824 | tf_op jit(solution)/shard_map/ppermute | solution.py:183
  101.2 1.9 %collective-permute-start.13 = (bf16[4,2,32,1856]{3,2,1,0:T(8,128)(2,1)S(1)}, bf16[4,2,32,1856]{3,2,1,0:T(8,128)(2,1)}, u32[]{:S(2)}, u32[]{:S(2)}) collective-permute-start(bf16[4,2,32,1856]{3,2,1,0:T(8,128)(2,1)S(1)} %copy-done.5), channel_id=1, source_target_pairs={{0,64},{64,0},{1,65},{65,1},{2,66},{66,2},{3,67},{67,3},{4,68},{68... | collective-permute-start | bytes 2850824 | tf_op jit(solution)/shard_map/ppermute | solution.py:183
  103.2 2.4 %collective-permute-start.14 = (bf16[4,2,32,1856]{3,2,1,0:T(8,128)(2,1)}, bf16[4,2,32,1856]{3,2,1,0:T(8,128)(2,1)}, u32[]{:S(2)}, u32[]{:S(2)}) collective-permute-start(bf16[4,2,32,1856]{3,2,1,0:T(8,128)(2,1)} %collective-permute-done.4.refs_1_.refs_2_), channel_id=1, source_target_pairs={{0,64},{64,0},{1,65},{65,1},{2,66},{66,2},{3,67},{67,3},{4,68},{68... | collective-permute-start | bytes 2850824 | tf_op jit(solution)/shard_map/ppermute | solution.py:183
  105.6 1.9 %collective-permute-start.15 = (bf16[4,2,32,1856]{3,2,1,0:T(8,128)(2,1)}, bf16[4,2,32,1856]{3,2,1,0:T(8,128)(2,1)}, u32[]{:S(2)}, u32[]{:S(2)}) collective-permute-start(bf16[4,2,32,1856]{3,2,1,0:T(8,128)(2,1)} %collective-permute-done.9.refs_2_.refs_3_), channel_id=1, source_target_pairs={{0,64},{64,0},{1,65},{65,1},{2,66},{66,2},{3,67},{67,3},{4,68},{68... | collective-permute-start | bytes 2850824 | tf_op jit(solution)/shard_map/ppermute | solution.py:183
  108.7 1.7 %collective-permute-done.15.refs_7_ = bf16[4,2,32,1856]{3,2,1,0:T(8,128)(2,1)} collective-permute-done((bf16[4,2,32,1856]{3,2,1,0:T(8,128)(2,1)}, bf16[4,2,32,1856]{3,2,1,0:T(8,128)(2,1)}, u32[]{:S(2)}, u32[]{:S(2)}) %collective-permute-start.15) | collective-permute-done | bytes 950304 | tf_op jit(solution)/shard_map/ppermute | solution.py:183
  110.4 8.3 %shard_map.61.after = bf16[232,1856]{1,0:T(8,128)(2,1)} custom-call(s32[2]{0:T(128)} %pad_add_fusion.place_ref, s32[32]{0:T(128)} %stack.175.where_ref, bf16[8,232,128]{2,1,0:T(8,128)(2,1)} %copy-done.7, bf16[8,232,128]{2,1,0:T(8,128)(2,1)} %collective-permute-done.10.refs_3_.more, bf16[4,2,32,1856]{3,2,1,0:T(8,128)(2,1)} %copy-done.2, ...), custom_call_target="tpu_custom_call" | custom-call | flops 1763704832 | bytes 7602176 | tf_op jit(solution)/shard_map/pallas_call | solution.py:112
  118.6 2.0 %all-to-all-done.received = bf16[16,2,64,256]{3,2,1,0:T(8,128)(2,1)S(1)} async-done(((bf16[16,2,64,256]{3,2,1,0:T(8,128)(2,1)}), bf16[16,2,64,256]{3,2,1,0:T(8,128)(2,1)S(1)}, u32[]{:S(2)}, u32[]{:S(2)}) %all-to-all-start) | async-done | bytes 1048608 | tf_op jit(solution)/shard_map/all_to_all | solution.py:219
  120.6 1.2 copy-done
  122.7 8.1 %all-gather.1 = f32[128,232]{1,0:T(8,128)S(1)} all-gather(f32[64,232]{1,0:T(8,128)S(1)} %get-tuple-element.17), channel_id=3, replica_groups=mesh['x'=4,'core'=2,'row'=4,'far'=2,'near'=8] {'core'}, dimensions={0}, use_global_device_ids=true | all-gather | bytes 178176 | tf_op jit(solution)/shard_map/all_gather | solution.py:223
  131.4 1.3 shard_map.63
  (41 shorter events, 5.5 us)
Async XLA Ops:
  11.0 8.4 %copy-start.8 = (bf16[128,232]{0,1:T(8,128)(2,1)S(1)}, bf16[128,232]{0,1:T(8,128)(2,1)}, u32[]{:S(2)}) copy-start(bf16[128,232]{0,1:T(8,128)(2,1)} %param.4) | copy-start | bytes 178180
  11.0 19.2 %collective-permute-start = (bf16[2,32,1856]{2,1,0:T(8,128)(2,1)S(1)}, bf16[2,32,1856]{2,1,0:T(8,128)(2,1)S(1)}, u32[]{:S(2)}, u32[]{:S(2)}) collective-permute-start(bf16[2,32,1856]{2,1,0:T(8,128)(2,1)S(1)} %constant_dynamic-slice_fusion), channel_id=1, source_target_pairs={{0,32},{16,48},{32,0},{48,16},{1,33},{17,49},{33,1},{49,17},{2,34}... | collective-permute-start | bytes 712712 | tf_op jit(solution)/shard_map/ppermute | solution.py:196
  13.0 22.6 %collective-permute-start.5 = (bf16[2,32,1856]{2,1,0:T(8,128)(2,1)S(1)}, bf16[2,32,1856]{2,1,0:T(8,128)(2,1)S(1)}, u32[]{:S(2)}, u32[]{:S(2)}) collective-permute-start(bf16[2,32,1856]{2,1,0:T(8,128)(2,1)S(1)} %constant_dynamic-slice_fusion), channel_id=1, source_target_pairs={{0,48},{16,32},{32,16},{48,0},{1,49},{17,33},{33,17},{49,1},{2,50}... | collective-permute-start | bytes 712712 | tf_op jit(solution)/shard_map/ppermute | solution.py:196
  15.2 20.3 %collective-permute-start.6 = (bf16[2,32,1856]{2,1,0:T(8,128)(2,1)S(1)}, bf16[2,32,1856]{2,1,0:T(8,128)(2,1)S(1)}, u32[]{:S(2)}, u32[]{:S(2)}) collective-permute-start(bf16[2,32,1856]{2,1,0:T(8,128)(2,1)S(1)} %constant_dynamic-slice_fusion), channel_id=1, source_target_pairs={{0,16},{16,0},{32,48},{48,32},{1,17},{17,1},{33,49},{49,33},{2,18}... | collective-permute-start | bytes 712712 | tf_op jit(solution)/shard_map/ppermute | solution.py:196
  19.4 12.8 %collective-permute-start.2 = (bf16[1,232,128]{2,1,0:T(8,128)(2,1)S(1)}, bf16[1,232,128]{2,1,0:T(8,128)(2,1)S(1)}, u32[]{:S(2)}, u32[]{:S(2)}) collective-permute-start(bf16[1,232,128]{2,1,0:T(8,128)(2,1)S(1)} %bitcast.56), channel_id=1, source_target_pairs={{0,4},{1,5},{2,6},{3,7},{4,0},{5,1},{6,2},{7,3},{8,12},{9,13},{10,... | collective-permute-start | bytes 178184 | tf_op jit(solution)/shard_map/ppermute | solution.py:189
  30.3 14.1 %collective-permute-start.1 = (bf16[2,2,32,1856]{3,2,1,0:T(8,128)(2,1)S(1)}, bf16[2,2,32,1856]{3,2,1,0:T(8,128)(2,1)S(1)}, u32[]{:S(2)}, u32[]{:S(2)}) collective-permute-start(bf16[2,2,32,1856]{3,2,1,0:T(8,128)(2,1)S(1)} %pad_maximum_fusion.2), channel_id=1, source_target_pairs={{0,128},{128,0},{256,384},{384,256},{1,129},{129,1},{257,385},{385... | collective-permute-start | bytes 1425416 | tf_op jit(solution)/shard_map/ppermute | solution.py:186
  32.3 10.5 %collective-permute-start.3 = (bf16[2,232,128]{2,1,0:T(8,128)(2,1)S(1)}, bf16[2,232,128]{2,1,0:T(8,128)(2,1)S(1)}, u32[]{:S(2)}, u32[]{:S(2)}) collective-permute-start(bf16[2,232,128]{2,1,0:T(8,128)(2,1)S(1)} %pad_maximum_fusion.6), channel_id=1, source_target_pairs={{0,2},{1,3},{2,0},{3,1},{4,6},{5,7},{6,4},{7,5},{8,10},{9,11},{10,... | collective-permute-start | bytes 356360 | tf_op jit(solution)/shard_map/ppermute | solution.py:189
  35.6 18.5 %collective-permute-start.7 = (bf16[2,2,32,1856]{3,2,1,0:T(8,128)(2,1)S(1)}, bf16[2,2,32,1856]{3,2,1,0:T(8,128)(2,1)S(1)}, u32[]{:S(2)}, u32[]{:S(2)}) collective-permute-start(bf16[2,2,32,1856]{3,2,1,0:T(8,128)(2,1)S(1)} %pad_maximum_fusion.3), channel_id=1, source_target_pairs={{0,384},{128,256},{256,128},{384,0},{1,385},{129,257},{257,129},{3... | collective-permute-start | bytes 1425416 | tf_op jit(solution)/shard_map/ppermute | solution.py:186
  44.6 17.9 %copy-start.2 = (bf16[4,2,32,1856]{3,2,1,0:T(8,128)(2,1)}, bf16[4,2,32,1856]{3,2,1,0:T(8,128)(2,1)S(1)}, u32[]{:S(2)}) copy-start(bf16[4,2,32,1856]{3,2,1,0:T(8,128)(2,1)S(1)} %pad_maximum_fusion.refs_1_.refs_0_) | copy-start | bytes 2850820
  44.6 17.8 %collective-permute-start.8 = (bf16[4,232,128]{2,1,0:T(8,128)(2,1)S(1)}, bf16[4,232,128]{2,1,0:T(8,128)(2,1)S(1)}, u32[]{:S(2)}, u32[]{:S(2)}) collective-permute-start(bf16[4,232,128]{2,1,0:T(8,128)(2,1)S(1)} %pad_maximum_fusion.5), channel_id=1, source_target_pairs={{0,8},{8,0},{1,9},{9,1},{2,10},{10,2},{3,11},{11,3},{4,12},{12,4},... | collective-permute-start | bytes 712712 | tf_op jit(solution)/shard_map/ppermute | solution.py:189
  49.6 33.0 %collective-permute-start.4 = (bf16[4,2,32,1856]{3,2,1,0:T(8,128)(2,1)S(1)}, bf16[4,2,32,1856]{3,2,1,0:T(8,128)(2,1)}, u32[]{:S(2)}, u32[]{:S(2)}) collective-permute-start(bf16[4,2,32,1856]{3,2,1,0:T(8,128)(2,1)S(1)} %pad_maximum_fusion.refs_1_.refs_0_), channel_id=1, source_target_pairs={{0,384},{128,256},{256,128},{384,0},{1,385},{129,257},{257,129},{3... | collective-permute-start | bytes 2850824 | tf_op jit(solution)/shard_map/ppermute | solution.py:186
  54.2 17.2 %copy-start.4 = (bf16[4,2,32,1856]{3,2,1,0:T(8,128)(2,1)}, bf16[4,2,32,1856]{3,2,1,0:T(8,128)(2,1)S(1)}, u32[]{:S(2)}) copy-start(bf16[4,2,32,1856]{3,2,1,0:T(8,128)(2,1)S(1)} %pad_maximum_fusion.1.refs_2_.refs_1_) | copy-start | bytes 2850820
  54.2 10.2 %copy-start.6 = (bf16[232,1856]{1,0:T(8,128)(2,1)S(1)}, bf16[232,1856]{1,0:T(8,128)(2,1)}, u32[]{:S(2)}) copy-start(bf16[232,1856]{1,0:T(8,128)(2,1)} %refs_5_.1) | copy-start | bytes 2583556
  62.5 13.5 %copy-start.7 = (bf16[8,232,128]{2,1,0:T(8,128)(2,1)}, bf16[8,232,128]{2,1,0:T(8,128)(2,1)S(1)}, u32[]{:S(2)}) copy-start(bf16[8,232,128]{2,1,0:T(8,128)(2,1)S(1)} %pad_maximum_fusion.4.inputs) | copy-start | bytes 1425412
  62.5 24.0 %collective-permute-start.9 = (bf16[4,2,32,1856]{3,2,1,0:T(8,128)(2,1)S(1)}, bf16[4,2,32,1856]{3,2,1,0:T(8,128)(2,1)}, u32[]{:S(2)}, u32[]{:S(2)}) collective-permute-start(bf16[4,2,32,1856]{3,2,1,0:T(8,128)(2,1)S(1)} %pad_maximum_fusion.1.refs_2_.refs_1_), channel_id=1, source_target_pairs={{0,128},{128,0},{256,384},{384,256},{1,129},{129,1},{257,385},{385... | collective-permute-start | bytes 2850824 | tf_op jit(solution)/shard_map/ppermute | solution.py:186
  64.4 7.0 %collective-permute-start.11 = (bf16[232,1856]{1,0:T(8,128)(2,1)S(1)}, bf16[232,1856]{1,0:T(8,128)(2,1)}, u32[]{:S(2)}, u32[]{:S(2)}) collective-permute-start(bf16[232,1856]{1,0:T(8,128)(2,1)S(1)} %copy-done.6), channel_id=1, source_target_pairs={{0,64},{64,0},{1,65},{65,1},{2,66},{66,2},{3,67},{67,3},{4,68},{68... | collective-permute-start | bytes 2583560 | tf_op jit(solution)/shard_map/ppermute | solution.py:183
  68.2 14.5 %collective-permute-start.10 = (bf16[8,232,128]{2,1,0:T(8,128)(2,1)S(1)}, bf16[8,232,128]{2,1,0:T(8,128)(2,1)}, u32[]{:S(2)}, u32[]{:S(2)}) collective-permute-start(bf16[8,232,128]{2,1,0:T(8,128)(2,1)S(1)} %pad_maximum_fusion.4.inputs), channel_id=1, source_target_pairs={{0,1},{1,0},{2,3},{3,2},{4,5},{5,4},{6,7},{7,6},{8,9},{9,8},{10,11... | collective-permute-start | bytes 1425416 | tf_op jit(solution)/shard_map/ppermute | solution.py:207
  91.0 4.6 %copy-start.3 = (bf16[4,2,32,1856]{3,2,1,0:T(8,128)(2,1)S(1)}, bf16[4,2,32,1856]{3,2,1,0:T(8,128)(2,1)}, u32[]{:S(2)}) copy-start(bf16[4,2,32,1856]{3,2,1,0:T(8,128)(2,1)} %copy-done.2) | copy-start | bytes 2850820
  91.0 10.2 %copy-start.5 = (bf16[4,2,32,1856]{3,2,1,0:T(8,128)(2,1)S(1)}, bf16[4,2,32,1856]{3,2,1,0:T(8,128)(2,1)}, u32[]{:S(2)}) copy-start(bf16[4,2,32,1856]{3,2,1,0:T(8,128)(2,1)} %copy-done.4) | copy-start | bytes 2850820
  91.0 29.6 %all-to-all-start = ((bf16[16,2,64,256]{3,2,1,0:T(8,128)(2,1)}), bf16[16,2,64,256]{3,2,1,0:T(8,128)(2,1)S(1)}, u32[]{:S(2)}, u32[]{:S(2)}) async-start(bf16[16,2,64,256]{3,2,1,0:T(8,128)(2,1)} %shard_map.60), calls=%async_computation | async-start | bytes 2097152 | tf_op jit(solution)/shard_map/all_to_all | solution.py:219
  95.6 13.1 %collective-permute-start.12 = (bf16[4,2,32,1856]{3,2,1,0:T(8,128)(2,1)S(1)}, bf16[4,2,32,1856]{3,2,1,0:T(8,128)(2,1)}, u32[]{:S(2)}, u32[]{:S(2)}) collective-permute-start(bf16[4,2,32,1856]{3,2,1,0:T(8,128)(2,1)S(1)} %copy-done.3), channel_id=1, source_target_pairs={{0,64},{64,0},{1,65},{65,1},{2,66},{66,2},{3,67},{67,3},{4,68},{68... | collective-permute-start | bytes 2850824 | tf_op jit(solution)/shard_map/ppermute | solution.py:183
  101.2 7.5 %collective-permute-start.13 = (bf16[4,2,32,1856]{3,2,1,0:T(8,128)(2,1)S(1)}, bf16[4,2,32,1856]{3,2,1,0:T(8,128)(2,1)}, u32[]{:S(2)}, u32[]{:S(2)}) collective-permute-start(bf16[4,2,32,1856]{3,2,1,0:T(8,128)(2,1)S(1)} %copy-done.5), channel_id=1, source_target_pairs={{0,64},{64,0},{1,65},{65,1},{2,66},{66,2},{3,67},{67,3},{4,68},{68... | collective-permute-start | bytes 2850824 | tf_op jit(solution)/shard_map/ppermute | solution.py:183
  103.2 5.6 %collective-permute-start.14 = (bf16[4,2,32,1856]{3,2,1,0:T(8,128)(2,1)}, bf16[4,2,32,1856]{3,2,1,0:T(8,128)(2,1)}, u32[]{:S(2)}, u32[]{:S(2)}) collective-permute-start(bf16[4,2,32,1856]{3,2,1,0:T(8,128)(2,1)} %collective-permute-done.4.refs_1_.refs_2_), channel_id=1, source_target_pairs={{0,64},{64,0},{1,65},{65,1},{2,66},{66,2},{3,67},{67,3},{4,68},{68... | collective-permute-start | bytes 2850824 | tf_op jit(solution)/shard_map/ppermute | solution.py:183
  105.6 4.8 %collective-permute-start.15 = (bf16[4,2,32,1856]{3,2,1,0:T(8,128)(2,1)}, bf16[4,2,32,1856]{3,2,1,0:T(8,128)(2,1)}, u32[]{:S(2)}, u32[]{:S(2)}) collective-permute-start(bf16[4,2,32,1856]{3,2,1,0:T(8,128)(2,1)} %collective-permute-done.9.refs_2_.refs_3_), channel_id=1, source_target_pairs={{0,64},{64,0},{1,65},{65,1},{2,66},{66,2},{3,67},{67,3},{4,68},{68... | collective-permute-start | bytes 2850824 | tf_op jit(solution)/shard_map/ppermute | solution.py:183
  120.6 1.2 copy-start
  130.8 0.6 copy-start.1
